TPU v7x, 32 devices: a whole 2x2x4 slice. The times are simulated.
32 devices in a mesh: groups: 2 (over y), dp: 4 (over z), expert: 2 (over x), tensor: 2 (over core).
Axes of the slice: x: 2, y: 2, z: 4, core: 2. Of those that a mesh axis runs over, the one named last changes fastest.
Arguments:
- tokens: bfloat16 [512, 3072], P(('groups', 'expert'), ('tensor', 'dp')), parts along dimension 0, may hold values from -6 to 6
- cotangent: bfloat16 [512, 3072], P(('groups', 'expert'), ('tensor', 'dp')), parts along dimension 0, may hold values from -6 to 6
- expert_ids: int32 [512, 2], P(('groups', 'expert')), parts along dimension 0, may hold values from 0 to 3, all different within a row; in each aligned block of 128 rows (0 to 127, 128 to 255, ...) at most 80 rows name the same one
- gate_values: bfloat16 [512, 2], P(('groups', 'expert')), parts along dimension 0, may hold values from 0.19921875 to 1
- gate_weight: bfloat16 [3072, 32768], P('tensor', ('expert', 'dp')), may hold values from -0.109375 to 0.109375
- up_weight: bfloat16 [3072, 32768], P('tensor', ('expert', 'dp')), may hold values from -0.109375 to 0.109375
- down_weight: bfloat16 [3072, 32768], P('tensor', ('expert', 'dp')), may hold values from -0.109375 to 0.109375
Outputs:
- token_grad: bfloat16 [512, 3072], P(('groups', 'expert'), ('tensor', 'dp')), parts along dimension 0
- gate_grad: bfloat16 [6144, 32768], P(('groups', 'tensor'), ('expert', 'dp')), parts along dimension 0
- up_grad: bfloat16 [6144, 32768], P(('groups', 'tensor'), ('expert', 'dp')), parts along dimension 0
- down_grad: bfloat16 [6144, 32768], P(('groups', 'tensor'), ('expert', 'dp')), parts along dimension 0
There are 2 independent parts, one for each index of `groups`. A program takes and returns all parts, laid end to end along the dimension named above; an argument that names none is the same for every part. Nothing has to cross between parts.
Inputs may be any that keep to these rules, and one draw needn't show every extreme that they name: `expert_ids`: each token names two different experts. Within each block of 128 rows (the rows of one index of expert) no expert is named more than 80 times, a bound that some block reaches.
All inputs are finite; a program needn't handle non-finite values.
Results may differ from a plain program's by a relative error of at most 0.019.
Values may be sent and summed in bfloat16 or wider, within the bound.
No kernel may reach another device: no remote copies, remote signals or barrier semaphores. Data moves between devices by JAX's collectives and lax.ppermute only.
A program may use at most 192 MiB of HBM per device.

v0:
```python
import math

import jax
import jax.numpy as jnp
import numpy as np
from jax import lax
from jax.sharding import PartitionSpec as P

FF = 8192
EXPERTS = 4
CAP = 80


def route_slots(expert_ids, capacity, experts):
    flat = expert_ids.reshape(-1)
    onehot = (flat[:, None] == jnp.arange(experts, dtype=jnp.int32)[None, :]).astype(jnp.int32)
    before = jnp.cumsum(onehot, axis=0) - onehot
    return flat * capacity + jnp.sum(before * onehot, axis=1)


def pick_local(stacked, owners, local, chosen):
    pieces = stacked.shape[0]
    shaped = stacked.reshape(pieces, 2, owners, local, stacked.shape[3], stacked.shape[4])
    taken = lax.dynamic_index_in_dim(shaped, chosen, 3, keepdims=False)
    return taken.reshape(pieces, 2, owners * stacked.shape[3], stacked.shape[4])


def body(tokens, cotangent, expert_ids, gate_values, gate_weight, up_weight, down_weight):
    owners = lax.axis_size("expert")
    replicas = lax.axis_size("dp")
    experts = EXPERTS
    capacity = CAP
    width_half = gate_weight.shape[0]
    columns = gate_weight.shape[1]
    narrow = tokens.shape[1]
    tok_rows = tokens.shape[0]
    span = experts * FF // owners
    local = max(1, span // FF)
    owner_expert = (np.arange(owners)[:, None] * span // FF + np.arange(local)[None, :]).reshape(-1)
    chosen = lax.axis_index("dp") * columns // FF
    gate_split = gate_weight.reshape(replicas, narrow, columns)
    up_split = up_weight.reshape(replicas, narrow, columns)
    down_split = down_weight.reshape(replicas, narrow, columns)
    dest_own = route_slots(expert_ids, capacity, experts)
    scaled = (
        gate_values.reshape(-1).astype(jnp.float32)[:, None]
        * jnp.repeat(cotangent, 2, axis=0).astype(jnp.float32)
    ).astype(jnp.bfloat16)
    x_exp = (
        jnp.zeros((experts * capacity, narrow), jnp.bfloat16)
        .at[dest_own]
        .set(jnp.repeat(tokens, 2, axis=0))
        .reshape(experts, capacity, narrow)
    )
    q_exp = (
        jnp.zeros((experts * capacity, narrow), jnp.bfloat16)
        .at[dest_own]
        .set(scaled)
        .reshape(experts, capacity, narrow)
    )
    x_in, q_in = (
        lax.all_to_all(x_exp[owner_expert], "expert", split_axis=0, concat_axis=0, tiled=True),
        lax.all_to_all(q_exp[owner_expert], "expert", split_axis=0, concat_axis=0, tiled=True),
    )
    stacked = jnp.stack((x_in, q_in))[None]
    gathered = lax.all_gather(stacked, "dp", axis=0, tiled=True)
    full_rows = pick_local(gathered, owners, local, chosen)
    part_g = jnp.einsum(
        "prw,pwf->rf", full_rows[:, 0], gate_split, preferred_element_type=jnp.float32
    )
    part_u = jnp.einsum(
        "prw,pwf->rf", full_rows[:, 0], up_split, preferred_element_type=jnp.float32
    )
    part_h = jnp.einsum(
        "prw,pwf->rf", full_rows[:, 1], down_split, preferred_element_type=jnp.float32
    )
    pre_gate, pre_up, d_hidden = (
        lax.psum(part_g.astype(jnp.bfloat16), "tensor").astype(jnp.float32),
        lax.psum(part_u.astype(jnp.bfloat16), "tensor").astype(jnp.float32),
        lax.psum(part_h.astype(jnp.bfloat16), "tensor").astype(jnp.float32),
    )
    sigma = jax.nn.sigmoid(pre_gate)
    act = sigma * pre_gate
    hidden = (act * pre_up).astype(jnp.bfloat16)
    d_gate = (d_hidden * pre_up * sigma * (1.0 + pre_gate * (1.0 - sigma))).astype(jnp.bfloat16)
    d_up = (d_hidden * act).astype(jnp.bfloat16)
    row_part = jnp.einsum("rf,pwf->prw", d_gate, gate_split, preferred_element_type=jnp.float32)
    row_part = row_part + jnp.einsum(
        "rf,pwf->prw", d_up, up_split, preferred_element_type=jnp.float32
    )
    selector = (jnp.arange(local, dtype=jnp.int32) == chosen).astype(jnp.float32)
    placed = (
        row_part.reshape(replicas, owners, 1, capacity, narrow)
        * selector[None, None, :, None, None]
    )
    summed = lax.psum_scatter(
        placed.astype(jnp.bfloat16), "dp", scatter_dimension=0, tiled=True
    ).astype(jnp.float32)
    back = lax.all_to_all(
        summed.reshape(owners * local, capacity, narrow).astype(jnp.bfloat16),
        "expert",
        split_axis=0,
        concat_axis=0,
        tiled=True,
    ).astype(jnp.float32)
    table = jnp.asarray((owner_expert[None, :] == np.arange(experts)[:, None]).astype(np.float32))
    by_expert = jnp.einsum("ek,kcd->ecd", table, back, precision=lax.Precision.HIGHEST)
    picked = by_expert.reshape(experts * capacity, narrow)[dest_own]
    token_grad = picked.reshape(tok_rows, 2, narrow).sum(axis=1).astype(jnp.bfloat16)
    factor = 1.0 / math.sqrt(tok_rows * owners)
    grad_gate = jnp.einsum(
        "prw,rf->pwf", full_rows[:, 0], d_gate, preferred_element_type=jnp.float32
    ).reshape(width_half, columns)
    grad_up = jnp.einsum(
        "prw,rf->pwf", full_rows[:, 0], d_up, preferred_element_type=jnp.float32
    ).reshape(width_half, columns)
    grad_down = jnp.einsum(
        "prw,rf->pwf", full_rows[:, 1], hidden, preferred_element_type=jnp.float32
    ).reshape(width_half, columns)
    return (
        token_grad,
        (grad_gate * factor).astype(jnp.bfloat16),
        (grad_up * factor).astype(jnp.bfloat16),
        (grad_down * factor).astype(jnp.bfloat16),
    )


def solution(mesh):
    in_specs = (
        P(("groups", "expert"), ("tensor", "dp")),
        P(("groups", "expert"), ("tensor", "dp")),
        P(("groups", "expert"), None),
        P(("groups", "expert"), None),
        P("tensor", ("expert", "dp")),
        P("tensor", ("expert", "dp")),
        P("tensor", ("expert", "dp")),
    )
    out_specs = (
        P(("groups", "expert"), ("tensor", "dp")),
        P(("groups", "tensor"), ("expert", "dp")),
        P(("groups", "tensor"), ("expert", "dp")),
        P(("groups", "tensor"), ("expert", "dp")),
    )
    return jax.shard_map(body, mesh=mesh, in_specs=in_specs, out_specs=out_specs, check_vma=False)
```

profile of v0, /device:TPU:0, one launch (start us, length us, event | category | flops | bytes accessed | tf_op | source)
XLA Modules:
  0.0 186.3 jit_solution(3180134220188205666)
XLA Ops:
  7.2 0.7 broadcast_multiply_fusion
  7.8 0.8 copy.30
  8.6 0.1 eq.39
  8.8 0.1 eq.35
  8.9 0.1 copy.29
  9.1 0.1 mul.77
  9.2 1.2 reduce-window.6
  10.4 0.1 slice.26
  10.5 0.1 copy.32
  10.7 0.1 copy.33
  10.7 0.1 add_bitcast_fusion
  10.8 1.0 broadcast_in_dim.10
  11.8 0.1 reshape.150
  11.9 1.5 scatter_custom_fusion
  13.5 1.3 gather_fusion
  14.8 4.2 %all-to-all-start = ((bf16[4,80,384]{2,1,0:T(8,128)(2,1)}), bf16[4,80,384]{2,1,0:T(8,128)(2,1)S(1)}, u32[]{:S(2)}, u32[]{:S(2)}) async-start(bf16[4,80,384]{2,1,0:T(8,128)(2,1)} %gather_fusion), calls=%async_computation | async-start | bytes 491520 | tf_op jit(solution)/shard_map/all_to_all | solution.py:62
  19.0 0.0 all-gather.3.cloned.1.call-start
  19.0 0.8 copy.34
  19.7 0.1 reshape.121
  19.9 1.0 broadcast_in_dim.23
  20.9 0.3 convert_element_type.87
  21.2 1.6 scatter_custom_fusion.1
  22.8 0.6 gather_fusion.1
  23.4 1.3 all-to-all-done
  24.7 7.5 %all_to_all.15 = bf16[4,80,384]{2,1,0:T(8,128)(2,1)S(1)} all-to-all(bf16[4,80,384]{2,1,0:T(8,128)(2,1)S(1)} %gather_fusion.1), channel_id=1, replica_groups=mesh['groups'=2,'dp'=4,'expert'=2,'tensor'=2] {'expert'}, dimensions={0} | all-to-all | bytes 491520 | tf_op jit(solution)/shard_map/all_to_all | solution.py:63
  32.1 0.8 pad_maximum_fusion
  32.9 0.0 all-gather.3.cloned.1.call-update
  33.0 0.0 all-reduce.3.cloned.1.call-start
  33.0 44.2 %all-gather.3.cloned.1.call-done = bf16[8,4,80,384]{3,2,1,0:T(8,128)(2,1)} async-done(((bf16[2,4,80,384]{3,2,1,0:T(8,128)(2,1)}), bf16[8,4,80,384]{3,2,1,0:T(8,128)(2,1)}) %all-gather.3.cloned.1.call-update) | async-done | bytes 1966096 | tf_op jit(solution)/shard_map/all_gather | solution.py:66
  77.3 1.3 constant_dynamic-slice_fusion
  78.6 0.0 copy-start
  78.6 0.1 copy.35
  78.7 0.0 slice-start
  78.7 0.0 slice-start.1
  78.7 8.1 %fusion.2 = bf16[160,4096]{1,0:T(8,128)(2,1)} fusion(bf16[4,384,4096]{2,1,0:T(8,128)(2,1)} %bitcast.91, bf16[4,2,160,384]{3,2,0,1:T(8,128)(2,1)S(1)} %bitcast.93), kind=kOutput, calls=%fused_computation.13 | convolution fusion | flops 2013921280 | bytes 14385152 | tf_op jit(solution)/shard_map/prw,pwf->rf/dot_general | solution.py:68
  86.8 0.0 copy-done
  86.8 3.4 %fusion.1 = bf16[160,4096]{1,0:T(8,128)(2,1)} fusion(bf16[4,384,4096]{2,1,0:T(8,128)(2,1)S(1)} %bitcast.90, bf16[4,2,160,384]{3,2,0,1:T(8,128)(2,1)S(1)} %bitcast.94), kind=kOutput, calls=%fused_computation.12 | convolution fusion | flops 2013921280 | bytes 14385152 | tf_op jit(solution)/shard_map/prw,pwf->rf/dot_general | solution.py:71
  90.3 0.0 slice-done
  90.3 0.0 slice-done.1
  90.3 1.1 slice-done.2
  91.4 3.4 %fusion = bf16[160,4096]{1,0:T(8,128)(2,1)} fusion(bf16[4,384,4096]{2,1,0:T(8,128)(2,1)S(1)} %bitcast.88, bf16[4,2,160,384]{3,2,0,1:T(8,128)(2,1)S(1)} %bitcast.95), kind=kOutput, calls=%fused_computation.11 | convolution fusion | flops 2013921280 | bytes 14385152 | tf_op jit(solution)/shard_map/prw,pwf->rf/dot_general | solution.py:74
  94.8 0.0 all-reduce.3.cloned.1.call-update
  94.8 0.2 reduce-scatter.2.cloned.1.call-start
  95.1 0.1 slice_bitcast_fusion
  95.2 0.1 copy.41
  95.3 0.1 copy.40
  95.3 23.6 %all-reduce.3.cloned.1.call-done = (bf16[160,4096]{1,0:T(8,128)(2,1)}, bf16[160,4096]{1,0:T(8,128)(2,1)}, bf16[160,4096]{1,0:T(8,128)(2,1)}) async-done(((bf16[160,4096]{1,0:T(8,128)(2,1)}, bf16[160,4096]{1,0:T(8,128)(2,1)}, bf16[160,4096]{1,0:T(8,128)(2,1)}), (bf16[160,4096]{1,0:T(8,128)(2,1)}, bf16[160,4096]{1,0:T(8,128)(2,1)}, bf16[160,4096]{1,0:T(8,128)(2,1)})) %all-reduce.3.cloned.1.call-update) | async-done | bytes 3932176 | tf_op jit(solution)/shard_map/psum | solution.py:80
  118.9 8.5 %fusion.13 = f32[160,4,384]{2,0,1:T(8,128)S(1)} fusion(bf16[4,384,4096]{2,1,0:T(8,128)(2,1)} %bitcast.89, bf16[160,4096]{1,0:T(8,128)(2,1)} %get-tuple-element.4, bf16[160,4096]{1,0:T(8,128)(2,1)} %get-tuple-element.5), kind=kOutput, calls=%fused_computation.30 | convolution fusion | flops 2018508800 | bytes 16187392 | tf_op jit(solution)/shard_map/rf,pwf->prw/dot_general | solution.py:88
  127.4 0.0 copy-done.2
  127.4 0.0 copy-done.3
  127.5 9.1 %fusion.17 = f32[160,4,384]{2,0,1:T(8,128)S(1)} fusion(f32[160,4,384]{2,0,1:T(8,128)S(1)} %fusion.13, bf16[4,384,4096]{2,1,0:T(8,128)(2,1)} %bitcast.92, bf16[160,4096]{1,0:T(8,128)(2,1)S(1)} %copy-done.3, bf16[160,4096]{1,0:T(8,128)(2,1)S(1)} %copy-done.5, bf16[160,4096]{1,0:T(8,128)(2,1)S(1)} %copy-done.2), kind=kOutput, calls=%fused_computation.34 | convolution fusion | flops 2022031360 | bytes 18481152 | tf_op jit(solution)/shard_map/rf,pwf->prw/dot_general | solution.py:87
  136.5 1.2 multiply_convert_fusion.3
  137.7 0.0 reduce-scatter.2.cloned.1.call-update
  137.7 8.2 %multiply_convert_fusion.1 = bf16[1536,4096]{1,0:T(8,128)(2,1)} fusion(bf16[1536,160]{0,1:T(8,128)(2,1)S(1)} %bitcast.104, bf16[160,4096]{1,0:T(8,128)(2,1)} %get-tuple-element.4, bf16[160,4096]{1,0:T(8,128)(2,1)S(1)} %copy-done.2), kind=kOutput, calls=%fused_computation.6 | convolution fusion | flops 2031091712 | bytes 15695872 | tf_op jit(solution)/shard_map/prw,rf->pwf/dot_general | solution.py:114
  145.9 6.7 %multiply_convert_fusion.2 = bf16[1536,4096]{1,0:T(8,128)(2,1)} fusion(bf16[1536,160]{0,1:T(8,128)(2,1)S(1)} %bitcast.105, bf16[160,4096]{1,0:T(8,128)(2,1)S(1)} %copy-done.4, bf16[160,4096]{1,0:T(8,128)(2,1)S(1)} %copy-done.6, bf16[160,4096]{1,0:T(8,128)(2,1)S(1)} %copy-done.2), kind=kOutput, calls=%fused_computation.7 | convolution fusion | flops 2034368512 | bytes 17006592 | tf_op jit(solution)/shard_map/prw,rf->pwf/dot_general | solution.py:111
  152.6 12.5 %reduce-scatter.2.cloned.1.call-done = bf16[1,2,2,80,384]{4,3,2,1,0:T(8,128)(2,1)} async-done(((bf16[4,2,2,80,384]{4,3,2,1,0:T(8,128)(2,1)}), bf16[1,2,2,80,384]{4,3,2,1,0:T(8,128)(2,1)}) %reduce-scatter.2.cloned.1.call-update) | async-done | bytes 245776 | tf_op jit(solution)/shard_map/reduce_scatter | solution.py:96
  165.2 3.7 %all-to-all-start.2 = ((bf16[4,80,384]{2,1,0:T(8,128)(2,1)}), bf16[4,80,384]{2,1,0:T(8,128)(2,1)S(1)}, u32[]{:S(2)}, u32[]{:S(2)}) async-start(bf16[4,80,384]{2,1,0:T(8,128)(2,1)} %bitcast.106), calls=%async_computation.3 | async-start | bytes 491520 | tf_op jit(solution)/shard_map/all_to_all | solution.py:99
  168.8 0.0 copy-start.1
  168.8 8.0 %multiply_convert_fusion = bf16[1536,4096]{1,0:T(8,128)(2,1)} fusion(bf16[1536,160]{0,1:T(8,128)(2,1)S(1)} %bitcast.103, bf16[160,4096]{1,0:T(8,128)(2,1)} %get-tuple-element.6, bf16[160,4096]{1,0:T(8,128)(2,1)S(1)} %copy-done.2), kind=kOutput, calls=%fused_computation.5 | convolution fusion | flops 2031091712 | bytes 15695872 | tf_op jit(solution)/shard_map/prw,rf->pwf/dot_general | solution.py:117
  176.9 0.0 all-to-all-done.2
  176.9 0.5 fusion.26
  177.5 1.0 gather_fusion.2
  178.5 0.2 reshape.120
  178.7 1.1 reduce_sum.22
  (21 shorter events, 0.1 us)
Async XLA Ops:
  14.8 9.9 %all-to-all-start = ((bf16[4,80,384]{2,1,0:T(8,128)(2,1)}), bf16[4,80,384]{2,1,0:T(8,128)(2,1)S(1)}, u32[]{:S(2)}, u32[]{:S(2)}) async-start(bf16[4,80,384]{2,1,0:T(8,128)(2,1)} %gather_fusion), calls=%async_computation | async-start | bytes 491520 | tf_op jit(solution)/shard_map/all_to_all | solution.py:62
  19.0 58.3 %all-gather.3.cloned.1.call-start = ((), (), s32[]{:S(2)}) async-start(), calls=%async_computation.5 | async-start | bytes 2457600 | tf_op jit(solution)/shard_map/all_gather | solution.py:66
  33.0 85.9 %all-reduce.3.cloned.1.call-start = ((), (), s32[]{:S(2)}) async-start(), calls=%async_computation.6 | async-start | bytes 7864320 | tf_op jit(solution)/shard_map/psum | solution.py:80
  78.6 8.3 %copy-start = (bf16[1536,4096]{1,0:T(8,128)(2,1)S(1)}, bf16[1536,4096]{1,0:T(8,128)(2,1)}, u32[]{:S(2)}) copy-start(bf16[1536,4096]{1,0:T(8,128)(2,1)} %param.16) | copy-start | bytes 37748740
  78.7 11.6 %slice-start = ((s8[12582912]{0:T(1024)(128)(4,1)}), s8[4194304]{0:T(1024)(128)(4,1)S(1)}, s32[]{:S(2)}) async-start(s8[12582912]{0:T(1024)(128)(4,1)} %bitcast.86), calls=%async_computation.7 | async-start | bytes 8388608
  78.7 11.6 %slice-start.1 = ((s8[12582912]{0:T(1024)(128)(4,1)}), s8[4194304]{0:T(1024)(128)(4,1)S(1)}, s32[]{:S(2)}) async-start(s8[12582912]{0:T(1024)(128)(4,1)} %bitcast.86), calls=%async_computation.8 | async-start | bytes 8388608
  86.8 4.6 %slice-start.2 = ((s8[12582912]{0:T(1024)(128)(4,1)}), s8[4194304]{0:T(1024)(128)(4,1)S(1)}, s32[]{:S(2)}) async-start(s8[12582912]{0:T(1024)(128)(4,1)} %bitcast.86), calls=%async_computation.9 | async-start | bytes 8388608
  94.8 70.3 %reduce-scatter.2.cloned.1.call-start = ((), (), s32[]{:S(2)}) async-start(), calls=%async_computation.4 | async-start | bytes 1228800 | tf_op jit(solution)/shard_map/reduce_scatter | solution.py:96
  118.9 8.5 %copy-start.2 = (bf16[160,4096]{1,0:T(8,128)(2,1)S(1)}, bf16[160,4096]{1,0:T(8,128)(2,1)}, u32[]{:S(2)}) copy-start(bf16[160,4096]{1,0:T(8,128)(2,1)} %get-tuple-element.5) | copy-start | bytes 3932164
  118.9 8.6 %copy-start.3 = (bf16[160,4096]{1,0:T(8,128)(2,1)S(1)}, bf16[160,4096]{1,0:T(8,128)(2,1)}, u32[]{:S(2)}) copy-start(bf16[160,4096]{1,0:T(8,128)(2,1)} %get-tuple-element.6) | copy-start | bytes 3932164
  118.9 8.6 %copy-start.5 = (bf16[160,4096]{1,0:T(8,128)(2,1)S(1)}, bf16[160,4096]{1,0:T(8,128)(2,1)}, u32[]{:S(2)}) copy-start(bf16[160,4096]{1,0:T(8,128)(2,1)} %get-tuple-element.4) | copy-start | bytes 3932164
  137.7 8.2 %copy-start.4 = (bf16[160,4096]{1,0:T(8,128)(2,1)S(1)}, bf16[160,4096]{1,0:T(8,128)(2,1)}, u32[]{:S(2)}) copy-start(bf16[160,4096]{1,0:T(8,128)(2,1)} %get-tuple-element.6) | copy-start | bytes 3932164
  137.7 8.2 %copy-start.6 = (bf16[160,4096]{1,0:T(8,128)(2,1)S(1)}, bf16[160,4096]{1,0:T(8,128)(2,1)}, u32[]{:S(2)}) copy-start(bf16[160,4096]{1,0:T(8,128)(2,1)} %get-tuple-element.4) | copy-start | bytes 3932164
  165.2 11.7 %all-to-all-start.2 = ((bf16[4,80,384]{2,1,0:T(8,128)(2,1)}), bf16[4,80,384]{2,1,0:T(8,128)(2,1)S(1)}, u32[]{:S(2)}, u32[]{:S(2)}) async-start(bf16[4,80,384]{2,1,0:T(8,128)(2,1)} %bitcast.106), calls=%async_computation.3 | async-start | bytes 491520 | tf_op jit(solution)/shard_map/all_to_all | solution.py:99
  168.8 8.0 %copy-start.1 = (f32[4,4,1]{1,0,2:T(4,128)S(1)}, f32[4,4,1]{1,0,2:T(4,128)}, u32[]{:S(2)}) copy-start(f32[4,4,1]{1,0,2:T(4,128)} %constant.56) | copy-start | bytes 196
Sparse Core Ops, SparseCore 0:
  33.1 44.1 all-gather.2
  95.0 23.8 all-reduce.2
  137.8 27.2 reduce-scatter.1
where the time goes:
time: 187 us; the launch traced here: 186 us
  waiting for transfers between devices  81.6 us (44%)
  matrix products  56 us (30%)
  between operations  14 us (7%)
  local copies, waits for them, and re-layouts  12.3 us (7%)
  starting transfers between devices  8.13 us (4%)
  blocking collectives  7.45 us (4%)
  other arithmetic  6.8 us (4%)
    all_gather x1, waiting for transfers between devices, body(): gathered = lax.all_gather(stacked, 'dp', axis=0, tiled=True)  44.2 us
    psum x1, waiting for transfers between devices, body(): lax.psum(part_h.astype(jnp.bfloat16), 'tensor').astype(jnp.float32)  23.6 us
    reduce_scatter x1, waiting for transfers between devices, body(): lax.psum_scatter(placed.astype(jnp.bfloat16), 'dp', scatter_dimension=0,...  12.5 us
    dot_general x1, matrix products, body(): jnp.einsum('rf,pwf->prw', d_gate, gate_split, preferred_element_type=jnp....  9.07 us
    dot_general x1, matrix products, body(): jnp.einsum('rf,pwf->prw', d_up, up_split, preferred_element_type=jnp.floa...  8.53 us
    dot_general x1, matrix products, body(): jnp.einsum('prw,rf->pwf', full_rows[:, 0], d_up, preferred_element_type=j...  8.17 us
    dot_general x1, matrix products, body(): jnp.einsum('prw,pwf->rf', full_rows[:, 0], gate_split, preferred_element_...  8.14 us
    dot_general x1, matrix products, body(): jnp.einsum('prw,rf->pwf', full_rows[:, 1], hidden, preferred_element_type...  8.02 us
  transfers between devices with their start and end apart: 5, of which 4 were waited for; matrix products, arithmetic and copies ran while one was open for 15% of the time, Pallas kernels for 0%

commit v1 on v0

v1 whole, which is shorter than its diff:
```python
import functools
import math

import jax
import jax.numpy as jnp
from jax import lax
from jax.experimental import pallas as pl
from jax.experimental.pallas import tpu as pltpu
from jax.sharding import PartitionSpec as P

FF = 8192
EXPERTS = 4
CAP = 80
F32 = jnp.float32
BF16 = jnp.bfloat16
VMEM_LIMIT = 48 * 1024 * 1024


def params():
    return pltpu.CompilerParams(vmem_limit_bytes=VMEM_LIMIT)


def cost(flops, moved):
    return pl.CostEstimate(flops=flops, bytes_accessed=moved, transcendentals=0)


def is_pow2(value):
    return value & (value - 1) == 0


def block_of(size, wanted):
    while size % wanted:
        wanted //= 2
    return wanted


class Plan:
    def __init__(self, mesh, columns):
        self.owners = mesh.shape["expert"]
        self.replicas = mesh.shape["dp"]
        self.partners = self.owners * self.replicas
        self.direct = self.partners <= 8 and is_pow2(self.owners) and is_pow2(self.replicas)
        self.columns = columns
        self.refs, self.each = (self.partners, 1) if self.direct else (1, self.partners)

    def width_index(self, j, z):
        dz = j % self.replicas
        return jnp.bitwise_xor(z, dz) if self.direct else dz

    def expert_of(self, j, x, z):
        if self.direct:
            device = jnp.bitwise_xor(x, j // self.replicas) * self.replicas + jnp.bitwise_xor(z, j % self.replicas)
        else:
            device = j
        return device * self.columns // FF

    def exchange(self, sends):
        if not self.direct:
            return [lax.all_to_all(sends[0], ("expert", "dp"), 0, 0, tiled=True)]
        out = [sends[0]]
        for j in range(1, self.partners):
            dx, dz = j // self.replicas, j % self.replicas
            pairs = []
            for x in range(self.owners):
                for z in range(self.replicas):
                    pairs.append((z * self.owners + x, (z ^ dz) * self.owners + (x ^ dx)))
            out.append(lax.ppermute(sends[j], ("dp", "expert"), pairs))
        return out


def dispatch_kernel(plan, where_ref, ids_ref, gates_ref, tok_ref, cot_ref, *outs):
    n = plan.refs
    x_refs, q_refs, sel_ref = outs[:n], outs[n:2 * n], outs[2 * n]
    x_at, z_at = where_ref[0], where_ref[1]
    count = tok_ref.shape[0]
    first, second = ids_ref[0:1, :], ids_ref[1:2, :]
    gate_first, gate_second = gates_ref[0:1, :].astype(F32), gates_ref[1:2, :].astype(F32)
    row = lax.broadcasted_iota(jnp.int32, (16, count), 0)
    named = ((row == first) | (row == second)).astype(F32)
    earlier = lax.broadcasted_iota(jnp.int32, (count, count), 0) < lax.broadcasted_iota(jnp.int32, (count, count), 1)
    before = jnp.dot(named.astype(BF16), earlier.astype(F32).astype(BF16), preferred_element_type=F32)
    slot = lax.broadcasted_iota(jnp.int32, (CAP, count), 0).astype(F32)
    tok, cot = tok_ref[...], cot_ref[...]

    def one(ref_index, inner, j):
        expert = plan.expert_of(j, x_at, z_at)
        mine = (row == expert).astype(F32)
        position = jnp.sum(mine * before, axis=0, keepdims=True)
        here = jnp.sum(mine * named, axis=0, keepdims=True)
        chosen = jnp.where((position == slot) & (here > 0.5), 1.0, 0.0)
        gate = jnp.where(first == expert, gate_first, gate_second)
        weight = jnp.sum(chosen * gate, axis=1, keepdims=True)
        chosen = chosen.astype(BF16)
        x_refs[ref_index][inner] = jnp.dot(chosen, tok, preferred_element_type=F32).astype(BF16)
        q_refs[ref_index][inner] = (weight * jnp.dot(chosen, cot, preferred_element_type=F32)).astype(BF16)
        sel_ref[j] = chosen

    if plan.direct:
        for j in range(n):
            one(j, 0, j)
    else:
        lax.fori_loop(0, plan.each, lambda j, c: (one(0, j, j), c)[1], 0)


def dispatch(plan, where, ids, gates, tokens, cotangent):
    count, narrow = tokens.shape
    piece = jax.ShapeDtypeStruct((plan.each, CAP, narrow), BF16)
    vmem = pl.BlockSpec(memory_space=pltpu.VMEM)
    outs = pl.pallas_call(
        functools.partial(dispatch_kernel, plan),
        out_shape=[piece] * (2 * plan.refs) + [jax.ShapeDtypeStruct((plan.partners, CAP, count), BF16)],
        in_specs=[pl.BlockSpec(memory_space=pltpu.SMEM)] + [vmem] * 4,
        out_specs=[vmem] * (2 * plan.refs + 1),
        compiler_params=params(),
        name="dispatch",
    )(where, ids.T, gates.T, tokens, cotangent)
    return outs[: plan.refs], outs[plan.refs : 2 * plan.refs], outs[-1]


def lanes(plan, j, z, narrow):
    start = plan.width_index(j, z) * narrow
    if plan.direct:
        start = pl.multiple_of(start, 128)
    return pl.ds(start, narrow)


def forward_kernel(plan, weights, where_ref, *refs):
    pieces, w_refs = refs[: plan.refs], refs[plan.refs : plan.refs + weights]
    full_ref, part_refs = refs[plan.refs + weights], refs[plan.refs + weights + 1 :]
    narrow = pieces[0].shape[2]

    @pl.when(pl.program_id(0) == 0)
    def _():
        for j in range(plan.partners):
            rows = pl.ds(j // plan.replicas * CAP, CAP)
            full_ref[rows, lanes(plan, j, where_ref[1], narrow)] = pieces[j // plan.each][j % plan.each]

    for w_ref, part_ref in zip(w_refs, part_refs):
        part_ref[...] = jnp.dot(full_ref[...], w_ref[...], preferred_element_type=F32).astype(BF16)


def forward(plan, where, pieces, weights, name, wanted=512):
    width, columns = weights[0].shape
    rows, block = plan.owners * CAP, block_of(columns, wanted)
    part = jax.ShapeDtypeStruct((rows, columns), BF16)
    whole = pl.BlockSpec(memory_space=pltpu.VMEM)
    resident = pl.BlockSpec((rows, width), lambda i: (0, 0))
    strip = pl.BlockSpec((width, block), lambda i: (0, i))
    part_spec = pl.BlockSpec((rows, block), lambda i: (0, i))
    k = len(weights)
    return pl.pallas_call(
        functools.partial(forward_kernel, plan, k),
        grid=(columns // block,),
        out_shape=[jax.ShapeDtypeStruct((rows, width), BF16)] + [part] * k,
        in_specs=[pl.BlockSpec(memory_space=pltpu.SMEM)] + [whole] * plan.refs + [strip] * k,
        out_specs=[resident] + [part_spec] * k,
        compiler_params=params(),
        cost_estimate=cost(2 * k * rows * width * columns, 2 * k * width * columns),
        name=name,
    )(where, *pieces, *weights)


def rows_kernel(plan, where_ref, g0, g1, u0, u1, d0, d1, wg_ref, wu_ref, h_ref, dg_ref, du_ref, *rest):
    outs, total = rest[: plan.refs], rest[plan.refs]
    gate = g0[...].astype(F32) + g1[...].astype(F32)
    up = u0[...].astype(F32) + u1[...].astype(F32)
    hidden = d0[...].astype(F32) + d1[...].astype(F32)
    sigma = jax.nn.sigmoid(gate)
    act = sigma * gate
    h_ref[...] = (act * up).astype(BF16)
    d_gate = (hidden * up * sigma * (1.0 + gate * (1.0 - sigma))).astype(BF16)
    d_up = (hidden * act).astype(BF16)
    dg_ref[...] = d_gate
    du_ref[...] = d_up
    turned = (((1,), (1,)), ((), ()))
    term = lax.dot_general(d_gate, wg_ref[...], turned, preferred_element_type=F32)
    term = term + lax.dot_general(d_up, wu_ref[...], turned, preferred_element_type=F32)
    step = pl.program_id(0)

    @pl.when(step == 0)
    def _():
        total[...] = term

    @pl.when(step > 0)
    def _():
        total[...] += term

    @pl.when(step == pl.num_programs(0) - 1)
    def _():
        narrow = outs[0].shape[2]
        for j in range(plan.partners):
            rows = pl.ds(j // plan.replicas * CAP, CAP)
            outs[j // plan.each][j % plan.each] = total[rows, lanes(plan, j, where_ref[1], narrow)].astype(BF16)


def row_grads(plan, where, parts, wg, wu, wanted=512):
    width, columns = wg.shape
    narrow = width // plan.replicas
    rows, block = plan.owners * CAP, block_of(columns, wanted)
    strip = pl.BlockSpec((width, block), lambda i: (0, i))
    part_spec = pl.BlockSpec((rows, block), lambda i: (0, i))
    piece = jax.ShapeDtypeStruct((plan.each, CAP, narrow), BF16)
    hidden = jax.ShapeDtypeStruct((rows, columns), BF16)
    outs = pl.pallas_call(
        functools.partial(rows_kernel, plan),
        grid=(columns // block,),
        out_shape=[hidden] * 3 + [piece] * plan.refs,
        in_specs=[pl.BlockSpec(memory_space=pltpu.SMEM)] + [part_spec] * 6 + [strip] * 2,
        out_specs=[part_spec] * 3 + [pl.BlockSpec((plan.each, CAP, narrow), lambda i: (0, 0, 0))] * plan.refs,
        scratch_shapes=[pltpu.VMEM((rows, width), F32)],
        compiler_params=params(),
        cost_estimate=cost(4 * rows * width * columns, 4 * width * columns),
        name="row_grads",
    )(where, *parts, wg, wu)
    return outs[:3], outs[3:]


def weights_kernel(factor, x_ref, q_ref, dg_ref, du_ref, h_ref, gg_ref, gu_ref, gd_ref):
    turned = (((0,), (0,)), ((), ()))
    for rows_ref, d_ref, out_ref in ((x_ref, dg_ref, gg_ref), (x_ref, du_ref, gu_ref), (q_ref, h_ref, gd_ref)):
        grad = lax.dot_general(rows_ref[...], d_ref[...], turned, preferred_element_type=F32)
        out_ref[...] = (grad * factor).astype(BF16)


def weight_grads(factor, x_full, q_full, hidden, wanted=512):
    rows, width = x_full.shape
    columns = hidden[0].shape[1]
    block = block_of(columns, wanted)
    resident = pl.BlockSpec((rows, width), lambda i: (0, 0))
    part_spec = pl.BlockSpec((rows, block), lambda i: (0, i))
    out_spec = pl.BlockSpec((width, block), lambda i: (0, i))
    return pl.pallas_call(
        functools.partial(weights_kernel, factor),
        grid=(columns // block,),
        out_shape=[jax.ShapeDtypeStruct((width, columns), BF16)] * 3,
        in_specs=[resident] * 2 + [part_spec] * 3,
        out_specs=[out_spec] * 3,
        compiler_params=params(),
        cost_estimate=cost(6 * rows * width * columns, 6 * width * columns),
        name="weight_grads",
    )(x_full, q_full, *hidden)


def combine_kernel(plan, sel_ref, *rest):
    backs, out_ref = rest[: plan.refs], rest[plan.refs]
    turned = (((0,), (0,)), ((), ()))

    def term(ref, inner, j):
        return lax.dot_general(sel_ref[j], ref[inner], turned, preferred_element_type=F32)

    if plan.direct:
        total = term(backs[0], 0, 0)
        for j in range(1, plan.refs):
            total = total + term(backs[j], 0, j)
    else:
        total = lax.fori_loop(0, plan.each, lambda j, t: t + term(backs[0], j, j), jnp.zeros(out_ref.shape, F32))
    out_ref[...] = total.astype(BF16)


def combine(plan, sel, backs):
    count, narrow = sel.shape[2], backs[0].shape[2]
    vmem = pl.BlockSpec(memory_space=pltpu.VMEM)
    return pl.pallas_call(
        functools.partial(combine_kernel, plan),
        out_shape=jax.ShapeDtypeStruct((count, narrow), BF16),
        in_specs=[vmem] * (1 + plan.refs),
        out_specs=vmem,
        compiler_params=params(),
        name="combine",
    )(sel, *backs)


def body(mesh, tokens, cotangent, expert_ids, gate_values, gate_weight, up_weight, down_weight):
    plan = Plan(mesh, gate_weight.shape[1])
    where = jnp.stack((lax.axis_index("expert"), lax.axis_index("dp"))).astype(jnp.int32)
    x_send, q_send, sel = dispatch(plan, where, expert_ids, gate_values, tokens, cotangent)
    x_pieces = plan.exchange(x_send)
    q_pieces = plan.exchange(q_send)

    def swap(part):
        size = mesh.shape["tensor"]
        return lax.ppermute(part, "tensor", [(i, i ^ 1) for i in range(size)])

    x_full, part_g, part_u = forward(plan, where, x_pieces, [gate_weight, up_weight], "forward_gu")
    other_g, other_u = swap(part_g), swap(part_u)
    q_full, part_h = forward(plan, where, q_pieces, [down_weight], "forward_h")
    other_h = swap(part_h)
    hidden, pieces = row_grads(plan, where, (part_g, other_g, part_u, other_u, part_h, other_h), gate_weight, up_weight)
    (h, d_gate, d_up) = hidden
    backs = plan.exchange(pieces)
    factor = 1.0 / math.sqrt(tokens.shape[0] * plan.owners)
    grads = weight_grads(factor, x_full, q_full, (d_gate, d_up, h))
    token_grad = combine(plan, sel, backs)
    return (token_grad, *grads)


def solution(mesh):
    in_specs = (
        P(("groups", "expert"), ("tensor", "dp")),
        P(("groups", "expert"), ("tensor", "dp")),
        P(("groups", "expert"), None),
        P(("groups", "expert"), None),
        P("tensor", ("expert", "dp")),
        P("tensor", ("expert", "dp")),
        P("tensor", ("expert", "dp")),
    )
    out_specs = (
        P(("groups", "expert"), ("tensor", "dp")),
        P(("groups", "tensor"), ("expert", "dp")),
        P(("groups", "tensor"), ("expert", "dp")),
        P(("groups", "tensor"), ("expert", "dp")),
    )
    return jax.shard_map(
        functools.partial(body, mesh), mesh=mesh, in_specs=in_specs, out_specs=out_specs, check_vma=False
    )
```

time: 187 us -> 101 us (0.54)
  waiting for transfers between devices: 81.6 us -> 5.22 us
  matrix products: 56 us -> 0 us
  Pallas kernels: 0 us -> 53.1 us
  starting transfers between devices: 8.13 us -> 37 us
  between operations: 14 us -> 0.8 us
  local copies, waits for them, and re-layouts: 12.3 us -> 4.19 us
  blocking collectives: 7.45 us -> 0 us
  other arithmetic: 6.8 us -> 0.08 us
    dot_general x9 -> x0, matrix products: 56 us -> none  [the longest x1 9.07 us: body(): jnp.einsum('rf,pwf->prw', d_gate, gate_split, preferred_element_type=jnp....]
    pallas_call x0 -> x6, Pallas kernels: none -> 53.1 us  [the longest x2 20.8 us: forward(): pl.pallas_call(functools.partial(forward_kernel, plan, k), grid=(columns...]
    all_gather x1 -> x0, waiting for transfers between devices: 44.2 us -> none  [body(): gathered = lax.all_gather(stacked, 'dp', axis=0, tiled=True)]
    ppermute x0 -> x24, starting transfers between devices: none -> 37 us  [the longest x21 36.3 us: exchange(): out.append(lax.ppermute(sends[j], ('dp', 'expert'), pairs))]
    psum x1 -> x0, waiting for transfers between devices: 23.6 us -> none  [body(): lax.psum(part_h.astype(jnp.bfloat16), 'tensor').astype(jnp.float32)]
    reduce_scatter x1 -> x0, waiting for transfers between devices: 12.5 us -> none  [body(): lax.psum_scatter(placed.astype(jnp.bfloat16), 'dp', scatter_dimension=0,...]
    all_to_all x2 -> x0, starting transfers between devices: 7.87 us -> none  [the longest x1 4.21 us: body(): lax.all_to_all(x_exp[owner_expert], 'expert', split_axis=0, concat_axis=0...]
    all_to_all x1 -> x0, blocking collectives: 7.45 us -> none  [body(): lax.all_to_all(q_exp[owner_expert], 'expert', split_axis=0, concat_axis=0...]
  transfers between devices with their start and end apart: 5 -> 24, of which waited for: 4 -> 4; matrix products, arithmetic and copies ran while one was open for 15% -> 0% of each run, Pallas kernels for 0% -> 35%
where the time goes in v1:
time: 101 us; the launch traced here: 100 us
  Pallas kernels  53.1 us (53%)
  starting transfers between devices  37 us (37%)
  waiting for transfers between devices  5.22 us (5%)
  local copies, waits for them, and re-layouts  4.19 us (4%)
    ppermute x21, starting transfers between devices, exchange(): out.append(lax.ppermute(sends[j], ('dp', 'expert'), pairs))  36.3 us
    pallas_call x2, Pallas kernels, forward(): pl.pallas_call(functools.partial(forward_kernel, plan, k), grid=(columns...  20.8 us
    pallas_call x1, Pallas kernels, row_grads(): pl.pallas_call(functools.partial(rows_kernel, plan), grid=(columns // blo...  15.9 us
    pallas_call x1, Pallas kernels, weight_grads(): pl.pallas_call(functools.partial(weights_kernel, factor), grid=(columns /...  14.2 us
    ppermute x3, waiting for transfers between devices, swap(): return lax.ppermute(part, 'tensor', [(i, i ^ 1) for i in range(size)])  4.39 us
    unnamed x18, local copies, waits for them, and re-layouts  4.19 us
  transfers between devices with their start and end apart: 24, of which 4 were waited for; matrix products, arithmetic and copies ran while one was open for 0% of the time, Pallas kernels for 35%

profile of v1, /device:TPU:0, one launch (start us, length us, event | category | flops | bytes accessed | tf_op | source)
XLA Modules:
  0.0 100.4 jit_solution(13273004526224498718)
XLA Ops:
  0.6 0.1 pad_add_fusion.where_ref
  0.7 0.9 copy-done.2
  1.6 0.9 copy-done.3
  2.5 0.7 copy-done.4
  3.2 0.7 copy-done.5
  3.8 1.2 %dispatch.1 = (bf16[1,80,384]{2,1,0:T(8,128)(2,1)S(1)}, bf16[1,80,384]{2,1,0:T(8,128)(2,1)S(1)}, bf16[1,80,384]{2,1,0:T(8,128)(2,1)S(1)}, bf16[1,80,384]{2,1,0:T...) custom-call(s32[2]{0:T(128)S(1)} %pad_add_fusion.where_ref, ...), custom_call_target="tpu_custom_call" | custom-call | tf_op jit(solution)/shard_map/dispatch/pallas_call | solution.py:109
  5.1 3.1 %collective-permute-start = (bf16[1,80,384]{2,1,0:T(8,128)(2,1)S(1)}, bf16[1,80,384]{2,1,0:T(8,128)(2,1)S(1)}, u32[]{:S(2)}, u32[]{:S(2)}) collective-permute-start(bf16[1,80,384]{2,1,0:T(8,128)(2,1)S(1)} %get-tuple-element.42), channel_id=1, source_target_pairs={{0,4},{4,0},{8,12},{12,8},{2,6},{6,2},{10,14},{14,10},{1,5},{5,1},... | collective-permute-start | bytes 184328 | tf_op jit(solution)/shard_map/ppermute | solution.py:67
  8.1 2.6 %collective-permute-start.1 = (bf16[1,80,384]{2,1,0:T(8,128)(2,1)S(1)}, bf16[1,80,384]{2,1,0:T(8,128)(2,1)S(1)}, u32[]{:S(2)}, u32[]{:S(2)}) collective-permute-start(bf16[1,80,384]{2,1,0:T(8,128)(2,1)S(1)} %get-tuple-element.43), channel_id=1, source_target_pairs={{0,8},{4,12},{8,0},{12,4},{2,10},{6,14},{10,2},{14,6},{1,9},{5,13}... | collective-permute-start | bytes 184328 | tf_op jit(solution)/shard_map/ppermute | solution.py:67
  10.7 0.5 collective-permute-start.9
  11.2 0.0 collective-permute-start.10
  11.2 3.9 %collective-permute-start.11 = (bf16[1,80,384]{2,1,0:T(8,128)(2,1)S(1)}, bf16[1,80,384]{2,1,0:T(8,128)(2,1)S(1)}, u32[]{:S(2)}, u32[]{:S(2)}) collective-permute-start(bf16[1,80,384]{2,1,0:T(8,128)(2,1)S(1)} %get-tuple-element.54), channel_id=1, source_target_pairs={{0,12},{4,8},{8,4},{12,0},{2,14},{6,10},{10,6},{14,2},{1,13},{5,9}... | collective-permute-start | bytes 184328 | tf_op jit(solution)/shard_map/ppermute | solution.py:67
  15.1 0.0 collective-permute-done.refs_1_
  15.1 1.5 %collective-permute-start.12 = (bf16[1,80,384]{2,1,0:T(8,128)(2,1)S(1)}, bf16[1,80,384]{2,1,0:T(8,128)(2,1)S(1)}, u32[]{:S(2)}, u32[]{:S(2)}) collective-permute-start(bf16[1,80,384]{2,1,0:T(8,128)(2,1)S(1)} %get-tuple-element.55), channel_id=1, source_target_pairs={{0,2},{4,6},{8,10},{12,14},{2,0},{6,4},{10,8},{14,12},{1,3},{5,7},... | collective-permute-start | bytes 184328 | tf_op jit(solution)/shard_map/ppermute | solution.py:67
  16.6 0.0 collective-permute-done.1.refs_2_
  16.6 0.0 collective-permute-start.13
  16.6 0.0 collective-permute-done.9.refs_1_
  16.6 2.8 %collective-permute-start.14 = (bf16[1,80,384]{2,1,0:T(8,128)(2,1)S(1)}, bf16[1,80,384]{2,1,0:T(8,128)(2,1)S(1)}, u32[]{:S(2)}, u32[]{:S(2)}) collective-permute-start(bf16[1,80,384]{2,1,0:T(8,128)(2,1)S(1)} %get-tuple-element.57), channel_id=1, source_target_pairs={{0,10},{4,14},{8,2},{12,6},{2,8},{6,12},{10,0},{14,4},{1,11},{5,15... | collective-permute-start | bytes 184328 | tf_op jit(solution)/shard_map/ppermute | solution.py:67
  19.4 0.0 collective-permute-done.10.refs_2_
  19.5 3.4 %collective-permute-start.15 = (bf16[1,80,384]{2,1,0:T(8,128)(2,1)S(1)}, bf16[1,80,384]{2,1,0:T(8,128)(2,1)S(1)}, u32[]{:S(2)}, u32[]{:S(2)}) collective-permute-start(bf16[1,80,384]{2,1,0:T(8,128)(2,1)S(1)} %get-tuple-element.58), channel_id=1, source_target_pairs={{0,14},{4,10},{8,6},{12,2},{2,12},{6,8},{10,4},{14,0},{1,15},{5,11... | collective-permute-start | bytes 184328 | tf_op jit(solution)/shard_map/ppermute | solution.py:67
  22.8 0.0 collective-permute-done.11.refs_3_
  22.8 1.4 %collective-permute-start.2 = (bf16[1,80,384]{2,1,0:T(8,128)(2,1)S(1)}, bf16[1,80,384]{2,1,0:T(8,128)(2,1)S(1)}, u32[]{:S(2)}, u32[]{:S(2)}) collective-permute-start(bf16[1,80,384]{2,1,0:T(8,128)(2,1)S(1)} %get-tuple-element.44), channel_id=1, source_target_pairs={{0,12},{4,8},{8,4},{12,0},{2,14},{6,10},{10,6},{14,2},{1,13},{5,9}... | collective-permute-start | bytes 184328 | tf_op jit(solution)/shard_map/ppermute | solution.py:67
  24.2 0.0 collective-permute-done.12.refs_4_
  24.2 0.5 collective-permute-start.3
  24.7 0.0 collective-permute-done.13.refs_5_
  24.8 0.0 collective-permute-start.4
  24.8 0.5 collective-permute-done.14.refs_6_
  25.3 3.4 %collective-permute-start.5 = (bf16[1,80,384]{2,1,0:T(8,128)(2,1)S(1)}, bf16[1,80,384]{2,1,0:T(8,128)(2,1)S(1)}, u32[]{:S(2)}, u32[]{:S(2)}) collective-permute-start(bf16[1,80,384]{2,1,0:T(8,128)(2,1)S(1)} %get-tuple-element.47), channel_id=1, source_target_pairs={{0,10},{4,14},{8,2},{12,6},{2,8},{6,12},{10,0},{14,4},{1,11},{5,15... | collective-permute-start | bytes 184328 | tf_op jit(solution)/shard_map/ppermute | solution.py:67
  28.7 0.0 collective-permute-done.15.refs_7_
  28.7 2.3 %collective-permute-start.6 = (bf16[1,80,384]{2,1,0:T(8,128)(2,1)S(1)}, bf16[1,80,384]{2,1,0:T(8,128)(2,1)S(1)}, u32[]{:S(2)}, u32[]{:S(2)}) collective-permute-start(bf16[1,80,384]{2,1,0:T(8,128)(2,1)S(1)} %get-tuple-element.48), channel_id=1, source_target_pairs={{0,14},{4,10},{8,6},{12,2},{2,12},{6,8},{10,4},{14,0},{1,15},{5,11... | collective-permute-start | bytes 184328 | tf_op jit(solution)/shard_map/ppermute | solution.py:67
  31.0 8.4 %forward_h.1 = (bf16[160,1536]{1,0:T(8,128)(2,1)S(1)}, bf16[160,4096]{1,0:T(8,128)(2,1)S(1)}) custom-call(s32[2]{0:T(128)S(1)} %pad_add_fusion.where_ref, bf16[1,80,384]{2,1,0:T(8,128)(2,1)S(1)} %get-tuple-element.51.refs_0_, bf16[1,80,384]{2,1,0:T(8,128)(2,1)S(1)} %collective-permute-done.9.refs_1_, ...), custom_call_target="tpu_custom_call" | custom-call | flops 2013265920 | bytes 12582912 | tf_op jit(solution)/shard_map/forward_h/pallas_call | solution.py:151
  39.3 0.0 copy-start
  39.4 0.0 collective-permute-done.2.refs_3_
  39.4 0.1 collective-permute-start.16
  39.4 0.0 collective-permute-done.3.refs_4_
  39.5 0.0 collective-permute-done.4.refs_5_
  39.5 0.0 collective-permute-done.5.refs_6_
  39.5 0.0 collective-permute-done.6.refs_7_
  39.5 12.4 %forward_gu.1 = (bf16[160,1536]{1,0:T(8,128)(2,1)S(1)}, bf16[160,4096]{1,0:T(8,128)(2,1)S(1)}, bf16[160,4096]{1,0:T(8,128)(2,1)S(1)}) custom-call(s32[2]{0:T(128)S(1)} %pad_add_fusion.where_ref, bf16[1,80,384]{2,1,0:T(8,128)(2,1)S(1)} %get-tuple-element.41.refs_0_, bf16[1,80,384]{2,1,0:T(8,128)(2,1)S(1)} %collective-permute-done.refs_1_, ...), custom_call_target="tpu_custom_call" | custom-call | flops 4026531840 | bytes 25165824 | tf_op jit(solution)/shard_map/forward_gu/pallas_call | solution.py:151
  51.9 0.0 copy-done
  51.9 0.0 copy-start.1
  52.0 0.2 collective-permute-start.7
  52.2 0.4 collective-permute-start.8
  52.5 0.0 collective-permute-done.16.d1
  52.5 2.5 %collective-permute-done.7.g1 = bf16[160,4096]{1,0:T(8,128)(2,1)S(1)} collective-permute-done((bf16[160,4096]{1,0:T(8,128)(2,1)S(1)}, bf16[160,4096]{1,0:T(8,128)(2,1)S(1)}, u32[]{:S(2)}, u32[]{:S(2)}) %collective-permute-start.7) | collective-permute-done | bytes 1310752 | tf_op jit(solution)/shard_map/ppermute | solution.py:282
  55.1 1.9 %collective-permute-done.8.u1 = bf16[160,4096]{1,0:T(8,128)(2,1)S(1)} collective-permute-done((bf16[160,4096]{1,0:T(8,128)(2,1)S(1)}, bf16[160,4096]{1,0:T(8,128)(2,1)S(1)}, u32[]{:S(2)}, u32[]{:S(2)}) %collective-permute-start.8) | collective-permute-done | bytes 1310752 | tf_op jit(solution)/shard_map/ppermute | solution.py:282
  56.9 0.0 copy-start.8
  57.0 1.0 %copy-done.8 = bf16[160,4096]{1,0:T(8,128)(2,1)} copy-done((bf16[160,4096]{1,0:T(8,128)(2,1)}, bf16[160,4096]{1,0:T(8,128)(2,1)S(1)}, u32[]{:S(2)}) %copy-start.8) | copy-done | bytes 1310744
  58.0 15.9 %row_grads.1 = (bf16[160,4096]{1,0:T(8,128)(2,1)S(1)}, bf16[160,4096]{1,0:T(8,128)(2,1)S(1)}, bf16[160,4096]{1,0:T(8,128)(2,1)S(1)}, bf16[1,80,384]{2,1,0:T(8,12...) custom-call(s32[2]{0:T(128)S(1)} %pad_add_fusion.where_ref, ...), custom_call_target="tpu_custom_call" | custom-call | flops 4026531840 | bytes 25165824 | tf_op jit(solution)/shard_map/row_grads/pallas_call | solution.py:204
  73.9 0.1 collective-permute-start.17
  74.0 3.0 %collective-permute-start.18 = (bf16[1,80,384]{2,1,0:T(8,128)(2,1)S(1)}, bf16[1,80,384]{2,1,0:T(8,128)(2,1)S(1)}, u32[]{:S(2)}, u32[]{:S(2)}) collective-permute-start(bf16[1,80,384]{2,1,0:T(8,128)(2,1)S(1)} %get-tuple-element.62), channel_id=1, source_target_pairs={{0,8},{4,12},{8,0},{12,4},{2,10},{6,14},{10,2},{14,6},{1,9},{5,13}... | collective-permute-start | bytes 184328 | tf_op jit(solution)/shard_map/ppermute | solution.py:67
  77.0 1.4 %collective-permute-start.19 = (bf16[1,80,384]{2,1,0:T(8,128)(2,1)S(1)}, bf16[1,80,384]{2,1,0:T(8,128)(2,1)S(1)}, u32[]{:S(2)}, u32[]{:S(2)}) collective-permute-start(bf16[1,80,384]{2,1,0:T(8,128)(2,1)S(1)} %get-tuple-element.63), channel_id=1, source_target_pairs={{0,12},{4,8},{8,4},{12,0},{2,14},{6,10},{10,6},{14,2},{1,13},{5,9}... | collective-permute-start | bytes 184328 | tf_op jit(solution)/shard_map/ppermute | solution.py:67
  78.3 0.5 collective-permute-start.20
  78.9 0.1 collective-permute-start.21
  79.0 0.2 collective-permute-done.17.rest_1_
  79.2 3.6 %collective-permute-start.22 = (bf16[1,80,384]{2,1,0:T(8,128)(2,1)S(1)}, bf16[1,80,384]{2,1,0:T(8,128)(2,1)S(1)}, u32[]{:S(2)}, u32[]{:S(2)}) collective-permute-start(bf16[1,80,384]{2,1,0:T(8,128)(2,1)S(1)} %get-tuple-element.66), channel_id=1, source_target_pairs={{0,10},{4,14},{8,2},{12,6},{2,8},{6,12},{10,0},{14,4},{1,11},{5,15... | collective-permute-start | bytes 184328 | tf_op jit(solution)/shard_map/ppermute | solution.py:67
  82.8 0.0 collective-permute-done.18.rest_2_
  82.8 2.3 %collective-permute-start.23 = (bf16[1,80,384]{2,1,0:T(8,128)(2,1)S(1)}, bf16[1,80,384]{2,1,0:T(8,128)(2,1)S(1)}, u32[]{:S(2)}, u32[]{:S(2)}) collective-permute-start(bf16[1,80,384]{2,1,0:T(8,128)(2,1)S(1)} %get-tuple-element.67), channel_id=1, source_target_pairs={{0,14},{4,10},{8,6},{12,2},{2,12},{6,8},{10,4},{14,0},{1,15},{5,11... | collective-permute-start | bytes 184328 | tf_op jit(solution)/shard_map/ppermute | solution.py:67
  85.1 14.2 %weight_grads.1 = (bf16[1536,4096]{1,0:T(8,128)(2,1)}, bf16[1536,4096]{1,0:T(8,128)(2,1)}, bf16[1536,4096]{1,0:T(8,128)(2,1)}) custom-call(bf16[160,1536]{1,0:T(8,128)(2,1)S(1)} %get-tuple-element.68.x_ref, bf16[160,1536]{1,0:T(8,128)(2,1)S(1)} %get-tuple-element.69.q_ref, bf16[160,4096]{1,0:T(8,128)(2,1)S(1)} %get-tuple-element.70.dg_ref, ...), custom_call_target="tpu_custom_call" | custom-call | flops 6039797760 | bytes 37748736 | tf_op jit(solution)/shard_map/weight_grads/pallas_call | solution.py:232
  99.3 0.0 collective-permute-done.19.rest_3_
  99.3 0.0 collective-permute-done.20.rest_4_
  99.3 0.0 collective-permute-done.21.rest_5_
  99.3 0.0 collective-permute-done.22.rest_6_
  99.3 0.0 collective-permute-done.23.rest_7_
  99.3 1.0 %combine.1 = bf16[128,384]{1,0:T(8,128)(2,1)} custom-call(bf16[8,80,128]{2,1,0:T(8,128)(2,1)S(1)} %get-tuple-element.40.sel_ref, bf16[1,80,384]{2,1,0:T(8,128)(2,1)S(1)} %get-tuple-element.60.rest_0_, bf16[1,80,384]{2,1,0:T(8,128)(2,1)S(1)} %collective-permute-done.17.rest_1_, bf16[1,80,384]{2,1,0:T(8,128)(2,1)S(1)} %collective-permute-done.18.rest_2_, ...), custom_call_target="tpu_custom_call" | custom-call | tf_op jit(solution)/shard_map/combine/pallas_call | solution.py:263
  (9 shorter events, 0.0 us)
Async XLA Ops:
  0.7 0.9 copy-start.2
  1.6 0.9 copy-start.3
  2.5 0.7 copy-start.4
  3.2 0.7 copy-start.5
  5.1 10.1 %collective-permute-start = (bf16[1,80,384]{2,1,0:T(8,128)(2,1)S(1)}, bf16[1,80,384]{2,1,0:T(8,128)(2,1)S(1)}, u32[]{:S(2)}, u32[]{:S(2)}) collective-permute-start(bf16[1,80,384]{2,1,0:T(8,128)(2,1)S(1)} %get-tuple-element.42), channel_id=1, source_target_pairs={{0,4},{4,0},{8,12},{12,8},{2,6},{6,2},{10,14},{14,10},{1,5},{5,1},... | collective-permute-start | bytes 184328 | tf_op jit(solution)/shard_map/ppermute | solution.py:67
  8.1 8.5 %collective-permute-start.1 = (bf16[1,80,384]{2,1,0:T(8,128)(2,1)S(1)}, bf16[1,80,384]{2,1,0:T(8,128)(2,1)S(1)}, u32[]{:S(2)}, u32[]{:S(2)}) collective-permute-start(bf16[1,80,384]{2,1,0:T(8,128)(2,1)S(1)} %get-tuple-element.43), channel_id=1, source_target_pairs={{0,8},{4,12},{8,0},{12,4},{2,10},{6,14},{10,2},{14,6},{1,9},{5,13}... | collective-permute-start | bytes 184328 | tf_op jit(solution)/shard_map/ppermute | solution.py:67
  10.7 5.9 %collective-permute-start.9 = (bf16[1,80,384]{2,1,0:T(8,128)(2,1)S(1)}, bf16[1,80,384]{2,1,0:T(8,128)(2,1)S(1)}, u32[]{:S(2)}, u32[]{:S(2)}) collective-permute-start(bf16[1,80,384]{2,1,0:T(8,128)(2,1)S(1)} %get-tuple-element.52), channel_id=1, source_target_pairs={{0,4},{4,0},{8,12},{12,8},{2,6},{6,2},{10,14},{14,10},{1,5},{5,1},... | collective-permute-start | bytes 184328 | tf_op jit(solution)/shard_map/ppermute | solution.py:67
  11.2 8.3 %collective-permute-start.10 = (bf16[1,80,384]{2,1,0:T(8,128)(2,1)S(1)}, bf16[1,80,384]{2,1,0:T(8,128)(2,1)S(1)}, u32[]{:S(2)}, u32[]{:S(2)}) collective-permute-start(bf16[1,80,384]{2,1,0:T(8,128)(2,1)S(1)} %get-tuple-element.53), channel_id=1, source_target_pairs={{0,8},{4,12},{8,0},{12,4},{2,10},{6,14},{10,2},{14,6},{1,9},{5,13}... | collective-permute-start | bytes 184328 | tf_op jit(solution)/shard_map/ppermute | solution.py:67
  11.2 11.7 %collective-permute-start.11 = (bf16[1,80,384]{2,1,0:T(8,128)(2,1)S(1)}, bf16[1,80,384]{2,1,0:T(8,128)(2,1)S(1)}, u32[]{:S(2)}, u32[]{:S(2)}) collective-permute-start(bf16[1,80,384]{2,1,0:T(8,128)(2,1)S(1)} %get-tuple-element.54), channel_id=1, source_target_pairs={{0,12},{4,8},{8,4},{12,0},{2,14},{6,10},{10,6},{14,2},{1,13},{5,9}... | collective-permute-start | bytes 184328 | tf_op jit(solution)/shard_map/ppermute | solution.py:67
  15.1 9.1 %collective-permute-start.12 = (bf16[1,80,384]{2,1,0:T(8,128)(2,1)S(1)}, bf16[1,80,384]{2,1,0:T(8,128)(2,1)S(1)}, u32[]{:S(2)}, u32[]{:S(2)}) collective-permute-start(bf16[1,80,384]{2,1,0:T(8,128)(2,1)S(1)} %get-tuple-element.55), channel_id=1, source_target_pairs={{0,2},{4,6},{8,10},{12,14},{2,0},{6,4},{10,8},{14,12},{1,3},{5,7},... | collective-permute-start | bytes 184328 | tf_op jit(solution)/shard_map/ppermute | solution.py:67
  16.6 8.1 %collective-permute-start.13 = (bf16[1,80,384]{2,1,0:T(8,128)(2,1)S(1)}, bf16[1,80,384]{2,1,0:T(8,128)(2,1)S(1)}, u32[]{:S(2)}, u32[]{:S(2)}) collective-permute-start(bf16[1,80,384]{2,1,0:T(8,128)(2,1)S(1)} %get-tuple-element.56), channel_id=1, source_target_pairs={{0,6},{4,2},{8,14},{12,10},{2,4},{6,0},{10,12},{14,8},{1,7},{5,3},... | collective-permute-start | bytes 184328 | tf_op jit(solution)/shard_map/ppermute | solution.py:67
  16.6 8.7 %collective-permute-start.14 = (bf16[1,80,384]{2,1,0:T(8,128)(2,1)S(1)}, bf16[1,80,384]{2,1,0:T(8,128)(2,1)S(1)}, u32[]{:S(2)}, u32[]{:S(2)}) collective-permute-start(bf16[1,80,384]{2,1,0:T(8,128)(2,1)S(1)} %get-tuple-element.57), channel_id=1, source_target_pairs={{0,10},{4,14},{8,2},{12,6},{2,8},{6,12},{10,0},{14,4},{1,11},{5,15... | collective-permute-start | bytes 184328 | tf_op jit(solution)/shard_map/ppermute | solution.py:67
  19.5 9.2 %collective-permute-start.15 = (bf16[1,80,384]{2,1,0:T(8,128)(2,1)S(1)}, bf16[1,80,384]{2,1,0:T(8,128)(2,1)S(1)}, u32[]{:S(2)}, u32[]{:S(2)}) collective-permute-start(bf16[1,80,384]{2,1,0:T(8,128)(2,1)S(1)} %get-tuple-element.58), channel_id=1, source_target_pairs={{0,14},{4,10},{8,6},{12,2},{2,12},{6,8},{10,4},{14,0},{1,15},{5,11... | collective-permute-start | bytes 184328 | tf_op jit(solution)/shard_map/ppermute | solution.py:67
  22.8 16.5 %collective-permute-start.2 = (bf16[1,80,384]{2,1,0:T(8,128)(2,1)S(1)}, bf16[1,80,384]{2,1,0:T(8,128)(2,1)S(1)}, u32[]{:S(2)}, u32[]{:S(2)}) collective-permute-start(bf16[1,80,384]{2,1,0:T(8,128)(2,1)S(1)} %get-tuple-element.44), channel_id=1, source_target_pairs={{0,12},{4,8},{8,4},{12,0},{2,14},{6,10},{10,6},{14,2},{1,13},{5,9}... | collective-permute-start | bytes 184328 | tf_op jit(solution)/shard_map/ppermute | solution.py:67
  24.2 15.2 %collective-permute-start.3 = (bf16[1,80,384]{2,1,0:T(8,128)(2,1)S(1)}, bf16[1,80,384]{2,1,0:T(8,128)(2,1)S(1)}, u32[]{:S(2)}, u32[]{:S(2)}) collective-permute-start(bf16[1,80,384]{2,1,0:T(8,128)(2,1)S(1)} %get-tuple-element.45), channel_id=1, source_target_pairs={{0,2},{4,6},{8,10},{12,14},{2,0},{6,4},{10,8},{14,12},{1,3},{5,7},... | collective-permute-start | bytes 184328 | tf_op jit(solution)/shard_map/ppermute | solution.py:67
  24.8 14.7 %collective-permute-start.4 = (bf16[1,80,384]{2,1,0:T(8,128)(2,1)S(1)}, bf16[1,80,384]{2,1,0:T(8,128)(2,1)S(1)}, u32[]{:S(2)}, u32[]{:S(2)}) collective-permute-start(bf16[1,80,384]{2,1,0:T(8,128)(2,1)S(1)} %get-tuple-element.46), channel_id=1, source_target_pairs={{0,6},{4,2},{8,14},{12,10},{2,4},{6,0},{10,12},{14,8},{1,7},{5,3},... | collective-permute-start | bytes 184328 | tf_op jit(solution)/shard_map/ppermute | solution.py:67
  25.3 14.2 %collective-permute-start.5 = (bf16[1,80,384]{2,1,0:T(8,128)(2,1)S(1)}, bf16[1,80,384]{2,1,0:T(8,128)(2,1)S(1)}, u32[]{:S(2)}, u32[]{:S(2)}) collective-permute-start(bf16[1,80,384]{2,1,0:T(8,128)(2,1)S(1)} %get-tuple-element.47), channel_id=1, source_target_pairs={{0,10},{4,14},{8,2},{12,6},{2,8},{6,12},{10,0},{14,4},{1,11},{5,15... | collective-permute-start | bytes 184328 | tf_op jit(solution)/shard_map/ppermute | solution.py:67
  28.7 10.8 %collective-permute-start.6 = (bf16[1,80,384]{2,1,0:T(8,128)(2,1)S(1)}, bf16[1,80,384]{2,1,0:T(8,128)(2,1)S(1)}, u32[]{:S(2)}, u32[]{:S(2)}) collective-permute-start(bf16[1,80,384]{2,1,0:T(8,128)(2,1)S(1)} %get-tuple-element.48), channel_id=1, source_target_pairs={{0,14},{4,10},{8,6},{12,2},{2,12},{6,8},{10,4},{14,0},{1,15},{5,11... | collective-permute-start | bytes 184328 | tf_op jit(solution)/shard_map/ppermute | solution.py:67
  39.3 12.6 %copy-start = (bf16[160,4096]{1,0:T(8,128)(2,1)}, bf16[160,4096]{1,0:T(8,128)(2,1)S(1)}, u32[]{:S(2)}) copy-start(bf16[160,4096]{1,0:T(8,128)(2,1)S(1)} %get-tuple-element.59.d0) | copy-start | bytes 3932164
  39.4 13.2 %collective-permute-start.16 = (bf16[160,4096]{1,0:T(8,128)(2,1)S(1)}, bf16[160,4096]{1,0:T(8,128)(2,1)S(1)}, u32[]{:S(2)}, u32[]{:S(2)}) collective-permute-start(bf16[160,4096]{1,0:T(8,128)(2,1)S(1)} %get-tuple-element.59.d0), channel_id=1, source_target_pairs={{0,1},{1,0},{2,3},{3,2},{4,5},{5,4},{6,7},{7,6},{8,9},{9,8},{10,11... | collective-permute-start | bytes 3932168 | tf_op jit(solution)/shard_map/ppermute | solution.py:282
  51.9 5.0 %copy-start.1 = (bf16[160,4096]{1,0:T(8,128)(2,1)}, bf16[160,4096]{1,0:T(8,128)(2,1)S(1)}, u32[]{:S(2)}) copy-start(bf16[160,4096]{1,0:T(8,128)(2,1)S(1)} %get-tuple-element.50.u0) | copy-start | bytes 3932164
  52.0 3.1 %collective-permute-start.7 = (bf16[160,4096]{1,0:T(8,128)(2,1)S(1)}, bf16[160,4096]{1,0:T(8,128)(2,1)S(1)}, u32[]{:S(2)}, u32[]{:S(2)}) collective-permute-start(bf16[160,4096]{1,0:T(8,128)(2,1)S(1)} %get-tuple-element.49.g0), channel_id=1, source_target_pairs={{0,1},{1,0},{2,3},{3,2},{4,5},{5,4},{6,7},{7,6},{8,9},{9,8},{10,11... | collective-permute-start | bytes 3932168 | tf_op jit(solution)/shard_map/ppermute | solution.py:282
  52.2 4.8 %collective-permute-start.8 = (bf16[160,4096]{1,0:T(8,128)(2,1)S(1)}, bf16[160,4096]{1,0:T(8,128)(2,1)S(1)}, u32[]{:S(2)}, u32[]{:S(2)}) collective-permute-start(bf16[160,4096]{1,0:T(8,128)(2,1)S(1)} %get-tuple-element.50.u0), channel_id=1, source_target_pairs={{0,1},{1,0},{2,3},{3,2},{4,5},{5,4},{6,7},{7,6},{8,9},{9,8},{10,11... | collective-permute-start | bytes 3932168 | tf_op jit(solution)/shard_map/ppermute | solution.py:282
  52.5 4.4 %copy-start.6 = (bf16[160,4096]{1,0:T(8,128)(2,1)}, bf16[160,4096]{1,0:T(8,128)(2,1)S(1)}, u32[]{:S(2)}) copy-start(bf16[160,4096]{1,0:T(8,128)(2,1)S(1)} %collective-permute-done.16.d1) | copy-start | bytes 3932164
  55.1 1.9 %copy-start.7 = (bf16[160,4096]{1,0:T(8,128)(2,1)}, bf16[160,4096]{1,0:T(8,128)(2,1)S(1)}, u32[]{:S(2)}) copy-start(bf16[160,4096]{1,0:T(8,128)(2,1)S(1)} %collective-permute-done.7.g1) | copy-start | bytes 3932164
  56.9 1.1 %copy-start.8 = (bf16[160,4096]{1,0:T(8,128)(2,1)}, bf16[160,4096]{1,0:T(8,128)(2,1)S(1)}, u32[]{:S(2)}) copy-start(bf16[160,4096]{1,0:T(8,128)(2,1)S(1)} %collective-permute-done.8.u1) | copy-start | bytes 3932164
  73.9 5.3 %collective-permute-start.17 = (bf16[1,80,384]{2,1,0:T(8,128)(2,1)S(1)}, bf16[1,80,384]{2,1,0:T(8,128)(2,1)S(1)}, u32[]{:S(2)}, u32[]{:S(2)}) collective-permute-start(bf16[1,80,384]{2,1,0:T(8,128)(2,1)S(1)} %get-tuple-element.61), channel_id=1, source_target_pairs={{0,4},{4,0},{8,12},{12,8},{2,6},{6,2},{10,14},{14,10},{1,5},{5,1},... | collective-permute-start | bytes 184328 | tf_op jit(solution)/shard_map/ppermute | solution.py:67
  74.0 8.8 %collective-permute-start.18 = (bf16[1,80,384]{2,1,0:T(8,128)(2,1)S(1)}, bf16[1,80,384]{2,1,0:T(8,128)(2,1)S(1)}, u32[]{:S(2)}, u32[]{:S(2)}) collective-permute-start(bf16[1,80,384]{2,1,0:T(8,128)(2,1)S(1)} %get-tuple-element.62), channel_id=1, source_target_pairs={{0,8},{4,12},{8,0},{12,4},{2,10},{6,14},{10,2},{14,6},{1,9},{5,13}... | collective-permute-start | bytes 184328 | tf_op jit(solution)/shard_map/ppermute | solution.py:67
  77.0 22.3 %collective-permute-start.19 = (bf16[1,80,384]{2,1,0:T(8,128)(2,1)S(1)}, bf16[1,80,384]{2,1,0:T(8,128)(2,1)S(1)}, u32[]{:S(2)}, u32[]{:S(2)}) collective-permute-start(bf16[1,80,384]{2,1,0:T(8,128)(2,1)S(1)} %get-tuple-element.63), channel_id=1, source_target_pairs={{0,12},{4,8},{8,4},{12,0},{2,14},{6,10},{10,6},{14,2},{1,13},{5,9}... | collective-permute-start | bytes 184328 | tf_op jit(solution)/shard_map/ppermute | solution.py:67
  78.3 21.0 %collective-permute-start.20 = (bf16[1,80,384]{2,1,0:T(8,128)(2,1)S(1)}, bf16[1,80,384]{2,1,0:T(8,128)(2,1)S(1)}, u32[]{:S(2)}, u32[]{:S(2)}) collective-permute-start(bf16[1,80,384]{2,1,0:T(8,128)(2,1)S(1)} %get-tuple-element.64), channel_id=1, source_target_pairs={{0,2},{4,6},{8,10},{12,14},{2,0},{6,4},{10,8},{14,12},{1,3},{5,7},... | collective-permute-start | bytes 184328 | tf_op jit(solution)/shard_map/ppermute | solution.py:67
  78.9 20.4 %collective-permute-start.21 = (bf16[1,80,384]{2,1,0:T(8,128)(2,1)S(1)}, bf16[1,80,384]{2,1,0:T(8,128)(2,1)S(1)}, u32[]{:S(2)}, u32[]{:S(2)}) collective-permute-start(bf16[1,80,384]{2,1,0:T(8,128)(2,1)S(1)} %get-tuple-element.65), channel_id=1, source_target_pairs={{0,6},{4,2},{8,14},{12,10},{2,4},{6,0},{10,12},{14,8},{1,7},{5,3},... | collective-permute-start | bytes 184328 | tf_op jit(solution)/shard_map/ppermute | solution.py:67
  79.2 20.1 %collective-permute-start.22 = (bf16[1,80,384]{2,1,0:T(8,128)(2,1)S(1)}, bf16[1,80,384]{2,1,0:T(8,128)(2,1)S(1)}, u32[]{:S(2)}, u32[]{:S(2)}) collective-permute-start(bf16[1,80,384]{2,1,0:T(8,128)(2,1)S(1)} %get-tuple-element.66), channel_id=1, source_target_pairs={{0,10},{4,14},{8,2},{12,6},{2,8},{6,12},{10,0},{14,4},{1,11},{5,15... | collective-permute-start | bytes 184328 | tf_op jit(solution)/shard_map/ppermute | solution.py:67
  82.8 16.5 %collective-permute-start.23 = (bf16[1,80,384]{2,1,0:T(8,128)(2,1)S(1)}, bf16[1,80,384]{2,1,0:T(8,128)(2,1)S(1)}, u32[]{:S(2)}, u32[]{:S(2)}) collective-permute-start(bf16[1,80,384]{2,1,0:T(8,128)(2,1)S(1)} %get-tuple-element.67), channel_id=1, source_target_pairs={{0,14},{4,10},{8,6},{12,2},{2,12},{6,8},{10,4},{14,0},{1,15},{5,11... | collective-permute-start | bytes 184328 | tf_op jit(solution)/shard_map/ppermute | solution.py:67

commit v2 on v1

v2 whole, which is shorter than its diff:
```python
import functools
import math

import jax
import jax.numpy as jnp
from jax import lax
from jax.experimental import pallas as pl
from jax.experimental.pallas import tpu as pltpu
from jax.sharding import PartitionSpec as P

FF = 8192
EXPERTS = 4
CAP = 80
F32 = jnp.float32
BF16 = jnp.bfloat16
PARTNERS = ((0, 0), (1, 0), (0, 2), (1, 2))
TURNED = (((1,), (1,)), ((), ()))
BOTH_FIRST = (((0,), (0,)), ((), ()))
VMEM = pl.BlockSpec(memory_space=pltpu.VMEM)
SMEM = pl.BlockSpec(memory_space=pltpu.SMEM)
ANY = pl.BlockSpec(memory_space=pl.ANY)
HBM = pl.BlockSpec(memory_space=pltpu.HBM)


def params(mebibytes):
    return pltpu.CompilerParams(vmem_limit_bytes=mebibytes * 1024 * 1024)


def cost(flops, moved):
    return pl.CostEstimate(flops=flops, bytes_accessed=moved, transcendentals=0)


def block_of(size, wanted):
    while size % wanted:
        wanted //= 2
    return wanted


class Plan:
    def __init__(self, mesh, columns):
        self.owners = mesh.shape["expert"]
        self.replicas = mesh.shape["dp"]
        self.devices = self.owners * self.replicas
        self.rows = self.owners * CAP
        self.columns = columns
        self.hops = self.owners == 2 and self.replicas == 4 and 2 * columns == FF

    def expert_of(self, x, z):
        return (x * self.replicas + z) * self.columns // FF

    def send(self, array, dx, dz):
        pairs = []
        for x in range(self.owners):
            for z in range(self.replicas):
                pairs.append((z * self.owners + x, (z ^ dz) * self.owners + (x ^ dx)))
        return lax.ppermute(array, ("dp", "expert"), pairs)

    def scatter(self, array):
        return lax.all_to_all(array, ("dp", "expert"), 0, 0, tiled=True)


def dispatch_kernel(plan, where_ref, ids_ref, gates_ref, tok_ref, cot_ref, sel_ref, *send_refs):
    count = tok_ref.shape[0]
    first, second = ids_ref[0:1, :], ids_ref[1:2, :]
    gate_first, gate_second = gates_ref[0:1, :].astype(F32), gates_ref[1:2, :].astype(F32)
    row = lax.broadcasted_iota(jnp.int32, (16, count), 0)
    named = ((row == first) | (row == second)).astype(F32)
    earlier = lax.broadcasted_iota(jnp.int32, (count, count), 0) < lax.broadcasted_iota(jnp.int32, (count, count), 1)
    before = jnp.dot(named.astype(BF16), earlier.astype(F32).astype(BF16), preferred_element_type=F32)
    slot = lax.broadcasted_iota(jnp.int32, (CAP, count), 0).astype(F32)

    def rows_for(expert):
        mine = row == expert
        position = jnp.sum(jnp.where(mine, before, 0.0), axis=0, keepdims=True)
        here = jnp.sum(jnp.where(mine, named, 0.0), axis=0, keepdims=True)
        chosen = jnp.where((position == slot) & (here > 0.5), 1.0, 0.0)
        gate = jnp.sum(chosen * jnp.where(first == expert, gate_first, gate_second), axis=1, keepdims=True)
        chosen = chosen.astype(BF16)
        x_rows = jnp.dot(chosen, tok_ref[...], preferred_element_type=F32).astype(BF16)
        q_rows = (gate * jnp.dot(chosen, cot_ref[...], preferred_element_type=F32)).astype(BF16)
        return chosen, x_rows, q_rows

    if plan.hops:
        for at, (dx, dz) in enumerate(PARTNERS):
            expert = plan.expert_of(jnp.bitwise_xor(where_ref[0], dx), jnp.bitwise_xor(where_ref[1], dz))
            sel_ref[at], send_refs[at][0, 0:CAP, :], send_refs[at][0, CAP : 2 * CAP, :] = rows_for(expert)
        return
    for expert in range(EXPERTS):
        chosen, x_rows, q_rows = rows_for(expert)
        sel_ref[expert] = chosen
        for z in range(plan.replicas):
            for x in range(plan.owners):
                if plan.expert_of(x, z) == expert:
                    send_refs[0][z * plan.owners + x, 0:CAP, :] = x_rows
                    send_refs[0][z * plan.owners + x, CAP : 2 * CAP, :] = q_rows


def dispatch(plan, where, ids, gates, tokens, cotangent, fetched):
    count, narrow = tokens.shape
    sends = [jax.ShapeDtypeStruct((1, 2 * CAP, narrow), BF16)] * len(PARTNERS)
    if not plan.hops:
        sends = [jax.ShapeDtypeStruct((plan.devices, 2 * CAP, narrow), BF16)]
    got = pl.pallas_call(
        functools.partial(dispatch_kernel, plan),
        out_shape=[jax.ShapeDtypeStruct((EXPERTS, CAP, count), BF16)] + sends,
        in_specs=[SMEM] + [VMEM] * 4,
        out_specs=[VMEM] * (1 + len(sends)),
        compiler_params=params(8),
        cost_estimate=cost(400 * fetched, fetched),
        name="dispatch",
    )(where, ids.T, gates.T, tokens, cotangent)
    return got[0], got[1:]


def forward_kernel(plan, half, block, *refs):
    part_ref = refs[-1]
    if half is None:
        rows_ref, w_ref = refs[:2]
    else:
        where_ref, pieces, w_ref, rows_ref = refs[0], refs[1:-3], refs[-3], refs[-2]
        narrow = pieces[0].shape[2]
        for z in range(plan.replicas):
            if plan.hops:
                index = jnp.bitwise_xor(where_ref[1], z)
                lanes = pl.ds(pl.multiple_of(index * narrow, 128), narrow)
            else:
                lanes = pl.ds(z * narrow, narrow)
            for x in range(plan.owners):
                at = z * plan.owners + x
                piece = pieces[at] if plan.hops else pieces[0].at[pl.ds(at, 1)]
                rows_ref[x * CAP : (x + 1) * CAP, lanes] = piece[0, half * CAP : (half + 1) * CAP, :]
    for start in range(0, w_ref.shape[1], block):
        cols = pl.ds(start, block)
        part_ref[:, cols] = jnp.dot(rows_ref[...], w_ref[:, cols], preferred_element_type=F32).astype(BF16)


def forward(plan, where, rows_in, half, w, name, wanted=512):
    width, columns = w.shape
    block = block_of(columns, wanted)
    fresh = half is not None
    outs = [jax.ShapeDtypeStruct((plan.rows, width), BF16)] * fresh
    outs.append(jax.ShapeDtypeStruct((plan.rows, columns), BF16))
    return pl.pallas_call(
        functools.partial(forward_kernel, plan, half, block),
        out_shape=outs,
        in_specs=[SMEM] * fresh + [VMEM] * (1 + len(rows_in)),
        out_specs=[VMEM] * len(outs),
        compiler_params=params(4),
        cost_estimate=cost(2 * plan.rows * width * columns, 8 * 1024 * 1024),
        name=name,
    )(*([where] * fresh), *rows_in, w)


def rows_kernel(plan, where_ref, g0, g1, u0, u1, d0, d1, wg_ref, wu_ref, h_ref, dg_ref, du_ref, *rest):
    outs, total = rest[:-1], rest[-1]
    gate = g0[...].astype(F32) + g1[...].astype(F32)
    up = u0[...].astype(F32) + u1[...].astype(F32)
    hidden = d0[...].astype(F32) + d1[...].astype(F32)
    sigma = jax.nn.sigmoid(gate)
    act = sigma * gate
    h_ref[...] = (act * up).astype(BF16)
    d_gate = (hidden * up * sigma * (1.0 + gate * (1.0 - sigma))).astype(BF16)
    d_up = (hidden * act).astype(BF16)
    dg_ref[...] = d_gate
    du_ref[...] = d_up
    term = lax.dot_general(d_gate, wg_ref[...], TURNED, preferred_element_type=F32)
    term = term + lax.dot_general(d_up, wu_ref[...], TURNED, preferred_element_type=F32)
    step = pl.program_id(0)

    @pl.when(step == 0)
    def _():
        total[...] = term

    @pl.when(step > 0)
    def _():
        total[...] += term

    @pl.when(step == pl.num_programs(0) - 1)
    def _():
        narrow = outs[0].shape[2]
        for z in range(plan.replicas):
            if plan.hops:
                index = jnp.bitwise_xor(where_ref[1], z)
                lanes = pl.ds(pl.multiple_of(index * narrow, 128), narrow)
            else:
                lanes = pl.ds(z * narrow, narrow)
            for x in range(plan.owners):
                at = z // 2 * plan.owners + x if plan.hops else z * plan.owners + x
                outs[z % len(outs)][at] = total[x * CAP : (x + 1) * CAP, lanes].astype(BF16)


def row_grads(plan, where, parts, wg, wu, wanted=1024):
    width, columns = wg.shape
    narrow = width // plan.replicas
    block = block_of(columns, wanted)
    strip = pl.BlockSpec((width, block), lambda i: (0, i))
    part_spec = pl.BlockSpec((plan.rows, block), lambda i: (0, i))
    sets = 2 if plan.hops else 1
    pieces = jax.ShapeDtypeStruct((plan.devices // sets, CAP, narrow), BF16)
    hidden = jax.ShapeDtypeStruct((plan.rows, columns), BF16)
    outs = pl.pallas_call(
        functools.partial(rows_kernel, plan),
        grid=(columns // block,),
        out_shape=[hidden] * 3 + [pieces] * sets,
        in_specs=[SMEM] + [part_spec] * 6 + [strip] * 2,
        out_specs=[part_spec] * 3 + [pl.BlockSpec(pieces.shape, lambda i: (0, 0, 0))] * sets,
        scratch_shapes=[pltpu.VMEM((plan.rows, width), F32)],
        compiler_params=params(48),
        cost_estimate=cost(4 * plan.rows * width * columns, 4 * width * columns),
        name="row_grads",
    )(where, *parts, wg, wu)
    return outs[:3], outs[3:]


def weights_kernel(factor, block, many, *refs):
    pairs = [(refs[2 * k], refs[2 * k + 1]) for k in range(many)]
    outs, done_ref, held, sems = refs[2 * many + 1 : 3 * many + 1], refs[-3], refs[-2], refs[-1]
    copies = []
    for i in range(held.shape[1]):
        cols = pl.ds(i * block, block)
        for k, (rows_ref, d_ref) in enumerate(pairs):
            grad = lax.dot_general(rows_ref[...], d_ref[:, cols], BOTH_FIRST, preferred_element_type=F32)
            held[k, i] = (grad * factor).astype(BF16)
            copy = pltpu.make_async_copy(held.at[k, i], outs[k].at[:, cols], sems.at[k, i])
            copy.start()
            copies.append(copy)
    done_ref[...] = jnp.zeros(done_ref.shape, F32)
    for copy in copies:
        copy.wait()


def weight_grads(factor, pairs, after, name, wanted=512):
    (rows, width), columns = pairs[0][0].shape, pairs[0][1].shape[1]
    block = block_of(columns, wanted)
    count, many = columns // block, len(pairs)
    return pl.pallas_call(
        functools.partial(weights_kernel, factor, block, many),
        out_shape=[jax.ShapeDtypeStruct((width, columns), BF16)] * many + [jax.ShapeDtypeStruct((8, 128), F32)],
        in_specs=[VMEM] * (2 * many) + [ANY],
        out_specs=[ANY] * many + [VMEM],
        scratch_shapes=[pltpu.VMEM((many, count, width, block), BF16), pltpu.SemaphoreType.DMA((many, count))],
        compiler_params=params(16 + 14 * many),
        cost_estimate=cost(2 * many * rows * width * columns, 2 * many * width * columns),
        name=name,
    )(*[array for pair in pairs for array in pair], after)


def pair_kernel(kept_ref, got_ref, after_ref, *outs):
    for at, out_ref in enumerate(outs):
        out_ref[0] = (kept_ref[at].astype(F32) + got_ref[at].astype(F32)).astype(BF16)


def pair_sum(kept, got, after):
    pieces, cap, narrow = kept.shape
    return pl.pallas_call(
        pair_kernel,
        out_shape=[jax.ShapeDtypeStruct((1, cap, narrow), BF16)] * pieces,
        in_specs=[VMEM, VMEM, ANY],
        out_specs=[VMEM] * pieces,
        compiler_params=params(8),
        name="pair_sum",
    )(kept, got, after)


def combine_kernel(plan, sel_ref, *refs):
    backs, out_ref = refs[:-1], refs[-1]
    total = jnp.zeros(out_ref.shape, F32)
    if plan.hops:
        for at in range(len(PARTNERS)):
            total = total + lax.dot_general(sel_ref[at], backs[at][0], BOTH_FIRST, preferred_element_type=F32)
    else:
        for z in range(plan.replicas):
            for x in range(plan.owners):
                chosen, piece = sel_ref[plan.expert_of(x, z)], backs[0][z * plan.owners + x]
                total = total + lax.dot_general(chosen, piece, BOTH_FIRST, preferred_element_type=F32)
    out_ref[...] = total.astype(BF16)


def combine(plan, sel, backs):
    count, narrow = sel.shape[2], backs[0].shape[2]
    return pl.pallas_call(
        functools.partial(combine_kernel, plan),
        out_shape=jax.ShapeDtypeStruct((count, narrow), BF16),
        in_specs=[VMEM] * (1 + len(backs)),
        out_specs=VMEM,
        compiler_params=params(8),
        name="combine",
    )(sel, *backs)


def body(mesh, tokens, cotangent, expert_ids, gate_values, gate_weight, up_weight, down_weight):
    plan = Plan(mesh, gate_weight.shape[1])
    where = jnp.stack((lax.axis_index("expert"), lax.axis_index("dp"))).astype(jnp.int32)
    wg, wu, wd = gate_weight, up_weight, down_weight

    def swap(part):
        size = mesh.shape["tensor"]
        return lax.ppermute(part, "tensor", [(i, i ^ 1) for i in range(size)])

    sel, sends = dispatch(plan, where, expert_ids, gate_values, tokens, cotangent, 6 * wg.size)
    if plan.hops:
        own, to_x, to_z, to_xz = sends
        far_x = plan.send(to_xz, 1, 0)
        far_own, near_own = plan.send(to_z, 0, 2), plan.send(own, 0, 1)
        from_x = plan.send(to_x, 1, 0)
        far_x, last_own = plan.send(far_x, 0, 2), plan.send(far_own, 0, 1)
        near_x = plan.send(from_x, 0, 1)
        last_x = plan.send(far_x, 0, 1)
        got = [own, from_x, near_own, near_x, far_own, far_x, last_own, last_x]
    else:
        got = [plan.scatter(sends[0])]
    q_full, part_h = forward(plan, where, got, 1, wd, "forward_h")
    other_h = swap(part_h)
    x_full, part_g = forward(plan, where, got, 0, wg, "forward_g")
    other_g = swap(part_g)
    (part_u,) = forward(plan, where, [x_full], None, wu, "forward_u")
    other_u = swap(part_u)
    parts = (part_g, other_g, part_u, other_u, part_h, other_h)
    factor = 1.0 / math.sqrt(tokens.shape[0] * plan.owners)
    (h, d_gate, d_up), pieces = row_grads(plan, where, parts, wg, wu)
    arrived = plan.send(pieces[1], 0, 1) if plan.hops else plan.scatter(pieces[0])
    grad_gate, grad_up, done = weight_grads(factor, ((x_full, d_gate), (x_full, d_up)), pieces[0], "grads_gu")
    if plan.hops:
        backs = pair_sum(pieces[0], arrived, done)
        backs = [plan.send(piece, *hop) if at else piece for at, (piece, hop) in enumerate(zip(backs, PARTNERS))]
        done = backs[0]
    else:
        backs = [arrived]
    grad_down, _ = weight_grads(factor, ((q_full, h),), done, "grad_down")
    token_grad = combine(plan, sel, backs)
    return (token_grad, grad_gate, grad_up, grad_down)


def solution(mesh):
    in_specs = (
        P(("groups", "expert"), ("tensor", "dp")),
        P(("groups", "expert"), ("tensor", "dp")),
        P(("groups", "expert"), None),
        P(("groups", "expert"), None),
        P("tensor", ("expert", "dp")),
        P("tensor", ("expert", "dp")),
        P("tensor", ("expert", "dp")),
    )
    out_specs = (
        P(("groups", "expert"), ("tensor", "dp")),
        P(("groups", "tensor"), ("expert", "dp")),
        P(("groups", "tensor"), ("expert", "dp")),
        P(("groups", "tensor"), ("expert", "dp")),
    )
    return jax.shard_map(
        functools.partial(body, mesh), mesh=mesh, in_specs=in_specs, out_specs=out_specs, check_vma=False
    )
```

time: 101 us -> 83.5 us (0.83)
  starting transfers between devices: 37 us -> 18.2 us
  Pallas kernels: 53.1 us -> 39.4 us
  waiting for transfers between devices: 5.22 us -> 16.1 us
  local copies, waits for them, and re-layouts: 4.19 us -> 8.67 us
    ppermute x21 -> x12, starting transfers between devices: 36.3 us -> 17.5 us  [send(): return lax.ppermute(array, ('dp', 'expert'), pairs)]
    pallas_call x4 -> x7, Pallas kernels: 36.2 us -> 23.9 us  [the longest x2 15 us: weight_grads(): pl.pallas_call(functools.partial(weights_kernel, factor, block, many), ou...]
    ppermute x21 -> x12, waiting for transfers between devices: 0.82 us -> 13.1 us  [send(): return lax.ppermute(array, ('dp', 'expert'), pairs)]
    unnamed x18 -> x28, local copies, waits for them, and re-layouts: 4.19 us -> 8.67 us
    ppermute x3, waiting for transfers between devices: 4.39 us -> 2.98 us  [swap(): return lax.ppermute(part, 'tensor', [(i, i ^ 1) for i in range(size)])]
    pallas_call x1, Pallas kernels: 15.9 us -> 14.6 us  [row_grads(): pl.pallas_call(functools.partial(rows_kernel, plan), grid=(columns // blo...]
  transfers between devices with their start and end apart: 24 -> 15, of which waited for: 4 -> 9; matrix products, arithmetic and copies ran while one was open for 0% -> 0% of each run, Pallas kernels for 35% -> 21%
where the time goes in v2:
time: 83.5 us; the launch traced here: 83.3 us
  Pallas kernels  39.4 us (47%)
  starting transfers between devices  18.2 us (22%)
  waiting for transfers between devices  16.1 us (19%)
  local copies, waits for them, and re-layouts  8.67 us (10%)
  between operations  0.85 us (1%)
    ppermute x12, starting transfers between devices, send(): return lax.ppermute(array, ('dp', 'expert'), pairs)  17.5 us
    pallas_call x2, Pallas kernels, weight_grads(): pl.pallas_call(functools.partial(weights_kernel, factor, block, many), ou...  15 us
    pallas_call x1, Pallas kernels, row_grads(): pl.pallas_call(functools.partial(rows_kernel, plan), grid=(columns // blo...  14.6 us
    ppermute x12, waiting for transfers between devices, send(): return lax.ppermute(array, ('dp', 'expert'), pairs)  13.1 us
    unnamed x28, local copies, waits for them, and re-layouts  8.67 us
    pallas_call x3, Pallas kernels, forward(): pl.pallas_call(functools.partial(forward_kernel, plan, half, block), out_...  7.86 us
    ppermute x3, waiting for transfers between devices, swap(): return lax.ppermute(part, 'tensor', [(i, i ^ 1) for i in range(size)])  2.98 us
  transfers between devices with their start and end apart: 15, of which 9 were waited for; matrix products, arithmetic and copies ran while one was open for 0% of the time, Pallas kernels for 21%

profile of v2, /device:TPU:0, one launch (start us, length us, event | category | flops | bytes accessed | tf_op | source)
XLA Modules:
  0.0 83.3 jit_solution(480293075154966716)
XLA Ops:
  0.6 0.1 pad_add_fusion.where_ref.refs_0_
  0.7 0.0 slice-start
  0.7 0.0 copy-start.4
  0.7 1.0 %copy-done.4 = bf16[128,384]{1,0:T(8,128)(2,1)S(1)} copy-done((bf16[128,384]{1,0:T(8,128)(2,1)S(1)}, bf16[128,384]{1,0:T(8,128)(2,1)}, u32[]{:S(2)}) %copy-start.4) | copy-done | bytes 98328
  1.8 0.0 copy-start.5
  1.8 1.2 %copy-done.5 = bf16[128,384]{1,0:T(8,128)(2,1)S(1)} copy-done((bf16[128,384]{1,0:T(8,128)(2,1)S(1)}, bf16[128,384]{1,0:T(8,128)(2,1)}, u32[]{:S(2)}) %copy-start.5) | copy-done | bytes 98328
  2.9 0.0 copy-start.6
  2.9 0.7 copy-done.6
  3.6 0.7 copy-done.7
  4.3 1.0 %dispatch.1 = (bf16[4,80,128]{2,1,0:T(8,128)(2,1)S(1)}, bf16[1,160,384]{2,1,0:T(8,128)(2,1)S(1)}, bf16[1,160,384]{2,1,0:T(8,128)(2,1)S(1)}, bf16[1,160,384]{2,1,0:T(8,128)(2,1)S(1)}, bf16[1,160,384]{2,1,0:T(8,128)(2,1)S(1)}) custom-call(s32[2]{0:T(128)S(1)} %pad_add_fusion.where_ref.refs_0_, s32[2,128]{1,0:T(2,128)S(1)} %bitcast.6, ...), custom_call_target="tpu_custom_call" | custom-call | flops 15099494400 | bytes 37748736 | tf_op jit(solution)/shard_map/dispatch/pallas_call | solution.py:103
  5.3 3.0 %collective-permute-start.4 = (bf16[1,160,384]{2,1,0:T(8,128)(2,1)S(1)}, bf16[1,160,384]{2,1,0:T(8,128)(2,1)S(1)}, u32[]{:S(2)}, u32[]{:S(2)}) collective-permute-start(bf16[1,160,384]{2,1,0:T(8,128)(2,1)S(1)} %get-tuple-element.30), channel_id=1, source_target_pairs={{0,2},{4,6},{8,10},{12,14},{2,0},{6,4},{10,8},{14,12},{1,3},{5,7},... | collective-permute-start | bytes 368648 | tf_op jit(solution)/shard_map/ppermute | solution.py:56
  8.3 0.1 collective-permute-start
  8.3 3.0 %collective-permute-start.3 = (bf16[1,160,384]{2,1,0:T(8,128)(2,1)S(1)}, bf16[1,160,384]{2,1,0:T(8,128)(2,1)S(1)}, u32[]{:S(2)}, u32[]{:S(2)}) collective-permute-start(bf16[1,160,384]{2,1,0:T(8,128)(2,1)S(1)} %get-tuple-element.29), channel_id=1, source_target_pairs={{0,8},{4,12},{8,0},{12,4},{2,10},{6,14},{10,2},{14,6},{1,9},{5,13}... | collective-permute-start | bytes 368648 | tf_op jit(solution)/shard_map/ppermute | solution.py:56
  11.4 1.0 %collective-permute-done.4 = bf16[1,160,384]{2,1,0:T(8,128)(2,1)S(1)} collective-permute-done((bf16[1,160,384]{2,1,0:T(8,128)(2,1)S(1)}, bf16[1,160,384]{2,1,0:T(8,128)(2,1)S(1)}, u32[]{:S(2)}, u32[]{:S(2)}) %collective-permute-start.4) | collective-permute-done | bytes 122912 | tf_op jit(solution)/shard_map/ppermute | solution.py:56
  12.4 3.2 %collective-permute-start.5 = (bf16[1,160,384]{2,1,0:T(8,128)(2,1)S(1)}, bf16[1,160,384]{2,1,0:T(8,128)(2,1)S(1)}, u32[]{:S(2)}, u32[]{:S(2)}) collective-permute-start(bf16[1,160,384]{2,1,0:T(8,128)(2,1)S(1)} %collective-permute-done.4), channel_id=1, source_target_pairs={{0,8},{4,12},{8,0},{12,4},{2,10},{6,14},{10,2},{14,6},{1,9},{5,13}... | collective-permute-start | bytes 368648 | tf_op jit(solution)/shard_map/ppermute | solution.py:56
  15.6 1.6 %collective-permute-start.1 = (bf16[1,160,384]{2,1,0:T(8,128)(2,1)S(1)}, bf16[1,160,384]{2,1,0:T(8,128)(2,1)S(1)}, u32[]{:S(2)}, u32[]{:S(2)}) collective-permute-start(bf16[1,160,384]{2,1,0:T(8,128)(2,1)S(1)} %get-tuple-element.27.refs_1_), channel_id=1, source_target_pairs={{0,4},{4,0},{8,12},{12,8},{2,6},{6,2},{10,14},{14,10},{1,5},{5,1},... | collective-permute-start | bytes 368648 | tf_op jit(solution)/shard_map/ppermute | solution.py:56
  17.1 0.0 collective-permute-done.refs_2_
  17.1 0.4 collective-permute-start.2
  17.6 2.5 %collective-permute-done.3.refs_5_ = bf16[1,160,384]{2,1,0:T(8,128)(2,1)S(1)} collective-permute-done((bf16[1,160,384]{2,1,0:T(8,128)(2,1)S(1)}, bf16[1,160,384]{2,1,0:T(8,128)(2,1)S(1)}, u32[]{:S(2)}, u32[]{:S(2)}) %collective-permute-start.3) | collective-permute-done | bytes 122912 | tf_op jit(solution)/shard_map/ppermute | solution.py:56
  20.1 0.0 collective-permute-start.6
  20.1 2.0 %collective-permute-done.5.refs_6_ = bf16[1,160,384]{2,1,0:T(8,128)(2,1)S(1)} collective-permute-done((bf16[1,160,384]{2,1,0:T(8,128)(2,1)S(1)}, bf16[1,160,384]{2,1,0:T(8,128)(2,1)S(1)}, u32[]{:S(2)}, u32[]{:S(2)}) %collective-permute-start.5) | collective-permute-done | bytes 122912 | tf_op jit(solution)/shard_map/ppermute | solution.py:56
  22.1 0.6 collective-permute-start.7
  22.8 1.0 %collective-permute-done.1.refs_3_ = bf16[1,160,384]{2,1,0:T(8,128)(2,1)S(1)} collective-permute-done((bf16[1,160,384]{2,1,0:T(8,128)(2,1)S(1)}, bf16[1,160,384]{2,1,0:T(8,128)(2,1)S(1)}, u32[]{:S(2)}, u32[]{:S(2)}) %collective-permute-start.1) | collective-permute-done | bytes 122912 | tf_op jit(solution)/shard_map/ppermute | solution.py:56
  23.8 2.6 %collective-permute-done.2.refs_4_ = bf16[1,160,384]{2,1,0:T(8,128)(2,1)S(1)} collective-permute-done((bf16[1,160,384]{2,1,0:T(8,128)(2,1)S(1)}, bf16[1,160,384]{2,1,0:T(8,128)(2,1)S(1)}, u32[]{:S(2)}, u32[]{:S(2)}) %collective-permute-start.2) | collective-permute-done | bytes 122912 | tf_op jit(solution)/shard_map/ppermute | solution.py:56
  26.4 2.3 %collective-permute-done.6.refs_7_ = bf16[1,160,384]{2,1,0:T(8,128)(2,1)S(1)} collective-permute-done((bf16[1,160,384]{2,1,0:T(8,128)(2,1)S(1)}, bf16[1,160,384]{2,1,0:T(8,128)(2,1)S(1)}, u32[]{:S(2)}, u32[]{:S(2)}) %collective-permute-start.6) | collective-permute-done | bytes 122912 | tf_op jit(solution)/shard_map/ppermute | solution.py:56
  28.7 1.3 %collective-permute-done.7.refs_8_ = bf16[1,160,384]{2,1,0:T(8,128)(2,1)S(1)} collective-permute-done((bf16[1,160,384]{2,1,0:T(8,128)(2,1)S(1)}, bf16[1,160,384]{2,1,0:T(8,128)(2,1)S(1)}, u32[]{:S(2)}, u32[]{:S(2)}) %collective-permute-start.7) | collective-permute-done | bytes 122912 | tf_op jit(solution)/shard_map/ppermute | solution.py:56
  30.0 0.0 slice-done
  30.1 0.0 slice-done.1
  30.1 0.0 slice-done.2
  30.1 0.0 copy-start
  30.1 2.8 %forward_g.1 = (bf16[160,1536]{1,0:T(8,128)(2,1)S(1)}, bf16[160,4096]{1,0:T(8,128)(2,1)S(1)}) custom-call(s32[2]{0:T(128)S(1)} %pad_add_fusion.where_ref.refs_0_, bf16[1,160,384]{2,1,0:T(8,128)(2,1)S(1)} %get-tuple-element.27.refs_1_, bf16[1,160,384]{2,1,0:T(8,128)(2,1)S(1)} %collective-permute-done.refs_2_, ...), custom_call_target="tpu_custom_call" | custom-call | flops 2013265920 | bytes 8388608 | tf_op jit(solution)/shard_map/forward_g/pallas_call | solution.py:143
  32.9 1.8 %copy-done = bf16[1536,4096]{1,0:T(8,128)(2,1)S(1)} copy-done((bf16[1536,4096]{1,0:T(8,128)(2,1)S(1)}, bf16[1536,4096]{1,0:T(8,128)(2,1)}, u32[]{:S(2)}) %copy-start) | copy-done | bytes 12582936
  34.6 2.2 %forward_u.1.u0 = bf16[160,4096]{1,0:T(8,128)(2,1)S(1)} custom-call(bf16[160,1536]{1,0:T(8,128)(2,1)S(1)} %get-tuple-element.32.refs_0_.refs_2_, bf16[1536,4096]{1,0:T(8,128)(2,1)S(1)} %copy-done), custom_call_target="tpu_custom_call" | custom-call | flops 2013265920 | bytes 8388608 | tf_op jit(solution)/shard_map/forward_u/pallas_call | solution.py:143
  36.9 0.0 copy-start.2
  36.9 0.1 collective-permute-start.9
  37.0 0.5 collective-permute-start.8
  37.4 2.2 %copy-done.1 = bf16[1536,4096]{1,0:T(8,128)(2,1)S(1)} copy-done((bf16[1536,4096]{1,0:T(8,128)(2,1)S(1)}, bf16[1536,4096]{1,0:T(8,128)(2,1)}, u32[]{:S(2)}) %copy-start.1) | copy-done | bytes 12582936
  39.7 2.9 %forward_h.1 = (bf16[160,1536]{1,0:T(8,128)(2,1)S(1)}, bf16[160,4096]{1,0:T(8,128)(2,1)S(1)}) custom-call(s32[2]{0:T(128)S(1)} %pad_add_fusion.where_ref.refs_0_, bf16[1,160,384]{2,1,0:T(8,128)(2,1)S(1)} %get-tuple-element.27.refs_1_, bf16[1,160,384]{2,1,0:T(8,128)(2,1)S(1)} %collective-permute-done.refs_2_, ...), custom_call_target="tpu_custom_call" | custom-call | flops 2013265920 | bytes 8388608 | tf_op jit(solution)/shard_map/forward_h/pallas_call | solution.py:143
  42.6 0.0 copy-done.2
  42.6 0.0 copy-start.3
  42.6 0.1 collective-permute-start.10
  42.7 0.0 collective-permute-done.9.u1
  42.7 0.0 copy-start.8
  42.7 0.0 collective-permute-done.8.g1
  42.7 0.0 copy-start.9
  42.7 3.0 %collective-permute-done.10.d1 = bf16[160,4096]{1,0:T(8,128)(2,1)S(1)} collective-permute-done((bf16[160,4096]{1,0:T(8,128)(2,1)S(1)}, bf16[160,4096]{1,0:T(8,128)(2,1)S(1)}, u32[]{:S(2)}, u32[]{:S(2)}) %collective-permute-start.10) | collective-permute-done | bytes 1310752 | tf_op jit(solution)/shard_map/ppermute | solution.py:298
  45.7 0.0 copy-done.3
  45.7 0.0 copy-done.8
  45.7 0.0 copy-done.9
  45.7 0.0 copy-start.10
  45.7 1.1 %copy-done.10 = bf16[160,4096]{1,0:T(8,128)(2,1)} copy-done((bf16[160,4096]{1,0:T(8,128)(2,1)}, bf16[160,4096]{1,0:T(8,128)(2,1)S(1)}, u32[]{:S(2)}) %copy-start.10) | copy-done | bytes 1310744
  46.8 14.6 %row_grads.1 = (bf16[160,4096]{1,0:T(8,128)(2,1)S(1)}, bf16[160,4096]{1,0:T(8,128)(2,1)S(1)}, bf16[160,4096]{1,0:T(8,128)(2,1)S(1)}, bf16[4,80,384]{2,1,0:T(8,128)(2,1)S(1)}, bf16[4,80,384]{2,1,0:T(8,128)(2,1)S(1)}) custom-call(s32[2]{0:T(128)S(1)} %pad_add_fusion.where_ref.refs_0_, bf16[160,4096]{1,0:T(8,128)(2,1)S(1)} %get-tuple-element.31.g0, ...), custom_call_target="tpu_custom_call" | custom-call | flops 4026531840 | bytes 25165824 | tf_op jit(solution)/shard_map/row_grads/pallas_call | solution.py:201
  61.4 0.1 collective-permute-start.11
  61.5 9.1 %grads_gu.1 = (bf16[1536,4096]{1,0:T(8,128)(2,1)}, bf16[1536,4096]{1,0:T(8,128)(2,1)}, f32[8,128]{1,0:T(8,128)S(1)}) custom-call(bf16[160,1536]{1,0:T(8,128)(2,1)S(1)} %get-tuple-element.32.refs_0_.refs_2_, bf16[160,4096]{1,0:T(8,128)(2,1)S(1)} %get-tuple-element.36.refs_1_, bf16[160,1536]{1,0:T(8,128)(2,1)S(1)} %get-tuple-element.32.refs_0_.refs_2_, ...), custom_call_target="tpu_custom_call" | custom-call | flops 4026531840 | bytes 25165824 | tf_op jit(solution)/shard_map/grads_gu/pallas_call | solution.py:236
  70.6 0.0 collective-permute-done.11.got_ref
  70.6 0.1 pair_sum.1
  70.7 1.6 %collective-permute-start.12 = (bf16[1,80,384]{2,1,0:T(8,128)(2,1)S(1)}, bf16[1,80,384]{2,1,0:T(8,128)(2,1)S(1)}, u32[]{:S(2)}, u32[]{:S(2)}) collective-permute-start(bf16[1,80,384]{2,1,0:T(8,128)(2,1)S(1)} %get-tuple-element.40), channel_id=1, source_target_pairs={{0,2},{4,6},{8,10},{12,14},{2,0},{6,4},{10,8},{14,12},{1,3},{5,7},... | collective-permute-start | bytes 184328 | tf_op jit(solution)/shard_map/ppermute | solution.py:56
  72.3 3.9 %collective-permute-start.13 = (bf16[1,80,384]{2,1,0:T(8,128)(2,1)S(1)}, bf16[1,80,384]{2,1,0:T(8,128)(2,1)S(1)}, u32[]{:S(2)}, u32[]{:S(2)}) collective-permute-start(bf16[1,80,384]{2,1,0:T(8,128)(2,1)S(1)} %get-tuple-element.41), channel_id=1, source_target_pairs={{0,8},{4,12},{8,0},{12,4},{2,10},{6,14},{10,2},{14,6},{1,9},{5,13}... | collective-permute-start | bytes 184328 | tf_op jit(solution)/shard_map/ppermute | solution.py:56
  76.2 0.0 collective-permute-start.14
  76.2 5.9 %grad_down.1 = (bf16[1536,4096]{1,0:T(8,128)(2,1)}, f32[8,128]{1,0:T(8,128)}) custom-call(bf16[160,1536]{1,0:T(8,128)(2,1)S(1)} %get-tuple-element.45.refs_0_, bf16[160,4096]{1,0:T(8,128)(2,1)S(1)} %get-tuple-element.46.refs_1_, bf16[1,80,384]{2,1,0:T(8,128)(2,1)S(1)} %get-tuple-element.39.refs_0_.refs_2_), custom_call_target="tpu_custom_call" | custom-call | flops 2013265920 | bytes 12582912 | tf_op jit(solution)/shard_map/grad_down/pallas_call | solution.py:236
  82.1 0.0 collective-permute-done.12.refs_1_
  82.1 0.0 collective-permute-done.13.refs_2_
  82.1 0.2 collective-permute-done.14.refs_3_
  82.3 0.9 %combine.1 = bf16[128,384]{1,0:T(8,128)(2,1)} custom-call(bf16[4,80,128]{2,1,0:T(8,128)(2,1)S(1)} %get-tuple-element.26.sel_ref, bf16[1,80,384]{2,1,0:T(8,128)(2,1)S(1)} %get-tuple-element.39.refs_0_.refs_2_, bf16[1,80,384]{2,1,0:T(8,128)(2,1)S(1)} %collective-permute-done.12.refs_1_, bf16[1,80,384]{2,1,0:T(8,128)(2,1)S(1)} %collective-permute-done.13.refs_2_, ...), custom_call_target="tpu_custom_call" | custom-call | tf_op jit(solution)/shard_map/combine/pallas_call | solution.py:281
  (5 shorter events, 0.0 us)
Async XLA Ops:
  0.7 29.3 %slice-start = ((s8[12582912]{0:T(1024)(128)(4,1)}), s8[4194304]{0:T(1024)(128)(4,1)S(1)}, s32[]{:S(2)}) async-start(s8[12582912]{0:T(1024)(128)(4,1)} %bitcast.4), calls=%async_computation | async-start | bytes 8388608
  0.7 1.0 %copy-start.4 = (bf16[128,384]{1,0:T(8,128)(2,1)S(1)}, bf16[128,384]{1,0:T(8,128)(2,1)}, u32[]{:S(2)}) copy-start(bf16[128,384]{1,0:T(8,128)(2,1)} %tok_ref.1) | copy-start | bytes 294916
  1.8 1.2 %copy-start.5 = (bf16[128,384]{1,0:T(8,128)(2,1)S(1)}, bf16[128,384]{1,0:T(8,128)(2,1)}, u32[]{:S(2)}) copy-start(bf16[128,384]{1,0:T(8,128)(2,1)} %cot_ref.1) | copy-start | bytes 294916
  2.9 0.7 copy-start.6
  3.6 0.7 copy-start.7
  4.2 25.8 %slice-start.1 = ((s8[12582912]{0:T(1024)(128)(4,1)}), s8[4194304]{0:T(1024)(128)(4,1)S(1)}, s32[]{:S(2)}) async-start(s8[12582912]{0:T(1024)(128)(4,1)} %bitcast.4), calls=%async_computation.1 | async-start | bytes 8388608
  4.2 25.8 %slice-start.2 = ((s8[12582912]{0:T(1024)(128)(4,1)}), s8[4194304]{0:T(1024)(128)(4,1)S(1)}, s32[]{:S(2)}) async-start(s8[12582912]{0:T(1024)(128)(4,1)} %bitcast.4), calls=%async_computation.2 | async-start | bytes 8388608
  5.3 7.2 %collective-permute-start.4 = (bf16[1,160,384]{2,1,0:T(8,128)(2,1)S(1)}, bf16[1,160,384]{2,1,0:T(8,128)(2,1)S(1)}, u32[]{:S(2)}, u32[]{:S(2)}) collective-permute-start(bf16[1,160,384]{2,1,0:T(8,128)(2,1)S(1)} %get-tuple-element.30), channel_id=1, source_target_pairs={{0,2},{4,6},{8,10},{12,14},{2,0},{6,4},{10,8},{14,12},{1,3},{5,7},... | collective-permute-start | bytes 368648 | tf_op jit(solution)/shard_map/ppermute | solution.py:56
  8.3 8.9 %collective-permute-start = (bf16[1,160,384]{2,1,0:T(8,128)(2,1)S(1)}, bf16[1,160,384]{2,1,0:T(8,128)(2,1)S(1)}, u32[]{:S(2)}, u32[]{:S(2)}) collective-permute-start(bf16[1,160,384]{2,1,0:T(8,128)(2,1)S(1)} %get-tuple-element.28), channel_id=1, source_target_pairs={{0,2},{4,6},{8,10},{12,14},{2,0},{6,4},{10,8},{14,12},{1,3},{5,7},... | collective-permute-start | bytes 368648 | tf_op jit(solution)/shard_map/ppermute | solution.py:56
  8.3 11.8 %collective-permute-start.3 = (bf16[1,160,384]{2,1,0:T(8,128)(2,1)S(1)}, bf16[1,160,384]{2,1,0:T(8,128)(2,1)S(1)}, u32[]{:S(2)}, u32[]{:S(2)}) collective-permute-start(bf16[1,160,384]{2,1,0:T(8,128)(2,1)S(1)} %get-tuple-element.29), channel_id=1, source_target_pairs={{0,8},{4,12},{8,0},{12,4},{2,10},{6,14},{10,2},{14,6},{1,9},{5,13}... | collective-permute-start | bytes 368648 | tf_op jit(solution)/shard_map/ppermute | solution.py:56
  12.4 9.7 %collective-permute-start.5 = (bf16[1,160,384]{2,1,0:T(8,128)(2,1)S(1)}, bf16[1,160,384]{2,1,0:T(8,128)(2,1)S(1)}, u32[]{:S(2)}, u32[]{:S(2)}) collective-permute-start(bf16[1,160,384]{2,1,0:T(8,128)(2,1)S(1)} %collective-permute-done.4), channel_id=1, source_target_pairs={{0,8},{4,12},{8,0},{12,4},{2,10},{6,14},{10,2},{14,6},{1,9},{5,13}... | collective-permute-start | bytes 368648 | tf_op jit(solution)/shard_map/ppermute | solution.py:56
  15.6 8.2 %collective-permute-start.1 = (bf16[1,160,384]{2,1,0:T(8,128)(2,1)S(1)}, bf16[1,160,384]{2,1,0:T(8,128)(2,1)S(1)}, u32[]{:S(2)}, u32[]{:S(2)}) collective-permute-start(bf16[1,160,384]{2,1,0:T(8,128)(2,1)S(1)} %get-tuple-element.27.refs_1_), channel_id=1, source_target_pairs={{0,4},{4,0},{8,12},{12,8},{2,6},{6,2},{10,14},{14,10},{1,5},{5,1},... | collective-permute-start | bytes 368648 | tf_op jit(solution)/shard_map/ppermute | solution.py:56
  17.1 9.3 %collective-permute-start.2 = (bf16[1,160,384]{2,1,0:T(8,128)(2,1)S(1)}, bf16[1,160,384]{2,1,0:T(8,128)(2,1)S(1)}, u32[]{:S(2)}, u32[]{:S(2)}) collective-permute-start(bf16[1,160,384]{2,1,0:T(8,128)(2,1)S(1)} %collective-permute-done.refs_2_), channel_id=1, source_target_pairs={{0,4},{4,0},{8,12},{12,8},{2,6},{6,2},{10,14},{14,10},{1,5},{5,1},... | collective-permute-start | bytes 368648 | tf_op jit(solution)/shard_map/ppermute | solution.py:56
  20.1 8.6 %collective-permute-start.6 = (bf16[1,160,384]{2,1,0:T(8,128)(2,1)S(1)}, bf16[1,160,384]{2,1,0:T(8,128)(2,1)S(1)}, u32[]{:S(2)}, u32[]{:S(2)}) collective-permute-start(bf16[1,160,384]{2,1,0:T(8,128)(2,1)S(1)} %collective-permute-done.3.refs_5_), channel_id=1, source_target_pairs={{0,4},{4,0},{8,12},{12,8},{2,6},{6,2},{10,14},{14,10},{1,5},{5,1},... | collective-permute-start | bytes 368648 | tf_op jit(solution)/shard_map/ppermute | solution.py:56
  22.1 7.9 %collective-permute-start.7 = (bf16[1,160,384]{2,1,0:T(8,128)(2,1)S(1)}, bf16[1,160,384]{2,1,0:T(8,128)(2,1)S(1)}, u32[]{:S(2)}, u32[]{:S(2)}) collective-permute-start(bf16[1,160,384]{2,1,0:T(8,128)(2,1)S(1)} %collective-permute-done.5.refs_6_), channel_id=1, source_target_pairs={{0,4},{4,0},{8,12},{12,8},{2,6},{6,2},{10,14},{14,10},{1,5},{5,1},... | collective-permute-start | bytes 368648 | tf_op jit(solution)/shard_map/ppermute | solution.py:56
  30.1 4.6 %copy-start = (bf16[1536,4096]{1,0:T(8,128)(2,1)S(1)}, bf16[1536,4096]{1,0:T(8,128)(2,1)}, u32[]{:S(2)}) copy-start(bf16[1536,4096]{1,0:T(8,128)(2,1)} %wu_ref.1) | copy-start | bytes 37748740
  34.6 5.0 %copy-start.1 = (bf16[1536,4096]{1,0:T(8,128)(2,1)S(1)}, bf16[1536,4096]{1,0:T(8,128)(2,1)}, u32[]{:S(2)}) copy-start(bf16[1536,4096]{1,0:T(8,128)(2,1)} %refs_9_.3) | copy-start | bytes 37748740
  36.9 5.7 %copy-start.2 = (bf16[160,4096]{1,0:T(8,128)(2,1)}, bf16[160,4096]{1,0:T(8,128)(2,1)S(1)}, u32[]{:S(2)}) copy-start(bf16[160,4096]{1,0:T(8,128)(2,1)S(1)} %forward_u.1.u0) | copy-start | bytes 3932164
  36.9 5.8 %collective-permute-start.9 = (bf16[160,4096]{1,0:T(8,128)(2,1)S(1)}, bf16[160,4096]{1,0:T(8,128)(2,1)S(1)}, u32[]{:S(2)}, u32[]{:S(2)}) collective-permute-start(bf16[160,4096]{1,0:T(8,128)(2,1)S(1)} %forward_u.1.u0), channel_id=1, source_target_pairs={{0,1},{1,0},{2,3},{3,2},{4,5},{5,4},{6,7},{7,6},{8,9},{9,8},{10,11... | collective-permute-start | bytes 3932168 | tf_op jit(solution)/shard_map/ppermute | solution.py:298
  37.0 5.8 %collective-permute-start.8 = (bf16[160,4096]{1,0:T(8,128)(2,1)S(1)}, bf16[160,4096]{1,0:T(8,128)(2,1)S(1)}, u32[]{:S(2)}, u32[]{:S(2)}) collective-permute-start(bf16[160,4096]{1,0:T(8,128)(2,1)S(1)} %get-tuple-element.31.g0), channel_id=1, source_target_pairs={{0,1},{1,0},{2,3},{3,2},{4,5},{5,4},{6,7},{7,6},{8,9},{9,8},{10,11... | collective-permute-start | bytes 3932168 | tf_op jit(solution)/shard_map/ppermute | solution.py:298
  42.6 3.1 %copy-start.3 = (bf16[160,4096]{1,0:T(8,128)(2,1)}, bf16[160,4096]{1,0:T(8,128)(2,1)S(1)}, u32[]{:S(2)}) copy-start(bf16[160,4096]{1,0:T(8,128)(2,1)S(1)} %get-tuple-element.33.d0) | copy-start | bytes 3932164
  42.6 3.1 %collective-permute-start.10 = (bf16[160,4096]{1,0:T(8,128)(2,1)S(1)}, bf16[160,4096]{1,0:T(8,128)(2,1)S(1)}, u32[]{:S(2)}, u32[]{:S(2)}) collective-permute-start(bf16[160,4096]{1,0:T(8,128)(2,1)S(1)} %get-tuple-element.33.d0), channel_id=1, source_target_pairs={{0,1},{1,0},{2,3},{3,2},{4,5},{5,4},{6,7},{7,6},{8,9},{9,8},{10,11... | collective-permute-start | bytes 3932168 | tf_op jit(solution)/shard_map/ppermute | solution.py:298
  42.7 3.0 %copy-start.8 = (bf16[160,4096]{1,0:T(8,128)(2,1)}, bf16[160,4096]{1,0:T(8,128)(2,1)S(1)}, u32[]{:S(2)}) copy-start(bf16[160,4096]{1,0:T(8,128)(2,1)S(1)} %collective-permute-done.9.u1) | copy-start | bytes 3932164
  42.7 3.0 %copy-start.9 = (bf16[160,4096]{1,0:T(8,128)(2,1)}, bf16[160,4096]{1,0:T(8,128)(2,1)S(1)}, u32[]{:S(2)}) copy-start(bf16[160,4096]{1,0:T(8,128)(2,1)S(1)} %collective-permute-done.8.g1) | copy-start | bytes 3932164
  45.7 1.1 %copy-start.10 = (bf16[160,4096]{1,0:T(8,128)(2,1)}, bf16[160,4096]{1,0:T(8,128)(2,1)S(1)}, u32[]{:S(2)}) copy-start(bf16[160,4096]{1,0:T(8,128)(2,1)S(1)} %collective-permute-done.10.d1) | copy-start | bytes 3932164
  61.4 9.2 %collective-permute-start.11 = (bf16[4,80,384]{2,1,0:T(8,128)(2,1)S(1)}, bf16[4,80,384]{2,1,0:T(8,128)(2,1)S(1)}, u32[]{:S(2)}, u32[]{:S(2)}) collective-permute-start(bf16[4,80,384]{2,1,0:T(8,128)(2,1)S(1)} %get-tuple-element.35), channel_id=1, source_target_pairs={{0,4},{4,0},{8,12},{12,8},{2,6},{6,2},{10,14},{14,10},{1,5},{5,1},... | collective-permute-start | bytes 737288 | tf_op jit(solution)/shard_map/ppermute | solution.py:56
  70.7 11.4 %collective-permute-start.12 = (bf16[1,80,384]{2,1,0:T(8,128)(2,1)S(1)}, bf16[1,80,384]{2,1,0:T(8,128)(2,1)S(1)}, u32[]{:S(2)}, u32[]{:S(2)}) collective-permute-start(bf16[1,80,384]{2,1,0:T(8,128)(2,1)S(1)} %get-tuple-element.40), channel_id=1, source_target_pairs={{0,2},{4,6},{8,10},{12,14},{2,0},{6,4},{10,8},{14,12},{1,3},{5,7},... | collective-permute-start | bytes 184328 | tf_op jit(solution)/shard_map/ppermute | solution.py:56
  72.3 9.8 %collective-permute-start.13 = (bf16[1,80,384]{2,1,0:T(8,128)(2,1)S(1)}, bf16[1,80,384]{2,1,0:T(8,128)(2,1)S(1)}, u32[]{:S(2)}, u32[]{:S(2)}) collective-permute-start(bf16[1,80,384]{2,1,0:T(8,128)(2,1)S(1)} %get-tuple-element.41), channel_id=1, source_target_pairs={{0,8},{4,12},{8,0},{12,4},{2,10},{6,14},{10,2},{14,6},{1,9},{5,13}... | collective-permute-start | bytes 184328 | tf_op jit(solution)/shard_map/ppermute | solution.py:56
  76.2 6.1 %collective-permute-start.14 = (bf16[1,80,384]{2,1,0:T(8,128)(2,1)S(1)}, bf16[1,80,384]{2,1,0:T(8,128)(2,1)S(1)}, u32[]{:S(2)}, u32[]{:S(2)}) collective-permute-start(bf16[1,80,384]{2,1,0:T(8,128)(2,1)S(1)} %get-tuple-element.42), channel_id=1, source_target_pairs={{0,10},{4,14},{8,2},{12,6},{2,8},{6,12},{10,0},{14,4},{1,11},{5,15... | collective-permute-start | bytes 184328 | tf_op jit(solution)/shard_map/ppermute | solution.py:56

commit v3 on v2

--- a/solution.py
+++ b/solution.py
@@ -17,9 +17,7 @@
 TURNED = (((1,), (1,)), ((), ()))
 BOTH_FIRST = (((0,), (0,)), ((), ()))
 VMEM = pl.BlockSpec(memory_space=pltpu.VMEM)
-SMEM = pl.BlockSpec(memory_space=pltpu.SMEM)
 ANY = pl.BlockSpec(memory_space=pl.ANY)
-HBM = pl.BlockSpec(memory_space=pltpu.HBM)
 
 
 def params(mebibytes):
@@ -59,7 +57,14 @@
         return lax.all_to_all(array, ("dp", "expert"), 0, 0, tiled=True)
 
 
-def dispatch_kernel(plan, where_ref, ids_ref, gates_ref, tok_ref, cot_ref, sel_ref, *send_refs):
+def dispatch_kernel(plan, *refs):
+    sources, sel_ref, send_refs, held, sems = refs[:4], refs[4], refs[5:-5], refs[-5:-1], refs[-1]
+    copies = [pltpu.make_async_copy(source, here, sems.at[k]) for k, (source, here) in enumerate(zip(sources, held))]
+    for copy in copies:
+        copy.start()
+    for copy in copies:
+        copy.wait()
+    ids_ref, gates_ref, tok_ref, cot_ref = held
     count = tok_ref.shape[0]
     first, second = ids_ref[0:1, :], ids_ref[1:2, :]
     gate_first, gate_second = gates_ref[0:1, :].astype(F32), gates_ref[1:2, :].astype(F32)
@@ -82,7 +87,7 @@
 
     if plan.hops:
         for at, (dx, dz) in enumerate(PARTNERS):
-            expert = plan.expert_of(jnp.bitwise_xor(where_ref[0], dx), jnp.bitwise_xor(where_ref[1], dz))
+            expert = plan.expert_of(jnp.bitwise_xor(lax.axis_index("expert"), dx), jnp.bitwise_xor(lax.axis_index("dp"), dz))
             sel_ref[at], send_refs[at][0, 0:CAP, :], send_refs[at][0, CAP : 2 * CAP, :] = rows_for(expert)
         return
     for expert in range(EXPERTS):
@@ -95,21 +100,38 @@
                     send_refs[0][z * plan.owners + x, CAP : 2 * CAP, :] = q_rows
 
 
-def dispatch(plan, where, ids, gates, tokens, cotangent, fetched):
+def dispatch(plan, ids, gates, tokens, cotangent):
     count, narrow = tokens.shape
     sends = [jax.ShapeDtypeStruct((1, 2 * CAP, narrow), BF16)] * len(PARTNERS)
     if not plan.hops:
         sends = [jax.ShapeDtypeStruct((plan.devices, 2 * CAP, narrow), BF16)]
+    arrays = (ids.T, gates.T, tokens, cotangent)
     got = pl.pallas_call(
         functools.partial(dispatch_kernel, plan),
         out_shape=[jax.ShapeDtypeStruct((EXPERTS, CAP, count), BF16)] + sends,
-        in_specs=[SMEM] + [VMEM] * 4,
+        in_specs=[ANY] * 4,
+        scratch_shapes=[pltpu.VMEM(array.shape, array.dtype) for array in arrays] + [pltpu.SemaphoreType.DMA((4,))],
         out_specs=[VMEM] * (1 + len(sends)),
-        compiler_params=params(8),
+        compiler_params=params(58),
+        name="dispatch",
+    )(*arrays)
+    return got[0], got[1:]
+
+
+def window_kernel(array_ref, *refs):
+    refs[-1][...] = array_ref[...]
+
+
+def window(array, after, fetched, name):
+    return pl.pallas_call(
+        window_kernel,
+        out_shape=jax.ShapeDtypeStruct(array.shape, array.dtype),
+        in_specs=[VMEM] + [ANY] * len(after),
+        out_specs=VMEM,
+        compiler_params=params(2),
         cost_estimate=cost(400 * fetched, fetched),
-        name="dispatch",
-    )(where, ids.T, gates.T, tokens, cotangent)
-    return got[0], got[1:]
+        name=name,
+    )(array, *after)
 
 
 def forward_kernel(plan, half, block, *refs):
@@ -117,11 +139,11 @@
     if half is None:
         rows_ref, w_ref = refs[:2]
     else:
-        where_ref, pieces, w_ref, rows_ref = refs[0], refs[1:-3], refs[-3], refs[-2]
+        pieces, w_ref, rows_ref = refs[:-3], refs[-3], refs[-2]
         narrow = pieces[0].shape[2]
         for z in range(plan.replicas):
             if plan.hops:
-                index = jnp.bitwise_xor(where_ref[1], z)
+                index = jnp.bitwise_xor(lax.axis_index("dp"), z)
                 lanes = pl.ds(pl.multiple_of(index * narrow, 128), narrow)
             else:
                 lanes = pl.ds(z * narrow, narrow)
@@ -134,7 +156,7 @@
         part_ref[:, cols] = jnp.dot(rows_ref[...], w_ref[:, cols], preferred_element_type=F32).astype(BF16)
 
 
-def forward(plan, where, rows_in, half, w, name, wanted=512):
+def forward(plan, rows_in, half, w, name, wanted=512):
     width, columns = w.shape
     block = block_of(columns, wanted)
     fresh = half is not None
@@ -143,15 +165,15 @@
     return pl.pallas_call(
         functools.partial(forward_kernel, plan, half, block),
         out_shape=outs,
-        in_specs=[SMEM] * fresh + [VMEM] * (1 + len(rows_in)),
+        in_specs=[VMEM] * (1 + len(rows_in)),
         out_specs=[VMEM] * len(outs),
         compiler_params=params(4),
         cost_estimate=cost(2 * plan.rows * width * columns, 8 * 1024 * 1024),
         name=name,
-    )(*([where] * fresh), *rows_in, w)
-
-
-def rows_kernel(plan, where_ref, g0, g1, u0, u1, d0, d1, wg_ref, wu_ref, h_ref, dg_ref, du_ref, *rest):
+    )(*rows_in, w)
+
+
+def rows_kernel(plan, g0, g1, u0, u1, d0, d1, wg_ref, wu_ref, h_ref, dg_ref, du_ref, *rest):
     outs, total = rest[:-1], rest[-1]
     gate = g0[...].astype(F32) + g1[...].astype(F32)
     up = u0[...].astype(F32) + u1[...].astype(F32)
@@ -163,8 +185,8 @@
     d_up = (hidden * act).astype(BF16)
     dg_ref[...] = d_gate
     du_ref[...] = d_up
-    term = lax.dot_general(d_gate, wg_ref[...], TURNED, preferred_element_type=F32)
-    term = term + lax.dot_general(d_up, wu_ref[...], TURNED, preferred_element_type=F32)
+    term = lax.dot_general(wg_ref[...], d_gate, TURNED, preferred_element_type=F32)
+    term = term + lax.dot_general(wu_ref[...], d_up, TURNED, preferred_element_type=F32)
     step = pl.program_id(0)
 
     @pl.when(step == 0)
@@ -179,17 +201,14 @@
     def _():
         narrow = outs[0].shape[2]
         for z in range(plan.replicas):
-            if plan.hops:
-                index = jnp.bitwise_xor(where_ref[1], z)
-                lanes = pl.ds(pl.multiple_of(index * narrow, 128), narrow)
-            else:
-                lanes = pl.ds(z * narrow, narrow)
+            index = jnp.bitwise_xor(lax.axis_index("dp"), z) if plan.hops else z
+            turned = total[pl.ds(pl.multiple_of(index * narrow, 32), narrow), :].T.astype(BF16)
             for x in range(plan.owners):
                 at = z // 2 * plan.owners + x if plan.hops else z * plan.owners + x
-                outs[z % len(outs)][at] = total[x * CAP : (x + 1) * CAP, lanes].astype(BF16)
-
-
-def row_grads(plan, where, parts, wg, wu, wanted=1024):
+                outs[z % len(outs)][at] = turned[x * CAP : (x + 1) * CAP, :]
+
+
+def row_grads(plan, parts, wg, wu, wanted=1024):
     width, columns = wg.shape
     narrow = width // plan.replicas
     block = block_of(columns, wanted)
@@ -202,13 +221,13 @@
         functools.partial(rows_kernel, plan),
         grid=(columns // block,),
         out_shape=[hidden] * 3 + [pieces] * sets,
-        in_specs=[SMEM] + [part_spec] * 6 + [strip] * 2,
+        in_specs=[part_spec] * 6 + [strip] * 2,
         out_specs=[part_spec] * 3 + [pl.BlockSpec(pieces.shape, lambda i: (0, 0, 0))] * sets,
-        scratch_shapes=[pltpu.VMEM((plan.rows, width), F32)],
-        compiler_params=params(48),
+        scratch_shapes=[pltpu.VMEM((width, plan.rows), F32)],
+        compiler_params=params(32),
         cost_estimate=cost(4 * plan.rows * width * columns, 4 * width * columns),
         name="row_grads",
-    )(where, *parts, wg, wu)
+    )(*parts, wg, wu)
     return outs[:3], outs[3:]
 
 
@@ -290,34 +309,33 @@
 
 def body(mesh, tokens, cotangent, expert_ids, gate_values, gate_weight, up_weight, down_weight):
     plan = Plan(mesh, gate_weight.shape[1])
-    where = jnp.stack((lax.axis_index("expert"), lax.axis_index("dp"))).astype(jnp.int32)
     wg, wu, wd = gate_weight, up_weight, down_weight
 
     def swap(part):
         size = mesh.shape["tensor"]
         return lax.ppermute(part, "tensor", [(i, i ^ 1) for i in range(size)])
 
-    sel, sends = dispatch(plan, where, expert_ids, gate_values, tokens, cotangent, 6 * wg.size)
+    sel, sends = dispatch(plan, expert_ids, gate_values, tokens, cotangent)
     if plan.hops:
         own, to_x, to_z, to_xz = sends
-        far_x = plan.send(to_xz, 1, 0)
-        far_own, near_own = plan.send(to_z, 0, 2), plan.send(own, 0, 1)
+        own = window(own, (), 4 * wg.size, "window_own")
+        to_x = window(to_x, (own,), 8 * wg.size, "window_side")
+        far_own, far_x = plan.send(to_z, 0, 2), plan.send(to_xz, 1, 2)
+        near_own, near_x = plan.send(own, 0, 1), plan.send(to_x, 1, 1)
         from_x = plan.send(to_x, 1, 0)
-        far_x, last_own = plan.send(far_x, 0, 2), plan.send(far_own, 0, 1)
-        near_x = plan.send(from_x, 0, 1)
-        last_x = plan.send(far_x, 0, 1)
+        last_own, last_x = plan.send(far_own, 0, 1), plan.send(far_x, 0, 1)
         got = [own, from_x, near_own, near_x, far_own, far_x, last_own, last_x]
     else:
         got = [plan.scatter(sends[0])]
-    q_full, part_h = forward(plan, where, got, 1, wd, "forward_h")
+    q_full, part_h = forward(plan, got, 1, wd, "forward_h")
     other_h = swap(part_h)
-    x_full, part_g = forward(plan, where, got, 0, wg, "forward_g")
+    x_full, part_g = forward(plan, got, 0, wg, "forward_g")
     other_g = swap(part_g)
-    (part_u,) = forward(plan, where, [x_full], None, wu, "forward_u")
+    (part_u,) = forward(plan, [x_full], None, wu, "forward_u")
     other_u = swap(part_u)
     parts = (part_g, other_g, part_u, other_u, part_h, other_h)
     factor = 1.0 / math.sqrt(tokens.shape[0] * plan.owners)
-    (h, d_gate, d_up), pieces = row_grads(plan, where, parts, wg, wu)
+    (h, d_gate, d_up), pieces = row_grads(plan, parts, wg, wu)
     arrived = plan.send(pieces[1], 0, 1) if plan.hops else plan.scatter(pieces[0])
     grad_gate, grad_up, done = weight_grads(factor, ((x_full, d_gate), (x_full, d_up)), pieces[0], "grads_gu")
     if plan.hops:

time: 83.5 us -> 74.4 us (0.89)
  local copies, waits for them, and re-layouts: 8.67 us -> 1.82 us
  Pallas kernels: 39.4 us -> 37.9 us
  starting transfers between devices: 18.2 us -> 16.9 us
    unnamed x28 -> x24, local copies, waits for them, and re-layouts: 8.67 us -> 1.82 us
    pallas_call x1, Pallas kernels: 14.6 us -> 13.1 us  [row_grads(): pl.pallas_call(functools.partial(rows_kernel, plan), grid=(columns // blo...]
    ppermute x12 -> x11, starting transfers between devices: 17.5 us -> 16.2 us  [send(): return lax.ppermute(array, ('dp', 'expert'), pairs)]
    pallas_call x3, Pallas kernels: 7.86 us -> 6.69 us  [forward(): pl.pallas_call(functools.partial(forward_kernel, plan, half, block), out_...]
    pallas_call x1, Pallas kernels: 1 us -> 2.12 us  [dispatch(): pl.pallas_call(functools.partial(dispatch_kernel, plan), out_shape=[jax.S...]
    ppermute x3, waiting for transfers between devices: 2.98 us -> 3.87 us  [swap(): return lax.ppermute(part, 'tensor', [(i, i ^ 1) for i in range(size)])]
    ppermute x12 -> x11, waiting for transfers between devices: 13.1 us -> 12.8 us  [send(): return lax.ppermute(array, ('dp', 'expert'), pairs)]
  transfers between devices with their start and end apart: 15 -> 14, of which waited for: 9 -> 10; matrix products, arithmetic and copies ran while one was open for 0% -> 0% of each run, Pallas kernels for 21% -> 23%
where the time goes in v3:
time: 74.4 us; the launch traced here: 74.2 us
  Pallas kernels  37.9 us (51%)
  starting transfers between devices  16.9 us (23%)
  waiting for transfers between devices  16.6 us (22%)
  local copies, waits for them, and re-layouts  1.82 us (2%)
  between operations  0.85 us (1%)
    ppermute x11, starting transfers between devices, send(): return lax.ppermute(array, ('dp', 'expert'), pairs)  16.2 us
    pallas_call x2, Pallas kernels, weight_grads(): pl.pallas_call(functools.partial(weights_kernel, factor, block, many), ou...  15 us
    pallas_call x1, Pallas kernels, row_grads(): pl.pallas_call(functools.partial(rows_kernel, plan), grid=(columns // blo...  13.1 us
    ppermute x11, waiting for transfers between devices, send(): return lax.ppermute(array, ('dp', 'expert'), pairs)  12.8 us
    pallas_call x3, Pallas kernels, forward(): pl.pallas_call(functools.partial(forward_kernel, plan, half, block), out_...  6.69 us
    ppermute x3, waiting for transfers between devices, swap(): return lax.ppermute(part, 'tensor', [(i, i ^ 1) for i in range(size)])  3.87 us
    pallas_call x1, Pallas kernels, dispatch(): pl.pallas_call(functools.partial(dispatch_kernel, plan), out_shape=[jax.S...  2.12 us
    unnamed x24, local copies, waits for them, and re-layouts  1.82 us
  transfers between devices with their start and end apart: 14, of which 10 were waited for; matrix products, arithmetic and copies ran while one was open for 0% of the time, Pallas kernels for 23%

profile of v3, /device:TPU:0, one launch (start us, length us, event | category | flops | bytes accessed | tf_op | source)
XLA Modules:
  0.0 74.2 jit_solution(5113730177755901305)
XLA Ops:
  0.6 2.1 %dispatch.1 = (bf16[4,80,128]{2,1,0:T(8,128)(2,1)}, bf16[1,160,384]{2,1,0:T(8,128)(2,1)}, bf16[1,160,384]{2,1,0:T(8,128)(2,1)}, bf16[1,160,384]{2,1,0:T(8,128)(2,1)}, bf16[1,160,384]{2,1,0:T(8,128)(2,1)}) custom-call(s32[2,128]{1,0:T(2,128)} %bitcast.8, bf16[2,128]{1,0:T(2,128)(2,1)} %bitcast.9, bf16[128,384]{1,0:T(8,128)(2,1)} %refs_2_.1, ...), custom_call_target="tpu_custom_call" | custom-call | tf_op jit(solution)/shard_map/dispatch/pallas_call | solution.py:109
  2.8 4.1 %collective-permute-start.3 = (bf16[1,160,384]{2,1,0:T(8,128)(2,1)}, bf16[1,160,384]{2,1,0:T(8,128)(2,1)S(1)}, u32[]{:S(2)}, u32[]{:S(2)}) collective-permute-start(bf16[1,160,384]{2,1,0:T(8,128)(2,1)} %get-tuple-element.29), channel_id=1, source_target_pairs={{0,8},{4,12},{8,0},{12,4},{2,10},{6,14},{10,2},{14,6},{1,9},{5,13}... | collective-permute-start | bytes 368648 | tf_op jit(solution)/shard_map/ppermute | solution.py:54
  6.9 1.3 %collective-permute-start.4 = (bf16[1,160,384]{2,1,0:T(8,128)(2,1)}, bf16[1,160,384]{2,1,0:T(8,128)(2,1)S(1)}, u32[]{:S(2)}, u32[]{:S(2)}) collective-permute-start(bf16[1,160,384]{2,1,0:T(8,128)(2,1)} %get-tuple-element.30), channel_id=1, source_target_pairs={{0,10},{4,14},{8,2},{12,6},{2,8},{6,12},{10,0},{14,4},{1,11},{5,15... | collective-permute-start | bytes 368648 | tf_op jit(solution)/shard_map/ppermute | solution.py:54
  8.1 0.0 copy-start.2
  8.1 0.9 %copy-done.2 = bf16[1,160,384]{2,1,0:T(8,128)(2,1)S(1)} copy-done((bf16[1,160,384]{2,1,0:T(8,128)(2,1)S(1)}, bf16[1,160,384]{2,1,0:T(8,128)(2,1)}, u32[]{:S(2)}) %copy-start.2) | copy-done | bytes 122904
  9.0 0.0 copy-start.1
  9.0 0.0 slice-start.3
  9.0 0.0 slice-start
  9.1 0.9 %copy-done.1 = bf16[1,160,384]{2,1,0:T(8,128)(2,1)S(1)} copy-done((bf16[1,160,384]{2,1,0:T(8,128)(2,1)S(1)}, bf16[1,160,384]{2,1,0:T(8,128)(2,1)}, u32[]{:S(2)}) %copy-start.1) | copy-done | bytes 122904
  9.9 0.0 slice-start.1
  9.9 0.0 slice-start.2
  9.9 0.0 slice-start.4
  9.9 0.0 slice-start.5
  10.0 1.6 %collective-permute-start.2 = (bf16[1,160,384]{2,1,0:T(8,128)(2,1)S(1)}, bf16[1,160,384]{2,1,0:T(8,128)(2,1)S(1)}, u32[]{:S(2)}, u32[]{:S(2)}) collective-permute-start(bf16[1,160,384]{2,1,0:T(8,128)(2,1)S(1)} %window_side.1), channel_id=1, source_target_pairs={{0,6},{4,2},{8,14},{12,10},{2,4},{6,0},{10,12},{14,8},{1,7},{5,3},... | collective-permute-start | bytes 368648 | tf_op jit(solution)/shard_map/ppermute | solution.py:54
  11.6 1.5 %collective-permute-start = (bf16[1,160,384]{2,1,0:T(8,128)(2,1)S(1)}, bf16[1,160,384]{2,1,0:T(8,128)(2,1)S(1)}, u32[]{:S(2)}, u32[]{:S(2)}) collective-permute-start(bf16[1,160,384]{2,1,0:T(8,128)(2,1)S(1)} %window_side.1), channel_id=1, source_target_pairs={{0,2},{4,6},{8,10},{12,14},{2,0},{6,4},{10,8},{14,12},{1,3},{5,7},... | collective-permute-start | bytes 368648 | tf_op jit(solution)/shard_map/ppermute | solution.py:54
  13.1 0.4 collective-permute-start.1
  13.5 3.0 %collective-permute-done.3.refs_4_ = bf16[1,160,384]{2,1,0:T(8,128)(2,1)S(1)} collective-permute-done((bf16[1,160,384]{2,1,0:T(8,128)(2,1)}, bf16[1,160,384]{2,1,0:T(8,128)(2,1)S(1)}, u32[]{:S(2)}, u32[]{:S(2)}) %collective-permute-start.3) | collective-permute-done | bytes 122912 | tf_op jit(solution)/shard_map/ppermute | solution.py:54
  16.5 0.1 collective-permute-start.5
  16.6 2.8 %collective-permute-done.4.refs_5_ = bf16[1,160,384]{2,1,0:T(8,128)(2,1)S(1)} collective-permute-done((bf16[1,160,384]{2,1,0:T(8,128)(2,1)}, bf16[1,160,384]{2,1,0:T(8,128)(2,1)S(1)}, u32[]{:S(2)}, u32[]{:S(2)}) %collective-permute-start.4) | collective-permute-done | bytes 122912 | tf_op jit(solution)/shard_map/ppermute | solution.py:54
  19.4 0.0 collective-permute-start.6
  19.4 1.8 %collective-permute-done.2.refs_3_ = bf16[1,160,384]{2,1,0:T(8,128)(2,1)S(1)} collective-permute-done((bf16[1,160,384]{2,1,0:T(8,128)(2,1)S(1)}, bf16[1,160,384]{2,1,0:T(8,128)(2,1)S(1)}, u32[]{:S(2)}, u32[]{:S(2)}) %collective-permute-start.2) | collective-permute-done | bytes 122912 | tf_op jit(solution)/shard_map/ppermute | solution.py:54
  21.3 0.0 collective-permute-done.refs_1_
  21.3 0.3 collective-permute-done.1.refs_2_
  21.6 2.6 %collective-permute-done.5.refs_6_ = bf16[1,160,384]{2,1,0:T(8,128)(2,1)S(1)} collective-permute-done((bf16[1,160,384]{2,1,0:T(8,128)(2,1)S(1)}, bf16[1,160,384]{2,1,0:T(8,128)(2,1)S(1)}, u32[]{:S(2)}, u32[]{:S(2)}) %collective-permute-start.5) | collective-permute-done | bytes 122912 | tf_op jit(solution)/shard_map/ppermute | solution.py:54
  24.2 2.0 %collective-permute-done.6.refs_7_ = bf16[1,160,384]{2,1,0:T(8,128)(2,1)S(1)} collective-permute-done((bf16[1,160,384]{2,1,0:T(8,128)(2,1)S(1)}, bf16[1,160,384]{2,1,0:T(8,128)(2,1)S(1)}, u32[]{:S(2)}, u32[]{:S(2)}) %collective-permute-start.6) | collective-permute-done | bytes 122912 | tf_op jit(solution)/shard_map/ppermute | solution.py:54
  26.2 0.0 slice-done
  26.2 0.0 slice-done.1
  26.2 0.0 slice-done.2
  26.2 0.0 slice-start.6
  26.2 0.0 slice-start.7
  26.2 2.2 %forward_g.1 = (bf16[160,1536]{1,0:T(8,128)(2,1)S(1)}, bf16[160,4096]{1,0:T(8,128)(2,1)S(1)}) custom-call(bf16[1,160,384]{2,1,0:T(8,128)(2,1)S(1)} %window_own.1.refs_0_, bf16[1,160,384]{2,1,0:T(8,128)(2,1)S(1)} %collective-permute-done.refs_1_, bf16[1,160,384]{2,1,0:T(8,128)(2,1)S(1)} %collective-permute-done.1.refs_2_, ...), custom_call_target="tpu_custom_call" | custom-call | flops 2013265920 | bytes 8388608 | tf_op jit(solution)/shard_map/forward_g/pallas_call | solution.py:165
  28.5 0.0 slice-done.3
  28.5 0.0 slice-done.4
  28.5 0.0 slice-done.5
  28.5 0.0 slice-start.8
  28.5 2.2 %forward_u.1.u0 = bf16[160,4096]{1,0:T(8,128)(2,1)S(1)} custom-call(bf16[160,1536]{1,0:T(8,128)(2,1)S(1)} %get-tuple-element.32.refs_0_.refs_2_, bf16[1536,4096]{1,0:T(8,128)(2,1)S(1)} %bitcast.5), custom_call_target="tpu_custom_call" | custom-call | flops 2013265920 | bytes 8388608 | tf_op jit(solution)/shard_map/forward_u/pallas_call | solution.py:165
  30.8 0.1 collective-permute-start.8
  30.8 0.5 collective-permute-start.7
  31.3 0.0 slice-done.6
  31.3 0.0 slice-done.7
  31.3 0.0 slice-done.8
  31.3 2.2 %forward_h.1 = (bf16[160,1536]{1,0:T(8,128)(2,1)S(1)}, bf16[160,4096]{1,0:T(8,128)(2,1)S(1)}) custom-call(bf16[1,160,384]{2,1,0:T(8,128)(2,1)S(1)} %window_own.1.refs_0_, bf16[1,160,384]{2,1,0:T(8,128)(2,1)S(1)} %collective-permute-done.refs_1_, bf16[1,160,384]{2,1,0:T(8,128)(2,1)S(1)} %collective-permute-done.1.refs_2_, ...), custom_call_target="tpu_custom_call" | custom-call | flops 2013265920 | bytes 8388608 | tf_op jit(solution)/shard_map/forward_h/pallas_call | solution.py:165
  33.6 0.1 collective-permute-start.9
  33.7 0.1 collective-permute-done.8.u1
  33.9 1.9 %collective-permute-done.7.g1 = bf16[160,4096]{1,0:T(8,128)(2,1)S(1)} collective-permute-done((bf16[160,4096]{1,0:T(8,128)(2,1)S(1)}, bf16[160,4096]{1,0:T(8,128)(2,1)S(1)}, u32[]{:S(2)}, u32[]{:S(2)}) %collective-permute-start.7) | collective-permute-done | bytes 1310752 | tf_op jit(solution)/shard_map/ppermute | solution.py:316
  35.7 1.9 %collective-permute-done.9.d1 = bf16[160,4096]{1,0:T(8,128)(2,1)S(1)} collective-permute-done((bf16[160,4096]{1,0:T(8,128)(2,1)S(1)}, bf16[160,4096]{1,0:T(8,128)(2,1)S(1)}, u32[]{:S(2)}, u32[]{:S(2)}) %collective-permute-start.9) | collective-permute-done | bytes 1310752 | tf_op jit(solution)/shard_map/ppermute | solution.py:316
  37.6 13.1 %row_grads.1 = (bf16[160,4096]{1,0:T(8,128)(2,1)S(1)}, bf16[160,4096]{1,0:T(8,128)(2,1)S(1)}, bf16[160,4096]{1,0:T(8,128)(2,1)S(1)}, bf16[4,80,384]{2,1,0:T(8,128)(2,1)S(1)}, bf16[4,80,384]{2,1,0:T(8,128)(2,1)S(1)}) custom-call(bf16[160,4096]{1,0:T(8,128)(2,1)S(1)} %get-tuple-element.31.g0, bf16[160,4096]{1,0:T(8,128)(2,1)S(1)} %collective-permute-done.7.g1, ...), custom_call_target="tpu_custom_call" | custom-call | flops 4026531840 | bytes 25165824 | tf_op jit(solution)/shard_map/row_grads/pallas_call | solution.py:220
  50.7 0.1 collective-permute-start.10
  50.8 9.1 %grads_gu.1 = (bf16[1536,4096]{1,0:T(8,128)(2,1)}, bf16[1536,4096]{1,0:T(8,128)(2,1)}, f32[8,128]{1,0:T(8,128)S(1)}) custom-call(bf16[160,1536]{1,0:T(8,128)(2,1)S(1)} %get-tuple-element.32.refs_0_.refs_2_, bf16[160,4096]{1,0:T(8,128)(2,1)S(1)} %get-tuple-element.36.refs_1_, bf16[160,1536]{1,0:T(8,128)(2,1)S(1)} %get-tuple-element.32.refs_0_.refs_2_, ...), custom_call_target="tpu_custom_call" | custom-call | flops 4026531840 | bytes 25165824 | tf_op jit(solution)/shard_map/grads_gu/pallas_call | solution.py:255
  60.0 0.0 collective-permute-done.10.got_ref
  60.0 0.1 pair_sum.1
  60.0 2.2 %collective-permute-start.11 = (bf16[1,80,384]{2,1,0:T(8,128)(2,1)S(1)}, bf16[1,80,384]{2,1,0:T(8,128)(2,1)S(1)}, u32[]{:S(2)}, u32[]{:S(2)}) collective-permute-start(bf16[1,80,384]{2,1,0:T(8,128)(2,1)S(1)} %get-tuple-element.40), channel_id=1, source_target_pairs={{0,2},{4,6},{8,10},{12,14},{2,0},{6,4},{10,8},{14,12},{1,3},{5,7},... | collective-permute-start | bytes 184328 | tf_op jit(solution)/shard_map/ppermute | solution.py:54
  62.2 4.9 %collective-permute-start.12 = (bf16[1,80,384]{2,1,0:T(8,128)(2,1)S(1)}, bf16[1,80,384]{2,1,0:T(8,128)(2,1)S(1)}, u32[]{:S(2)}, u32[]{:S(2)}) collective-permute-start(bf16[1,80,384]{2,1,0:T(8,128)(2,1)S(1)} %get-tuple-element.41), channel_id=1, source_target_pairs={{0,8},{4,12},{8,0},{12,4},{2,10},{6,14},{10,2},{14,6},{1,9},{5,13}... | collective-permute-start | bytes 184328 | tf_op jit(solution)/shard_map/ppermute | solution.py:54
  67.1 0.0 collective-permute-start.13
  67.2 0.0 copy-start
  67.2 5.8 %grad_down.1 = (bf16[1536,4096]{1,0:T(8,128)(2,1)}, f32[8,128]{1,0:T(8,128)}) custom-call(bf16[160,1536]{1,0:T(8,128)(2,1)S(1)} %get-tuple-element.45.refs_0_, bf16[160,4096]{1,0:T(8,128)(2,1)S(1)} %get-tuple-element.46.refs_1_, bf16[1,80,384]{2,1,0:T(8,128)(2,1)S(1)} %get-tuple-element.39.refs_0_.refs_2_), custom_call_target="tpu_custom_call" | custom-call | flops 2013265920 | bytes 12582912 | tf_op jit(solution)/shard_map/grad_down/pallas_call | solution.py:255
  73.0 0.0 collective-permute-done.11.refs_1_
  73.0 0.0 collective-permute-done.12.refs_2_
  73.0 0.2 collective-permute-done.13.refs_3_
  73.3 0.0 copy-done
  73.3 0.9 %combine.1 = bf16[128,384]{1,0:T(8,128)(2,1)} custom-call(bf16[4,80,128]{2,1,0:T(8,128)(2,1)S(1)} %copy-done, bf16[1,80,384]{2,1,0:T(8,128)(2,1)S(1)} %get-tuple-element.39.refs_0_.refs_2_, bf16[1,80,384]{2,1,0:T(8,128)(2,1)S(1)} %collective-permute-done.11.refs_1_, bf16[1,80,384]{2,1,0:T(8,128)(2,1)S(1)} %collective-permute-done.12.refs_2_, ...), custom_call_target="tpu_custom_call" | custom-call | tf_op jit(solution)/shard_map/combine/pallas_call | solution.py:300
  (5 shorter events, 0.0 us)
Async XLA Ops:
  2.8 13.7 %collective-permute-start.3 = (bf16[1,160,384]{2,1,0:T(8,128)(2,1)}, bf16[1,160,384]{2,1,0:T(8,128)(2,1)S(1)}, u32[]{:S(2)}, u32[]{:S(2)}) collective-permute-start(bf16[1,160,384]{2,1,0:T(8,128)(2,1)} %get-tuple-element.29), channel_id=1, source_target_pairs={{0,8},{4,12},{8,0},{12,4},{2,10},{6,14},{10,2},{14,6},{1,9},{5,13}... | collective-permute-start | bytes 368648 | tf_op jit(solution)/shard_map/ppermute | solution.py:54
  6.9 12.6 %collective-permute-start.4 = (bf16[1,160,384]{2,1,0:T(8,128)(2,1)}, bf16[1,160,384]{2,1,0:T(8,128)(2,1)S(1)}, u32[]{:S(2)}, u32[]{:S(2)}) collective-permute-start(bf16[1,160,384]{2,1,0:T(8,128)(2,1)} %get-tuple-element.30), channel_id=1, source_target_pairs={{0,10},{4,14},{8,2},{12,6},{2,8},{6,12},{10,0},{14,4},{1,11},{5,15... | collective-permute-start | bytes 368648 | tf_op jit(solution)/shard_map/ppermute | solution.py:54
  8.1 0.9 %copy-start.2 = (bf16[1,160,384]{2,1,0:T(8,128)(2,1)S(1)}, bf16[1,160,384]{2,1,0:T(8,128)(2,1)}, u32[]{:S(2)}) copy-start(bf16[1,160,384]{2,1,0:T(8,128)(2,1)} %get-tuple-element.27.array_ref) | copy-start | bytes 368644
  9.0 0.9 %copy-start.1 = (bf16[1,160,384]{2,1,0:T(8,128)(2,1)S(1)}, bf16[1,160,384]{2,1,0:T(8,128)(2,1)}, u32[]{:S(2)}) copy-start(bf16[1,160,384]{2,1,0:T(8,128)(2,1)} %get-tuple-element.28.array_ref) | copy-start | bytes 368644
  9.0 19.5 %slice-start.3 = ((s8[12582912]{0:T(1024)(128)(4,1)}), s8[4194304]{0:T(1024)(128)(4,1)S(1)}, s32[]{:S(2)}) async-start(s8[12582912]{0:T(1024)(128)(4,1)} %bitcast.4), calls=%async_computation.3 | async-start | bytes 8388608
  9.0 17.2 %slice-start = ((s8[12582912]{0:T(1024)(128)(4,1)}), s8[4194304]{0:T(1024)(128)(4,1)S(1)}, s32[]{:S(2)}) async-start(s8[12582912]{0:T(1024)(128)(4,1)} %bitcast.2), calls=%async_computation | async-start | bytes 8388608
  9.9 16.3 %slice-start.1 = ((s8[12582912]{0:T(1024)(128)(4,1)}), s8[4194304]{0:T(1024)(128)(4,1)S(1)}, s32[]{:S(2)}) async-start(s8[12582912]{0:T(1024)(128)(4,1)} %bitcast.2), calls=%async_computation.1 | async-start | bytes 8388608
  9.9 16.3 %slice-start.2 = ((s8[12582912]{0:T(1024)(128)(4,1)}), s8[4194304]{0:T(1024)(128)(4,1)S(1)}, s32[]{:S(2)}) async-start(s8[12582912]{0:T(1024)(128)(4,1)} %bitcast.2), calls=%async_computation.2 | async-start | bytes 8388608
  9.9 18.6 %slice-start.4 = ((s8[12582912]{0:T(1024)(128)(4,1)}), s8[4194304]{0:T(1024)(128)(4,1)S(1)}, s32[]{:S(2)}) async-start(s8[12582912]{0:T(1024)(128)(4,1)} %bitcast.4), calls=%async_computation.4 | async-start | bytes 8388608
  9.9 18.6 %slice-start.5 = ((s8[12582912]{0:T(1024)(128)(4,1)}), s8[4194304]{0:T(1024)(128)(4,1)S(1)}, s32[]{:S(2)}) async-start(s8[12582912]{0:T(1024)(128)(4,1)} %bitcast.4), calls=%async_computation.5 | async-start | bytes 8388608
  10.0 11.3 %collective-permute-start.2 = (bf16[1,160,384]{2,1,0:T(8,128)(2,1)S(1)}, bf16[1,160,384]{2,1,0:T(8,128)(2,1)S(1)}, u32[]{:S(2)}, u32[]{:S(2)}) collective-permute-start(bf16[1,160,384]{2,1,0:T(8,128)(2,1)S(1)} %window_side.1), channel_id=1, source_target_pairs={{0,6},{4,2},{8,14},{12,10},{2,4},{6,0},{10,12},{14,8},{1,7},{5,3},... | collective-permute-start | bytes 368648 | tf_op jit(solution)/shard_map/ppermute | solution.py:54
  11.6 9.7 %collective-permute-start = (bf16[1,160,384]{2,1,0:T(8,128)(2,1)S(1)}, bf16[1,160,384]{2,1,0:T(8,128)(2,1)S(1)}, u32[]{:S(2)}, u32[]{:S(2)}) collective-permute-start(bf16[1,160,384]{2,1,0:T(8,128)(2,1)S(1)} %window_side.1), channel_id=1, source_target_pairs={{0,2},{4,6},{8,10},{12,14},{2,0},{6,4},{10,8},{14,12},{1,3},{5,7},... | collective-permute-start | bytes 368648 | tf_op jit(solution)/shard_map/ppermute | solution.py:54
  13.1 8.5 %collective-permute-start.1 = (bf16[1,160,384]{2,1,0:T(8,128)(2,1)S(1)}, bf16[1,160,384]{2,1,0:T(8,128)(2,1)S(1)}, u32[]{:S(2)}, u32[]{:S(2)}) collective-permute-start(bf16[1,160,384]{2,1,0:T(8,128)(2,1)S(1)} %window_own.1.refs_0_), channel_id=1, source_target_pairs={{0,4},{4,0},{8,12},{12,8},{2,6},{6,2},{10,14},{14,10},{1,5},{5,1},... | collective-permute-start | bytes 368648 | tf_op jit(solution)/shard_map/ppermute | solution.py:54
  16.5 7.7 %collective-permute-start.5 = (bf16[1,160,384]{2,1,0:T(8,128)(2,1)S(1)}, bf16[1,160,384]{2,1,0:T(8,128)(2,1)S(1)}, u32[]{:S(2)}, u32[]{:S(2)}) collective-permute-start(bf16[1,160,384]{2,1,0:T(8,128)(2,1)S(1)} %collective-permute-done.3.refs_4_), channel_id=1, source_target_pairs={{0,4},{4,0},{8,12},{12,8},{2,6},{6,2},{10,14},{14,10},{1,5},{5,1},... | collective-permute-start | bytes 368648 | tf_op jit(solution)/shard_map/ppermute | solution.py:54
  19.4 6.8 %collective-permute-start.6 = (bf16[1,160,384]{2,1,0:T(8,128)(2,1)S(1)}, bf16[1,160,384]{2,1,0:T(8,128)(2,1)S(1)}, u32[]{:S(2)}, u32[]{:S(2)}) collective-permute-start(bf16[1,160,384]{2,1,0:T(8,128)(2,1)S(1)} %collective-permute-done.4.refs_5_), channel_id=1, source_target_pairs={{0,4},{4,0},{8,12},{12,8},{2,6},{6,2},{10,14},{14,10},{1,5},{5,1},... | collective-permute-start | bytes 368648 | tf_op jit(solution)/shard_map/ppermute | solution.py:54
  26.2 5.1 %slice-start.6 = ((s8[12582912]{0:T(1024)(128)(4,1)}), s8[4194304]{0:T(1024)(128)(4,1)S(1)}, s32[]{:S(2)}) async-start(s8[12582912]{0:T(1024)(128)(4,1)} %bitcast.6), calls=%async_computation.6 | async-start | bytes 8388608
  26.2 5.1 %slice-start.7 = ((s8[12582912]{0:T(1024)(128)(4,1)}), s8[4194304]{0:T(1024)(128)(4,1)S(1)}, s32[]{:S(2)}) async-start(s8[12582912]{0:T(1024)(128)(4,1)} %bitcast.6), calls=%async_computation.7 | async-start | bytes 8388608
  28.5 2.8 %slice-start.8 = ((s8[12582912]{0:T(1024)(128)(4,1)}), s8[4194304]{0:T(1024)(128)(4,1)S(1)}, s32[]{:S(2)}) async-start(s8[12582912]{0:T(1024)(128)(4,1)} %bitcast.6), calls=%async_computation.8 | async-start | bytes 8388608
  30.8 3.1 %collective-permute-start.8 = (bf16[160,4096]{1,0:T(8,128)(2,1)S(1)}, bf16[160,4096]{1,0:T(8,128)(2,1)S(1)}, u32[]{:S(2)}, u32[]{:S(2)}) collective-permute-start(bf16[160,4096]{1,0:T(8,128)(2,1)S(1)} %forward_u.1.u0), channel_id=1, source_target_pairs={{0,1},{1,0},{2,3},{3,2},{4,5},{5,4},{6,7},{7,6},{8,9},{9,8},{10,11... | collective-permute-start | bytes 3932168 | tf_op jit(solution)/shard_map/ppermute | solution.py:316
  30.8 4.9 %collective-permute-start.7 = (bf16[160,4096]{1,0:T(8,128)(2,1)S(1)}, bf16[160,4096]{1,0:T(8,128)(2,1)S(1)}, u32[]{:S(2)}, u32[]{:S(2)}) collective-permute-start(bf16[160,4096]{1,0:T(8,128)(2,1)S(1)} %get-tuple-element.31.g0), channel_id=1, source_target_pairs={{0,1},{1,0},{2,3},{3,2},{4,5},{5,4},{6,7},{7,6},{8,9},{9,8},{10,11... | collective-permute-start | bytes 3932168 | tf_op jit(solution)/shard_map/ppermute | solution.py:316
  33.6 4.0 %collective-permute-start.9 = (bf16[160,4096]{1,0:T(8,128)(2,1)S(1)}, bf16[160,4096]{1,0:T(8,128)(2,1)S(1)}, u32[]{:S(2)}, u32[]{:S(2)}) collective-permute-start(bf16[160,4096]{1,0:T(8,128)(2,1)S(1)} %get-tuple-element.33.d0), channel_id=1, source_target_pairs={{0,1},{1,0},{2,3},{3,2},{4,5},{5,4},{6,7},{7,6},{8,9},{9,8},{10,11... | collective-permute-start | bytes 3932168 | tf_op jit(solution)/shard_map/ppermute | solution.py:316
  50.7 9.2 %collective-permute-start.10 = (bf16[4,80,384]{2,1,0:T(8,128)(2,1)S(1)}, bf16[4,80,384]{2,1,0:T(8,128)(2,1)S(1)}, u32[]{:S(2)}, u32[]{:S(2)}) collective-permute-start(bf16[4,80,384]{2,1,0:T(8,128)(2,1)S(1)} %get-tuple-element.35), channel_id=1, source_target_pairs={{0,4},{4,0},{8,12},{12,8},{2,6},{6,2},{10,14},{14,10},{1,5},{5,1},... | collective-permute-start | bytes 737288 | tf_op jit(solution)/shard_map/ppermute | solution.py:54
  60.0 13.0 %collective-permute-start.11 = (bf16[1,80,384]{2,1,0:T(8,128)(2,1)S(1)}, bf16[1,80,384]{2,1,0:T(8,128)(2,1)S(1)}, u32[]{:S(2)}, u32[]{:S(2)}) collective-permute-start(bf16[1,80,384]{2,1,0:T(8,128)(2,1)S(1)} %get-tuple-element.40), channel_id=1, source_target_pairs={{0,2},{4,6},{8,10},{12,14},{2,0},{6,4},{10,8},{14,12},{1,3},{5,7},... | collective-permute-start | bytes 184328 | tf_op jit(solution)/shard_map/ppermute | solution.py:54
  62.2 10.8 %collective-permute-start.12 = (bf16[1,80,384]{2,1,0:T(8,128)(2,1)S(1)}, bf16[1,80,384]{2,1,0:T(8,128)(2,1)S(1)}, u32[]{:S(2)}, u32[]{:S(2)}) collective-permute-start(bf16[1,80,384]{2,1,0:T(8,128)(2,1)S(1)} %get-tuple-element.41), channel_id=1, source_target_pairs={{0,8},{4,12},{8,0},{12,4},{2,10},{6,14},{10,2},{14,6},{1,9},{5,13}... | collective-permute-start | bytes 184328 | tf_op jit(solution)/shard_map/ppermute | solution.py:54
  67.1 6.1 %collective-permute-start.13 = (bf16[1,80,384]{2,1,0:T(8,128)(2,1)S(1)}, bf16[1,80,384]{2,1,0:T(8,128)(2,1)S(1)}, u32[]{:S(2)}, u32[]{:S(2)}) collective-permute-start(bf16[1,80,384]{2,1,0:T(8,128)(2,1)S(1)} %get-tuple-element.42), channel_id=1, source_target_pairs={{0,10},{4,14},{8,2},{12,6},{2,8},{6,12},{10,0},{14,4},{1,11},{5,15... | collective-permute-start | bytes 184328 | tf_op jit(solution)/shard_map/ppermute | solution.py:54
  67.2 6.1 %copy-start = (bf16[4,80,128]{2,1,0:T(8,128)(2,1)S(1)}, bf16[4,80,128]{2,1,0:T(8,128)(2,1)}, u32[]{:S(2)}) copy-start(bf16[4,80,128]{2,1,0:T(8,128)(2,1)} %get-tuple-element.26.sel_ref) | copy-start | bytes 245764

commit v4 on v3

--- a/solution.py
+++ b/solution.py
@@ -134,7 +134,8 @@
     )(array, *after)
 
 
-def forward_kernel(plan, half, block, *refs):
+def forward_kernel(plan, half, after, block, *refs):
+    refs = refs[after:]
     part_ref = refs[-1]
     if half is None:
         rows_ref, w_ref = refs[:2]
@@ -156,37 +157,59 @@
         part_ref[:, cols] = jnp.dot(rows_ref[...], w_ref[:, cols], preferred_element_type=F32).astype(BF16)
 
 
-def forward(plan, rows_in, half, w, name, wanted=512):
+def forward(plan, rows_in, half, w, after, name, wanted=512):
     width, columns = w.shape
     block = block_of(columns, wanted)
     fresh = half is not None
     outs = [jax.ShapeDtypeStruct((plan.rows, width), BF16)] * fresh
     outs.append(jax.ShapeDtypeStruct((plan.rows, columns), BF16))
     return pl.pallas_call(
-        functools.partial(forward_kernel, plan, half, block),
+        functools.partial(forward_kernel, plan, half, len(after), block),
         out_shape=outs,
-        in_specs=[VMEM] * (1 + len(rows_in)),
+        in_specs=[ANY] * len(after) + [VMEM] * (1 + len(rows_in)),
         out_specs=[VMEM] * len(outs),
         compiler_params=params(4),
-        cost_estimate=cost(2 * plan.rows * width * columns, 8 * 1024 * 1024),
+        cost_estimate=cost(2 * plan.rows * width * columns // 1, 8 * 1024 * 1024 // 1),
         name=name,
-    )(*rows_in, w)
-
-
-def rows_kernel(plan, g0, g1, u0, u1, d0, d1, wg_ref, wu_ref, h_ref, dg_ref, du_ref, *rest):
+    )(*after, *rows_in, w)
+
+
+def act_kernel(block, g0, g1, u0, u1, h_ref, by_gate_ref, by_up_ref):
+    for start in range(0, g0.shape[1], block):
+        cols = pl.ds(start, block)
+        gate = g0[:, cols].astype(F32) + g1[:, cols].astype(F32)
+        up = u0[:, cols].astype(F32) + u1[:, cols].astype(F32)
+        sigma = jax.nn.sigmoid(gate)
+        act = sigma * gate
+        h_ref[:, cols] = (act * up).astype(BF16)
+        by_gate_ref[:, cols] = (up * sigma * (1.0 + gate * (1.0 - sigma))).astype(BF16)
+        by_up_ref[:, cols] = act.astype(BF16)
+
+
+def activations(parts, wanted=256):
+    rows, columns = parts[0].shape
+    return pl.pallas_call(
+        functools.partial(act_kernel, block_of(columns, wanted)),
+        out_shape=[jax.ShapeDtypeStruct((rows, columns), BF16)] * 3,
+        in_specs=[VMEM] * 4,
+        out_specs=[VMEM] * 3,
+        compiler_params=params(4),
+        cost_estimate=cost(9000 * rows * columns, 14 * rows * columns),
+        name="activations",
+    )(*parts)
+
+
+def rows_kernel(plan, by_gate_ref, by_up_ref, d0, d1, wg_ref, wu_ref, dg_ref, du_ref, *rest):
     outs, total = rest[:-1], rest[-1]
-    gate = g0[...].astype(F32) + g1[...].astype(F32)
-    up = u0[...].astype(F32) + u1[...].astype(F32)
     hidden = d0[...].astype(F32) + d1[...].astype(F32)
-    sigma = jax.nn.sigmoid(gate)
-    act = sigma * gate
-    h_ref[...] = (act * up).astype(BF16)
-    d_gate = (hidden * up * sigma * (1.0 + gate * (1.0 - sigma))).astype(BF16)
-    d_up = (hidden * act).astype(BF16)
+    d_gate = (hidden * by_gate_ref[...].astype(F32)).astype(BF16)
+    d_up = (hidden * by_up_ref[...].astype(F32)).astype(BF16)
     dg_ref[...] = d_gate
     du_ref[...] = d_up
-    term = lax.dot_general(wg_ref[...], d_gate, TURNED, preferred_element_type=F32)
-    term = term + lax.dot_general(wu_ref[...], d_up, TURNED, preferred_element_type=F32)
+    step, block = pl.program_id(0), d_gate.shape[1]
+    cols = pl.ds(pl.multiple_of(step * block, block), block)
+    term = lax.dot_general(wg_ref[:, cols], d_gate, TURNED, preferred_element_type=F32)
+    term = term + lax.dot_general(wu_ref[:, cols], d_up, TURNED, preferred_element_type=F32)
     step = pl.program_id(0)
 
     @pl.when(step == 0)
@@ -212,7 +235,7 @@
     width, columns = wg.shape
     narrow = width // plan.replicas
     block = block_of(columns, wanted)
-    strip = pl.BlockSpec((width, block), lambda i: (0, i))
+    strip = VMEM
     part_spec = pl.BlockSpec((plan.rows, block), lambda i: (0, i))
     sets = 2 if plan.hops else 1
     pieces = jax.ShapeDtypeStruct((plan.devices // sets, CAP, narrow), BF16)
@@ -220,15 +243,15 @@
     outs = pl.pallas_call(
         functools.partial(rows_kernel, plan),
         grid=(columns // block,),
-        out_shape=[hidden] * 3 + [pieces] * sets,
-        in_specs=[part_spec] * 6 + [strip] * 2,
-        out_specs=[part_spec] * 3 + [pl.BlockSpec(pieces.shape, lambda i: (0, 0, 0))] * sets,
+        out_shape=[hidden] * 2 + [pieces] * sets,
+        in_specs=[part_spec] * 4 + [strip] * 2,
+        out_specs=[part_spec] * 2 + [pl.BlockSpec(pieces.shape, lambda i: (0, 0, 0))] * sets,
         scratch_shapes=[pltpu.VMEM((width, plan.rows), F32)],
-        compiler_params=params(32),
+        compiler_params=params(14),
         cost_estimate=cost(4 * plan.rows * width * columns, 4 * width * columns),
         name="row_grads",
     )(*parts, wg, wu)
-    return outs[:3], outs[3:]
+    return outs[:2], outs[2:]
 
 
 def weights_kernel(factor, block, many, *refs):
@@ -318,8 +341,8 @@
     sel, sends = dispatch(plan, expert_ids, gate_values, tokens, cotangent)
     if plan.hops:
         own, to_x, to_z, to_xz = sends
-        own = window(own, (), 4 * wg.size, "window_own")
-        to_x = window(to_x, (own,), 8 * wg.size, "window_side")
+        to_x = window(to_x, (), 4 * wg.size, "window_first")
+        to_x = window(to_x, (), 8 * wg.size, "window_second")
         far_own, far_x = plan.send(to_z, 0, 2), plan.send(to_xz, 1, 2)
         near_own, near_x = plan.send(own, 0, 1), plan.send(to_x, 1, 1)
         from_x = plan.send(to_x, 1, 0)
@@ -327,15 +350,16 @@
         got = [own, from_x, near_own, near_x, far_own, far_x, last_own, last_x]
     else:
         got = [plan.scatter(sends[0])]
-    q_full, part_h = forward(plan, got, 1, wd, "forward_h")
+    x_full, part_g = forward(plan, got, 0, wg, (), "forward_g")
+    other_g = swap(part_g)
+    (part_u,) = forward(plan, [x_full], None, wu, (), "forward_u")
+    other_u = swap(part_u)
+    q_full, part_h = forward(plan, got, 1, wd, (other_g,), "forward_h")
     other_h = swap(part_h)
-    x_full, part_g = forward(plan, got, 0, wg, "forward_g")
-    other_g = swap(part_g)
-    (part_u,) = forward(plan, [x_full], None, wu, "forward_u")
-    other_u = swap(part_u)
-    parts = (part_g, other_g, part_u, other_u, part_h, other_h)
+    h, by_gate, by_up = activations((part_g, other_g, part_u, other_u))
+    parts = (by_gate, by_up, part_h, other_h)
     factor = 1.0 / math.sqrt(tokens.shape[0] * plan.owners)
-    (h, d_gate, d_up), pieces = row_grads(plan, parts, wg, wu)
+    (d_gate, d_up), pieces = row_grads(plan, parts, wg, wu)
     arrived = plan.send(pieces[1], 0, 1) if plan.hops else plan.scatter(pieces[0])
     grad_gate, grad_up, done = weight_grads(factor, ((x_full, d_gate), (x_full, d_up)), pieces[0], "grads_gu")
     if plan.hops:

time: 74.4 us -> 68.9 us (0.926)
  Pallas kernels: 37.9 us -> 35.6 us
  waiting for transfers between devices: 16.6 us -> 14.6 us
  local copies, waits for them, and re-layouts: 1.82 us -> 0.99 us
    pallas_call x1, Pallas kernels: 13.1 us -> 8.99 us  [row_grads(): pl.pallas_call(functools.partial(rows_kernel, plan), grid=(columns // blo...]
    ppermute x3, waiting for transfers between devices: 3.87 us -> 1.45 us  [swap(): return lax.ppermute(part, 'tensor', [(i, i ^ 1) for i in range(size)])]
    pallas_call x3 -> x4, Pallas kernels: 6.69 us -> 8.45 us  [the longest x3 6.78 us: forward(): pl.pallas_call(functools.partial(forward_kernel, plan, half, len(after),...]
    unnamed x24 -> x30, local copies, waits for them, and re-layouts: 1.82 us -> 0.99 us
  transfers between devices with their start and end apart: 14 -> 14, of which waited for: 10 -> 9; matrix products, arithmetic and copies ran while one was open for 0% -> 0% of each run, Pallas kernels for 23% -> 31%
where the time goes in v4:
time: 68.9 us; the launch traced here: 68.7 us
  Pallas kernels  35.6 us (52%)
  starting transfers between devices  16.7 us (24%)
  waiting for transfers between devices  14.6 us (21%)
  local copies, waits for them, and re-layouts  0.99 us (1%)
  between operations  0.92 us (1%)
    ppermute x11, starting transfers between devices, send(): return lax.ppermute(array, ('dp', 'expert'), pairs)  15.9 us
    pallas_call x2, Pallas kernels, weight_grads(): pl.pallas_call(functools.partial(weights_kernel, factor, block, many), ou...  15 us
    ppermute x11, waiting for transfers between devices, send(): return lax.ppermute(array, ('dp', 'expert'), pairs)  13.1 us
    pallas_call x1, Pallas kernels, row_grads(): pl.pallas_call(functools.partial(rows_kernel, plan), grid=(columns // blo...  8.99 us
    pallas_call x3, Pallas kernels, forward(): pl.pallas_call(functools.partial(forward_kernel, plan, half, len(after),...  6.78 us
    pallas_call x1, Pallas kernels, dispatch(): pl.pallas_call(functools.partial(dispatch_kernel, plan), out_shape=[jax.S...  2.13 us
    pallas_call x1, Pallas kernels, activations(): pl.pallas_call(functools.partial(act_kernel, block_of(columns, wanted)),...  1.66 us
    ppermute x3, waiting for transfers between devices, swap(): return lax.ppermute(part, 'tensor', [(i, i ^ 1) for i in range(size)])  1.45 us
  transfers between devices with their start and end apart: 14, of which 9 were waited for; matrix products, arithmetic and copies ran while one was open for 0% of the time, Pallas kernels for 31%

profile of v4, /device:TPU:0, one launch (start us, length us, event | category | flops | bytes accessed | tf_op | source)
XLA Modules:
  0.0 68.7 jit_solution(2626585727191476762)
XLA Ops:
  0.6 2.1 %dispatch.1 = (bf16[4,80,128]{2,1,0:T(8,128)(2,1)}, bf16[1,160,384]{2,1,0:T(8,128)(2,1)}, bf16[1,160,384]{2,1,0:T(8,128)(2,1)}, bf16[1,160,384]{2,1,0:T(8,128)(2,1)}, bf16[1,160,384]{2,1,0:T(8,128)(2,1)}) custom-call(s32[2,128]{1,0:T(2,128)} %bitcast.10, bf16[2,128]{1,0:T(2,128)(2,1)} %bitcast.11, bf16[128,384]{1,0:T(8,128)(2,1)} %refs_2_.1, ...), custom_call_target="tpu_custom_call" | custom-call | tf_op jit(solution)/shard_map/dispatch/pallas_call | solution.py:109
  2.8 4.1 %collective-permute-start.3 = (bf16[1,160,384]{2,1,0:T(8,128)(2,1)}, bf16[1,160,384]{2,1,0:T(8,128)(2,1)S(1)}, u32[]{:S(2)}, u32[]{:S(2)}) collective-permute-start(bf16[1,160,384]{2,1,0:T(8,128)(2,1)} %get-tuple-element.31), channel_id=1, source_target_pairs={{0,8},{4,12},{8,0},{12,4},{2,10},{6,14},{10,2},{14,6},{1,9},{5,13}... | collective-permute-start | bytes 368648 | tf_op jit(solution)/shard_map/ppermute | solution.py:54
  6.9 1.3 %collective-permute-start.4 = (bf16[1,160,384]{2,1,0:T(8,128)(2,1)}, bf16[1,160,384]{2,1,0:T(8,128)(2,1)S(1)}, u32[]{:S(2)}, u32[]{:S(2)}) collective-permute-start(bf16[1,160,384]{2,1,0:T(8,128)(2,1)} %get-tuple-element.32), channel_id=1, source_target_pairs={{0,10},{4,14},{8,2},{12,6},{2,8},{6,12},{10,0},{14,4},{1,11},{5,15... | collective-permute-start | bytes 368648 | tf_op jit(solution)/shard_map/ppermute | solution.py:54
  8.1 0.9 %copy-done.2 = bf16[1,160,384]{2,1,0:T(8,128)(2,1)S(1)} copy-done((bf16[1,160,384]{2,1,0:T(8,128)(2,1)S(1)}, bf16[1,160,384]{2,1,0:T(8,128)(2,1)}, u32[]{:S(2)}) %copy-start.2) | copy-done | bytes 122904
  9.1 0.0 copy-start
  9.1 0.0 slice-start.1
  9.1 0.0 slice-start.2
  9.1 0.0 slice-start.4
  9.1 0.0 slice-start.5
  9.1 1.6 %collective-permute-start.2 = (bf16[1,160,384]{2,1,0:T(8,128)(2,1)S(1)}, bf16[1,160,384]{2,1,0:T(8,128)(2,1)S(1)}, u32[]{:S(2)}, u32[]{:S(2)}) collective-permute-start(bf16[1,160,384]{2,1,0:T(8,128)(2,1)S(1)} %window_second.1), channel_id=1, source_target_pairs={{0,6},{4,2},{8,14},{12,10},{2,4},{6,0},{10,12},{14,8},{1,7},{5,3},... | collective-permute-start | bytes 368648 | tf_op jit(solution)/shard_map/ppermute | solution.py:54
  10.8 1.5 %collective-permute-start = (bf16[1,160,384]{2,1,0:T(8,128)(2,1)S(1)}, bf16[1,160,384]{2,1,0:T(8,128)(2,1)S(1)}, u32[]{:S(2)}, u32[]{:S(2)}) collective-permute-start(bf16[1,160,384]{2,1,0:T(8,128)(2,1)S(1)} %window_second.1), channel_id=1, source_target_pairs={{0,2},{4,6},{8,10},{12,14},{2,0},{6,4},{10,8},{14,12},{1,3},{5,7},... | collective-permute-start | bytes 368648 | tf_op jit(solution)/shard_map/ppermute | solution.py:54
  12.2 0.0 copy-done
  12.2 0.4 collective-permute-start.1
  12.7 3.8 %collective-permute-done.3.refs_4_.refs_5_ = bf16[1,160,384]{2,1,0:T(8,128)(2,1)S(1)} collective-permute-done((bf16[1,160,384]{2,1,0:T(8,128)(2,1)}, bf16[1,160,384]{2,1,0:T(8,128)(2,1)S(1)}, u32[]{:S(2)}, u32[]{:S(2)}) %collective-permute-start.3) | collective-permute-done | bytes 122912 | tf_op jit(solution)/shard_map/ppermute | solution.py:54
  16.5 0.1 collective-permute-start.5
  16.6 2.7 %collective-permute-done.4.refs_5_.refs_6_ = bf16[1,160,384]{2,1,0:T(8,128)(2,1)S(1)} collective-permute-done((bf16[1,160,384]{2,1,0:T(8,128)(2,1)}, bf16[1,160,384]{2,1,0:T(8,128)(2,1)S(1)}, u32[]{:S(2)}, u32[]{:S(2)}) %collective-permute-start.4) | collective-permute-done | bytes 122912 | tf_op jit(solution)/shard_map/ppermute | solution.py:54
  19.3 0.0 collective-permute-start.6
  19.3 1.1 %collective-permute-done.2.refs_3_.refs_4_ = bf16[1,160,384]{2,1,0:T(8,128)(2,1)S(1)} collective-permute-done((bf16[1,160,384]{2,1,0:T(8,128)(2,1)S(1)}, bf16[1,160,384]{2,1,0:T(8,128)(2,1)S(1)}, u32[]{:S(2)}, u32[]{:S(2)}) %collective-permute-start.2) | collective-permute-done | bytes 122912 | tf_op jit(solution)/shard_map/ppermute | solution.py:54
  20.4 0.0 collective-permute-done.refs_1_.refs_2_
  20.5 0.7 %collective-permute-done.1.refs_2_.refs_3_ = bf16[1,160,384]{2,1,0:T(8,128)(2,1)S(1)} collective-permute-done((bf16[1,160,384]{2,1,0:T(8,128)(2,1)S(1)}, bf16[1,160,384]{2,1,0:T(8,128)(2,1)S(1)}, u32[]{:S(2)}, u32[]{:S(2)}) %collective-permute-start.1) | collective-permute-done | bytes 122912 | tf_op jit(solution)/shard_map/ppermute | solution.py:54
  21.2 2.6 %collective-permute-done.5.refs_6_.refs_7_ = bf16[1,160,384]{2,1,0:T(8,128)(2,1)S(1)} collective-permute-done((bf16[1,160,384]{2,1,0:T(8,128)(2,1)S(1)}, bf16[1,160,384]{2,1,0:T(8,128)(2,1)S(1)}, u32[]{:S(2)}, u32[]{:S(2)}) %collective-permute-start.5) | collective-permute-done | bytes 122912 | tf_op jit(solution)/shard_map/ppermute | solution.py:54
  23.8 1.9 %collective-permute-done.6.refs_7_.refs_8_ = bf16[1,160,384]{2,1,0:T(8,128)(2,1)S(1)} collective-permute-done((bf16[1,160,384]{2,1,0:T(8,128)(2,1)S(1)}, bf16[1,160,384]{2,1,0:T(8,128)(2,1)S(1)}, u32[]{:S(2)}, u32[]{:S(2)}) %collective-permute-start.6) | collective-permute-done | bytes 122912 | tf_op jit(solution)/shard_map/ppermute | solution.py:54
  25.7 0.0 slice-done
  25.7 0.0 slice-done.1
  25.7 0.0 slice-done.2
  25.7 0.0 slice-start.9
  25.7 0.0 slice-start.10
  25.7 2.2 %forward_g.1 = (bf16[160,1536]{1,0:T(8,128)(2,1)S(1)}, bf16[160,4096]{1,0:T(8,128)(2,1)S(1)}) custom-call(bf16[1,160,384]{2,1,0:T(8,128)(2,1)S(1)} %copy-done, bf16[1,160,384]{2,1,0:T(8,128)(2,1)S(1)} %collective-permute-done.refs_1_.refs_2_, bf16[1,160,384]{2,1,0:T(8,128)(2,1)S(1)} %collective-permute-done.1.refs_2_.refs_3_, ...), custom_call_target="tpu_custom_call" | custom-call | flops 2013265920 | bytes 8388608 | tf_op jit(solution)/shard_map/forward_g/pallas_call | solution.py:166
  28.0 0.1 collective-permute-start.7
  28.1 0.0 slice-done.3
  28.1 0.0 slice-done.4
  28.1 0.0 slice-done.5
  28.1 0.0 slice-start.11
  28.1 2.2 %forward_u.1.u0 = bf16[160,4096]{1,0:T(8,128)(2,1)S(1)} custom-call(bf16[160,1536]{1,0:T(8,128)(2,1)S(1)} %get-tuple-element.34.refs_0_.refs_2_, bf16[1536,4096]{1,0:T(8,128)(2,1)S(1)} %bitcast.5), custom_call_target="tpu_custom_call" | custom-call | flops 2013265920 | bytes 8388608 | tf_op jit(solution)/shard_map/forward_u/pallas_call | solution.py:166
  30.3 0.5 collective-permute-start.8
  30.9 0.2 collective-permute-done.7.g1.refs_0_
  31.1 0.0 slice-done.9
  31.1 0.0 slice-done.10
  31.1 0.0 slice-done.11
  31.1 0.0 slice-start.6
  31.1 0.0 slice-start.7
  31.1 2.3 %forward_h.1 = (bf16[160,1536]{1,0:T(8,128)(2,1)S(1)}, bf16[160,4096]{1,0:T(8,128)(2,1)S(1)}) custom-call(bf16[160,4096]{1,0:T(8,128)(2,1)S(1)} %collective-permute-done.7.g1.refs_0_, bf16[1,160,384]{2,1,0:T(8,128)(2,1)S(1)} %copy-done, bf16[1,160,384]{2,1,0:T(8,128)(2,1)S(1)} %collective-permute-done.refs_1_.refs_2_, ...), custom_call_target="tpu_custom_call" | custom-call | flops 2013265920 | bytes 8388608 | tf_op jit(solution)/shard_map/forward_h/pallas_call | solution.py:166
  33.5 0.0 slice-start.8
  33.5 0.2 collective-permute-start.9
  33.7 0.0 collective-permute-done.8.u1
  33.7 1.7 %activations.1 = (bf16[160,4096]{1,0:T(8,128)(2,1)S(1)}, bf16[160,4096]{1,0:T(8,128)(2,1)S(1)}, bf16[160,4096]{1,0:T(8,128)(2,1)S(1)}) custom-call(bf16[160,4096]{1,0:T(8,128)(2,1)S(1)} %get-tuple-element.33.g0, bf16[160,4096]{1,0:T(8,128)(2,1)S(1)} %collective-permute-done.7.g1.refs_0_, bf16[160,4096]{1,0:T(8,128)(2,1)S(1)} %forward_u.1.u0, ...), custom_call_target="tpu_custom_call" | custom-call | flops 5898240000 | bytes 9175040 | tf_op jit(solution)/shard_map/activations/pallas_call | solution.py:191
  35.4 1.2 %collective-permute-done.9.d1 = bf16[160,4096]{1,0:T(8,128)(2,1)S(1)} collective-permute-done((bf16[160,4096]{1,0:T(8,128)(2,1)S(1)}, bf16[160,4096]{1,0:T(8,128)(2,1)S(1)}, u32[]{:S(2)}, u32[]{:S(2)}) %collective-permute-start.9) | collective-permute-done | bytes 1310752 | tf_op jit(solution)/shard_map/ppermute | solution.py:339
  36.6 0.0 slice-done.6
  36.6 0.0 slice-done.7
  36.6 0.0 slice-done.8
  36.6 9.0 %row_grads.1 = (bf16[160,4096]{1,0:T(8,128)(2,1)S(1)}, bf16[160,4096]{1,0:T(8,128)(2,1)S(1)}, bf16[4,80,384]{2,1,0:T(8,128)(2,1)S(1)}, bf16[4,80,384]{2,1,0:T(8,128)(2,1)S(1)}) custom-call(bf16[160,4096]{1,0:T(8,128)(2,1)S(1)} %get-tuple-element.35.by_gate_ref, bf16[160,4096]{1,0:T(8,128)(2,1)S(1)} %get-tuple-element.36.by_up_ref, ...), custom_call_target="tpu_custom_call" | custom-call | flops 4026531840 | bytes 25165824 | tf_op jit(solution)/shard_map/row_grads/pallas_call | solution.py:243
  45.6 0.1 collective-permute-start.10
  45.7 9.1 %grads_gu.1 = (bf16[1536,4096]{1,0:T(8,128)(2,1)}, bf16[1536,4096]{1,0:T(8,128)(2,1)}, f32[8,128]{1,0:T(8,128)S(1)}) custom-call(bf16[160,1536]{1,0:T(8,128)(2,1)S(1)} %get-tuple-element.34.refs_0_.refs_2_, bf16[160,4096]{1,0:T(8,128)(2,1)S(1)} %get-tuple-element.40.refs_1_, bf16[160,1536]{1,0:T(8,128)(2,1)S(1)} %get-tuple-element.34.refs_0_.refs_2_, ...), custom_call_target="tpu_custom_call" | custom-call | flops 4026531840 | bytes 25165824 | tf_op jit(solution)/shard_map/grads_gu/pallas_call | solution.py:278
  54.8 0.0 collective-permute-done.10.got_ref
  54.8 0.1 pair_sum.1
  54.9 1.8 %collective-permute-start.11 = (bf16[1,80,384]{2,1,0:T(8,128)(2,1)S(1)}, bf16[1,80,384]{2,1,0:T(8,128)(2,1)S(1)}, u32[]{:S(2)}, u32[]{:S(2)}) collective-permute-start(bf16[1,80,384]{2,1,0:T(8,128)(2,1)S(1)} %get-tuple-element.44), channel_id=1, source_target_pairs={{0,2},{4,6},{8,10},{12,14},{2,0},{6,4},{10,8},{14,12},{1,3},{5,7},... | collective-permute-start | bytes 184328 | tf_op jit(solution)/shard_map/ppermute | solution.py:54
  56.8 4.9 %collective-permute-start.12 = (bf16[1,80,384]{2,1,0:T(8,128)(2,1)S(1)}, bf16[1,80,384]{2,1,0:T(8,128)(2,1)S(1)}, u32[]{:S(2)}, u32[]{:S(2)}) collective-permute-start(bf16[1,80,384]{2,1,0:T(8,128)(2,1)S(1)} %get-tuple-element.45), channel_id=1, source_target_pairs={{0,8},{4,12},{8,0},{12,4},{2,10},{6,14},{10,2},{14,6},{1,9},{5,13}... | collective-permute-start | bytes 184328 | tf_op jit(solution)/shard_map/ppermute | solution.py:54
  61.7 0.0 collective-permute-start.13
  61.7 5.9 %grad_down.1 = (bf16[1536,4096]{1,0:T(8,128)(2,1)}, f32[8,128]{1,0:T(8,128)}) custom-call(bf16[160,1536]{1,0:T(8,128)(2,1)S(1)} %get-tuple-element.49.refs_0_, bf16[160,4096]{1,0:T(8,128)(2,1)S(1)} %get-tuple-element.50.refs_1_, bf16[1,80,384]{2,1,0:T(8,128)(2,1)S(1)} %get-tuple-element.43.refs_0_.refs_2_), custom_call_target="tpu_custom_call" | custom-call | flops 2013265920 | bytes 12582912 | tf_op jit(solution)/shard_map/grad_down/pallas_call | solution.py:278
  67.5 0.0 collective-permute-done.11.refs_1_
  67.5 0.0 collective-permute-done.12.refs_2_
  67.6 0.2 collective-permute-done.13.refs_3_
  67.8 0.0 copy-done.1
  67.8 0.9 %combine.1 = bf16[128,384]{1,0:T(8,128)(2,1)} custom-call(bf16[4,80,128]{2,1,0:T(8,128)(2,1)S(1)} %copy-done.1, bf16[1,80,384]{2,1,0:T(8,128)(2,1)S(1)} %get-tuple-element.43.refs_0_.refs_2_, bf16[1,80,384]{2,1,0:T(8,128)(2,1)S(1)} %collective-permute-done.11.refs_1_, bf16[1,80,384]{2,1,0:T(8,128)(2,1)S(1)} %collective-permute-done.12.refs_2_, ...), custom_call_target="tpu_custom_call" | custom-call | tf_op jit(solution)/shard_map/combine/pallas_call | solution.py:323
  (10 shorter events, 0.0 us)
Async XLA Ops:
  2.8 13.7 %collective-permute-start.3 = (bf16[1,160,384]{2,1,0:T(8,128)(2,1)}, bf16[1,160,384]{2,1,0:T(8,128)(2,1)S(1)}, u32[]{:S(2)}, u32[]{:S(2)}) collective-permute-start(bf16[1,160,384]{2,1,0:T(8,128)(2,1)} %get-tuple-element.31), channel_id=1, source_target_pairs={{0,8},{4,12},{8,0},{12,4},{2,10},{6,14},{10,2},{14,6},{1,9},{5,13}... | collective-permute-start | bytes 368648 | tf_op jit(solution)/shard_map/ppermute | solution.py:54
  6.9 12.4 %collective-permute-start.4 = (bf16[1,160,384]{2,1,0:T(8,128)(2,1)}, bf16[1,160,384]{2,1,0:T(8,128)(2,1)S(1)}, u32[]{:S(2)}, u32[]{:S(2)}) collective-permute-start(bf16[1,160,384]{2,1,0:T(8,128)(2,1)} %get-tuple-element.32), channel_id=1, source_target_pairs={{0,10},{4,14},{8,2},{12,6},{2,8},{6,12},{10,0},{14,4},{1,11},{5,15... | collective-permute-start | bytes 368648 | tf_op jit(solution)/shard_map/ppermute | solution.py:54
  8.1 0.9 %copy-start.2 = (bf16[1,160,384]{2,1,0:T(8,128)(2,1)S(1)}, bf16[1,160,384]{2,1,0:T(8,128)(2,1)}, u32[]{:S(2)}) copy-start(bf16[1,160,384]{2,1,0:T(8,128)(2,1)} %get-tuple-element.30.array_ref) | copy-start | bytes 368644
  9.0 16.7 %slice-start = ((s8[12582912]{0:T(1024)(128)(4,1)}), s8[4194304]{0:T(1024)(128)(4,1)S(1)}, s32[]{:S(2)}) async-start(s8[12582912]{0:T(1024)(128)(4,1)} %bitcast.2), calls=%async_computation | async-start | bytes 8388608
  9.0 19.0 %slice-start.3 = ((s8[12582912]{0:T(1024)(128)(4,1)}), s8[4194304]{0:T(1024)(128)(4,1)S(1)}, s32[]{:S(2)}) async-start(s8[12582912]{0:T(1024)(128)(4,1)} %bitcast.4), calls=%async_computation.3 | async-start | bytes 8388608
  9.1 3.2 %copy-start = (bf16[1,160,384]{2,1,0:T(8,128)(2,1)S(1)}, bf16[1,160,384]{2,1,0:T(8,128)(2,1)}, u32[]{:S(2)}) copy-start(bf16[1,160,384]{2,1,0:T(8,128)(2,1)} %get-tuple-element.29.refs_0_.refs_1_) | copy-start | bytes 368644
  9.1 16.6 %slice-start.1 = ((s8[12582912]{0:T(1024)(128)(4,1)}), s8[4194304]{0:T(1024)(128)(4,1)S(1)}, s32[]{:S(2)}) async-start(s8[12582912]{0:T(1024)(128)(4,1)} %bitcast.2), calls=%async_computation.1 | async-start | bytes 8388608
  9.1 16.6 %slice-start.2 = ((s8[12582912]{0:T(1024)(128)(4,1)}), s8[4194304]{0:T(1024)(128)(4,1)S(1)}, s32[]{:S(2)}) async-start(s8[12582912]{0:T(1024)(128)(4,1)} %bitcast.2), calls=%async_computation.2 | async-start | bytes 8388608
  9.1 19.0 %slice-start.4 = ((s8[12582912]{0:T(1024)(128)(4,1)}), s8[4194304]{0:T(1024)(128)(4,1)S(1)}, s32[]{:S(2)}) async-start(s8[12582912]{0:T(1024)(128)(4,1)} %bitcast.4), calls=%async_computation.4 | async-start | bytes 8388608
  9.1 19.0 %slice-start.5 = ((s8[12582912]{0:T(1024)(128)(4,1)}), s8[4194304]{0:T(1024)(128)(4,1)S(1)}, s32[]{:S(2)}) async-start(s8[12582912]{0:T(1024)(128)(4,1)} %bitcast.4), calls=%async_computation.5 | async-start | bytes 8388608
  9.1 11.3 %collective-permute-start.2 = (bf16[1,160,384]{2,1,0:T(8,128)(2,1)S(1)}, bf16[1,160,384]{2,1,0:T(8,128)(2,1)S(1)}, u32[]{:S(2)}, u32[]{:S(2)}) collective-permute-start(bf16[1,160,384]{2,1,0:T(8,128)(2,1)S(1)} %window_second.1), channel_id=1, source_target_pairs={{0,6},{4,2},{8,14},{12,10},{2,4},{6,0},{10,12},{14,8},{1,7},{5,3},... | collective-permute-start | bytes 368648 | tf_op jit(solution)/shard_map/ppermute | solution.py:54
  10.8 9.7 %collective-permute-start = (bf16[1,160,384]{2,1,0:T(8,128)(2,1)S(1)}, bf16[1,160,384]{2,1,0:T(8,128)(2,1)S(1)}, u32[]{:S(2)}, u32[]{:S(2)}) collective-permute-start(bf16[1,160,384]{2,1,0:T(8,128)(2,1)S(1)} %window_second.1), channel_id=1, source_target_pairs={{0,2},{4,6},{8,10},{12,14},{2,0},{6,4},{10,8},{14,12},{1,3},{5,7},... | collective-permute-start | bytes 368648 | tf_op jit(solution)/shard_map/ppermute | solution.py:54
  12.2 8.9 %collective-permute-start.1 = (bf16[1,160,384]{2,1,0:T(8,128)(2,1)S(1)}, bf16[1,160,384]{2,1,0:T(8,128)(2,1)S(1)}, u32[]{:S(2)}, u32[]{:S(2)}) collective-permute-start(bf16[1,160,384]{2,1,0:T(8,128)(2,1)S(1)} %copy-done), channel_id=1, source_target_pairs={{0,4},{4,0},{8,12},{12,8},{2,6},{6,2},{10,14},{14,10},{1,5},{5,1},... | collective-permute-start | bytes 368648 | tf_op jit(solution)/shard_map/ppermute | solution.py:54
  16.5 7.3 %collective-permute-start.5 = (bf16[1,160,384]{2,1,0:T(8,128)(2,1)S(1)}, bf16[1,160,384]{2,1,0:T(8,128)(2,1)S(1)}, u32[]{:S(2)}, u32[]{:S(2)}) collective-permute-start(bf16[1,160,384]{2,1,0:T(8,128)(2,1)S(1)} %collective-permute-done.3.refs_4_.refs_5_), channel_id=1, source_target_pairs={{0,4},{4,0},{8,12},{12,8},{2,6},{6,2},{10,14},{14,10},{1,5},{5,1},... | collective-permute-start | bytes 368648 | tf_op jit(solution)/shard_map/ppermute | solution.py:54
  19.3 6.4 %collective-permute-start.6 = (bf16[1,160,384]{2,1,0:T(8,128)(2,1)S(1)}, bf16[1,160,384]{2,1,0:T(8,128)(2,1)S(1)}, u32[]{:S(2)}, u32[]{:S(2)}) collective-permute-start(bf16[1,160,384]{2,1,0:T(8,128)(2,1)S(1)} %collective-permute-done.4.refs_5_.refs_6_), channel_id=1, source_target_pairs={{0,4},{4,0},{8,12},{12,8},{2,6},{6,2},{10,14},{14,10},{1,5},{5,1},... | collective-permute-start | bytes 368648 | tf_op jit(solution)/shard_map/ppermute | solution.py:54
  25.7 5.4 %slice-start.9 = ((s8[12582912]{0:T(1024)(128)(4,1)}), s8[4194304]{0:T(1024)(128)(4,1)S(1)}, s32[]{:S(2)}) async-start(s8[12582912]{0:T(1024)(128)(4,1)} %bitcast.8), calls=%async_computation.9 | async-start | bytes 8388608
  25.7 5.4 %slice-start.10 = ((s8[12582912]{0:T(1024)(128)(4,1)}), s8[4194304]{0:T(1024)(128)(4,1)S(1)}, s32[]{:S(2)}) async-start(s8[12582912]{0:T(1024)(128)(4,1)} %bitcast.8), calls=%async_computation.10 | async-start | bytes 8388608
  28.0 3.1 %collective-permute-start.7 = (bf16[160,4096]{1,0:T(8,128)(2,1)S(1)}, bf16[160,4096]{1,0:T(8,128)(2,1)S(1)}, u32[]{:S(2)}, u32[]{:S(2)}) collective-permute-start(bf16[160,4096]{1,0:T(8,128)(2,1)S(1)} %get-tuple-element.33.g0), channel_id=1, source_target_pairs={{0,1},{1,0},{2,3},{3,2},{4,5},{5,4},{6,7},{7,6},{8,9},{9,8},{10,11... | collective-permute-start | bytes 3932168 | tf_op jit(solution)/shard_map/ppermute | solution.py:339
  28.1 3.0 %slice-start.11 = ((s8[12582912]{0:T(1024)(128)(4,1)}), s8[4194304]{0:T(1024)(128)(4,1)S(1)}, s32[]{:S(2)}) async-start(s8[12582912]{0:T(1024)(128)(4,1)} %bitcast.8), calls=%async_computation.11 | async-start | bytes 8388608
  30.3 3.4 %collective-permute-start.8 = (bf16[160,4096]{1,0:T(8,128)(2,1)S(1)}, bf16[160,4096]{1,0:T(8,128)(2,1)S(1)}, u32[]{:S(2)}, u32[]{:S(2)}) collective-permute-start(bf16[160,4096]{1,0:T(8,128)(2,1)S(1)} %forward_u.1.u0), channel_id=1, source_target_pairs={{0,1},{1,0},{2,3},{3,2},{4,5},{5,4},{6,7},{7,6},{8,9},{9,8},{10,11... | collective-permute-start | bytes 3932168 | tf_op jit(solution)/shard_map/ppermute | solution.py:339
  31.1 5.5 %slice-start.6 = ((s8[12582912]{0:T(1024)(128)(4,1)}), s8[4194304]{0:T(1024)(128)(4,1)S(1)}, s32[]{:S(2)}) async-start(s8[12582912]{0:T(1024)(128)(4,1)} %bitcast.6), calls=%async_computation.6 | async-start | bytes 8388608
  31.1 5.5 %slice-start.7 = ((s8[12582912]{0:T(1024)(128)(4,1)}), s8[4194304]{0:T(1024)(128)(4,1)S(1)}, s32[]{:S(2)}) async-start(s8[12582912]{0:T(1024)(128)(4,1)} %bitcast.6), calls=%async_computation.7 | async-start | bytes 8388608
  33.5 3.1 %slice-start.8 = ((s8[12582912]{0:T(1024)(128)(4,1)}), s8[4194304]{0:T(1024)(128)(4,1)S(1)}, s32[]{:S(2)}) async-start(s8[12582912]{0:T(1024)(128)(4,1)} %bitcast.6), calls=%async_computation.8 | async-start | bytes 8388608
  33.5 3.1 %collective-permute-start.9 = (bf16[160,4096]{1,0:T(8,128)(2,1)S(1)}, bf16[160,4096]{1,0:T(8,128)(2,1)S(1)}, u32[]{:S(2)}, u32[]{:S(2)}) collective-permute-start(bf16[160,4096]{1,0:T(8,128)(2,1)S(1)} %get-tuple-element.37.d0), channel_id=1, source_target_pairs={{0,1},{1,0},{2,3},{3,2},{4,5},{5,4},{6,7},{7,6},{8,9},{9,8},{10,11... | collective-permute-start | bytes 3932168 | tf_op jit(solution)/shard_map/ppermute | solution.py:339
  45.6 9.2 %collective-permute-start.10 = (bf16[4,80,384]{2,1,0:T(8,128)(2,1)S(1)}, bf16[4,80,384]{2,1,0:T(8,128)(2,1)S(1)}, u32[]{:S(2)}, u32[]{:S(2)}) collective-permute-start(bf16[4,80,384]{2,1,0:T(8,128)(2,1)S(1)} %get-tuple-element.39), channel_id=1, source_target_pairs={{0,4},{4,0},{8,12},{12,8},{2,6},{6,2},{10,14},{14,10},{1,5},{5,1},... | collective-permute-start | bytes 737288 | tf_op jit(solution)/shard_map/ppermute | solution.py:54
  54.9 12.6 %collective-permute-start.11 = (bf16[1,80,384]{2,1,0:T(8,128)(2,1)S(1)}, bf16[1,80,384]{2,1,0:T(8,128)(2,1)S(1)}, u32[]{:S(2)}, u32[]{:S(2)}) collective-permute-start(bf16[1,80,384]{2,1,0:T(8,128)(2,1)S(1)} %get-tuple-element.44), channel_id=1, source_target_pairs={{0,2},{4,6},{8,10},{12,14},{2,0},{6,4},{10,8},{14,12},{1,3},{5,7},... | collective-permute-start | bytes 184328 | tf_op jit(solution)/shard_map/ppermute | solution.py:54
  56.8 10.8 %collective-permute-start.12 = (bf16[1,80,384]{2,1,0:T(8,128)(2,1)S(1)}, bf16[1,80,384]{2,1,0:T(8,128)(2,1)S(1)}, u32[]{:S(2)}, u32[]{:S(2)}) collective-permute-start(bf16[1,80,384]{2,1,0:T(8,128)(2,1)S(1)} %get-tuple-element.45), channel_id=1, source_target_pairs={{0,8},{4,12},{8,0},{12,4},{2,10},{6,14},{10,2},{14,6},{1,9},{5,13}... | collective-permute-start | bytes 184328 | tf_op jit(solution)/shard_map/ppermute | solution.py:54
  61.7 6.1 %collective-permute-start.13 = (bf16[1,80,384]{2,1,0:T(8,128)(2,1)S(1)}, bf16[1,80,384]{2,1,0:T(8,128)(2,1)S(1)}, u32[]{:S(2)}, u32[]{:S(2)}) collective-permute-start(bf16[1,80,384]{2,1,0:T(8,128)(2,1)S(1)} %get-tuple-element.46), channel_id=1, source_target_pairs={{0,10},{4,14},{8,2},{12,6},{2,8},{6,12},{10,0},{14,4},{1,11},{5,15... | collective-permute-start | bytes 184328 | tf_op jit(solution)/shard_map/ppermute | solution.py:54
  61.7 6.1 %copy-start.1 = (bf16[4,80,128]{2,1,0:T(8,128)(2,1)S(1)}, bf16[4,80,128]{2,1,0:T(8,128)(2,1)}, u32[]{:S(2)}) copy-start(bf16[4,80,128]{2,1,0:T(8,128)(2,1)} %get-tuple-element.28.sel_ref) | copy-start | bytes 245764

commit v5 on v4

--- a/solution.py
+++ b/solution.py
@@ -199,55 +199,40 @@
     )(*parts)
 
 
-def rows_kernel(plan, by_gate_ref, by_up_ref, d0, d1, wg_ref, wu_ref, dg_ref, du_ref, *rest):
+def rows_kernel(plan, block, by_gate_ref, by_up_ref, d0, d1, wg_ref, wu_ref, dg_ref, du_ref, *rest):
     outs, total = rest[:-1], rest[-1]
-    hidden = d0[...].astype(F32) + d1[...].astype(F32)
-    d_gate = (hidden * by_gate_ref[...].astype(F32)).astype(BF16)
-    d_up = (hidden * by_up_ref[...].astype(F32)).astype(BF16)
-    dg_ref[...] = d_gate
-    du_ref[...] = d_up
-    step, block = pl.program_id(0), d_gate.shape[1]
-    cols = pl.ds(pl.multiple_of(step * block, block), block)
-    term = lax.dot_general(wg_ref[:, cols], d_gate, TURNED, preferred_element_type=F32)
-    term = term + lax.dot_general(wu_ref[:, cols], d_up, TURNED, preferred_element_type=F32)
-    step = pl.program_id(0)
-
-    @pl.when(step == 0)
-    def _():
-        total[...] = term
-
-    @pl.when(step > 0)
-    def _():
-        total[...] += term
-
-    @pl.when(step == pl.num_programs(0) - 1)
-    def _():
-        narrow = outs[0].shape[2]
-        for z in range(plan.replicas):
-            index = jnp.bitwise_xor(lax.axis_index("dp"), z) if plan.hops else z
-            turned = total[pl.ds(pl.multiple_of(index * narrow, 32), narrow), :].T.astype(BF16)
-            for x in range(plan.owners):
-                at = z // 2 * plan.owners + x if plan.hops else z * plan.owners + x
-                outs[z % len(outs)][at] = turned[x * CAP : (x + 1) * CAP, :]
-
-
-def row_grads(plan, parts, wg, wu, wanted=1024):
+    for start in range(0, wg_ref.shape[1], block):
+        cols = pl.ds(start, block)
+        hidden = d0[:, cols].astype(F32) + d1[:, cols].astype(F32)
+        d_gate = (hidden * by_gate_ref[:, cols].astype(F32)).astype(BF16)
+        d_up = (hidden * by_up_ref[:, cols].astype(F32)).astype(BF16)
+        dg_ref[:, cols] = d_gate
+        du_ref[:, cols] = d_up
+        term = lax.dot_general(wg_ref[:, cols], d_gate, TURNED, preferred_element_type=F32)
+        term = term + lax.dot_general(wu_ref[:, cols], d_up, TURNED, preferred_element_type=F32)
+        total[...] = term if start == 0 else total[...] + term
+    narrow = outs[0].shape[2]
+    for z in range(plan.replicas):
+        index = jnp.bitwise_xor(lax.axis_index("dp"), z) if plan.hops else z
+        turned = total[pl.ds(pl.multiple_of(index * narrow, 32), narrow), :].T.astype(BF16)
+        for x in range(plan.owners):
+            at = z // 2 * plan.owners + x if plan.hops else z * plan.owners + x
+            outs[z % len(outs)][at] = turned[x * CAP : (x + 1) * CAP, :]
+
+
+def row_grads(plan, parts, wg, wu, wanted=2048):
     width, columns = wg.shape
     narrow = width // plan.replicas
-    block = block_of(columns, wanted)
-    strip = VMEM
-    part_spec = pl.BlockSpec((plan.rows, block), lambda i: (0, i))
     sets = 2 if plan.hops else 1
     pieces = jax.ShapeDtypeStruct((plan.devices // sets, CAP, narrow), BF16)
     hidden = jax.ShapeDtypeStruct((plan.rows, columns), BF16)
     outs = pl.pallas_call(
-        functools.partial(rows_kernel, plan),
-        grid=(columns // block,),
+        functools.partial(rows_kernel, plan, block_of(columns, wanted)),
         out_shape=[hidden] * 2 + [pieces] * sets,
-        in_specs=[part_spec] * 4 + [strip] * 2,
-        out_specs=[part_spec] * 2 + [pl.BlockSpec(pieces.shape, lambda i: (0, 0, 0))] * sets,
+        in_specs=[VMEM] * 6,
+        out_specs=[VMEM] * (2 + sets),
         scratch_shapes=[pltpu.VMEM((width, plan.rows), F32)],
-        compiler_params=params(14),
+        compiler_params=params(12),
         cost_estimate=cost(4 * plan.rows * width * columns, 4 * width * columns),
         name="row_grads",
     )(*parts, wg, wu)

time: 68.9 us -> 67.2 us (0.975)
  Pallas kernels: 35.6 us -> 33.9 us
    pallas_call x1, Pallas kernels: 8.99 us -> 7.4 us  [row_grads(): pl.pallas_call(functools.partial(rows_kernel, plan, block_of(columns, wan...]
  transfers between devices with their start and end apart: 14 -> 14, of which waited for: 9 -> 9; matrix products, arithmetic and copies ran while one was open for 0% -> 0% of each run, Pallas kernels for 31% -> 32%
where the time goes in v5:
time: 67.2 us; the launch traced here: 67 us
  Pallas kernels  33.9 us (50%)
  starting transfers between devices  16.7 us (25%)
  waiting for transfers between devices  14.5 us (22%)
  local copies, waits for them, and re-layouts  0.99 us (1%)
  between operations  0.92 us (1%)
    ppermute x11, starting transfers between devices, send(): return lax.ppermute(array, ('dp', 'expert'), pairs)  15.9 us
    pallas_call x2, Pallas kernels, weight_grads(): pl.pallas_call(functools.partial(weights_kernel, factor, block, many), ou...  15 us
    ppermute x11, waiting for transfers between devices, send(): return lax.ppermute(array, ('dp', 'expert'), pairs)  13.1 us
    pallas_call x1, Pallas kernels, row_grads(): pl.pallas_call(functools.partial(rows_kernel, plan, block_of(columns, wan...  7.4 us
    pallas_call x3, Pallas kernels, forward(): pl.pallas_call(functools.partial(forward_kernel, plan, half, len(after),...  6.68 us
    pallas_call x1, Pallas kernels, dispatch(): pl.pallas_call(functools.partial(dispatch_kernel, plan), out_shape=[jax.S...  2.13 us
    pallas_call x1, Pallas kernels, activations(): pl.pallas_call(functools.partial(act_kernel, block_of(columns, wanted)),...  1.71 us
    ppermute x3, waiting for transfers between devices, swap(): return lax.ppermute(part, 'tensor', [(i, i ^ 1) for i in range(size)])  1.41 us
  transfers between devices with their start and end apart: 14, of which 9 were waited for; matrix products, arithmetic and copies ran while one was open for 0% of the time, Pallas kernels for 32%

profile of v5, /device:TPU:0, one launch (start us, length us, event | category | flops | bytes accessed | tf_op | source)
XLA Modules:
  0.0 67.0 jit_solution(14524252531395328550)
XLA Ops:
  0.6 2.1 %dispatch.1 = (bf16[4,80,128]{2,1,0:T(8,128)(2,1)}, bf16[1,160,384]{2,1,0:T(8,128)(2,1)}, bf16[1,160,384]{2,1,0:T(8,128)(2,1)}, bf16[1,160,384]{2,1,0:T(8,128)(2,1)}, bf16[1,160,384]{2,1,0:T(8,128)(2,1)}) custom-call(s32[2,128]{1,0:T(2,128)} %bitcast.10, bf16[2,128]{1,0:T(2,128)(2,1)} %bitcast.11, bf16[128,384]{1,0:T(8,128)(2,1)} %refs_2_.1, ...), custom_call_target="tpu_custom_call" | custom-call | tf_op jit(solution)/shard_map/dispatch/pallas_call | solution.py:109
  2.8 4.1 %collective-permute-start.3 = (bf16[1,160,384]{2,1,0:T(8,128)(2,1)}, bf16[1,160,384]{2,1,0:T(8,128)(2,1)S(1)}, u32[]{:S(2)}, u32[]{:S(2)}) collective-permute-start(bf16[1,160,384]{2,1,0:T(8,128)(2,1)} %get-tuple-element.31), channel_id=1, source_target_pairs={{0,8},{4,12},{8,0},{12,4},{2,10},{6,14},{10,2},{14,6},{1,9},{5,13}... | collective-permute-start | bytes 368648 | tf_op jit(solution)/shard_map/ppermute | solution.py:54
  6.9 1.3 %collective-permute-start.4 = (bf16[1,160,384]{2,1,0:T(8,128)(2,1)}, bf16[1,160,384]{2,1,0:T(8,128)(2,1)S(1)}, u32[]{:S(2)}, u32[]{:S(2)}) collective-permute-start(bf16[1,160,384]{2,1,0:T(8,128)(2,1)} %get-tuple-element.32), channel_id=1, source_target_pairs={{0,10},{4,14},{8,2},{12,6},{2,8},{6,12},{10,0},{14,4},{1,11},{5,15... | collective-permute-start | bytes 368648 | tf_op jit(solution)/shard_map/ppermute | solution.py:54
  8.1 0.9 %copy-done.2 = bf16[1,160,384]{2,1,0:T(8,128)(2,1)S(1)} copy-done((bf16[1,160,384]{2,1,0:T(8,128)(2,1)S(1)}, bf16[1,160,384]{2,1,0:T(8,128)(2,1)}, u32[]{:S(2)}) %copy-start.2) | copy-done | bytes 122904
  9.1 0.0 copy-start
  9.1 0.0 slice-start.1
  9.1 0.0 slice-start.2
  9.1 0.0 slice-start.4
  9.1 0.0 slice-start.5
  9.1 1.6 %collective-permute-start.2 = (bf16[1,160,384]{2,1,0:T(8,128)(2,1)S(1)}, bf16[1,160,384]{2,1,0:T(8,128)(2,1)S(1)}, u32[]{:S(2)}, u32[]{:S(2)}) collective-permute-start(bf16[1,160,384]{2,1,0:T(8,128)(2,1)S(1)} %window_second.1), channel_id=1, source_target_pairs={{0,6},{4,2},{8,14},{12,10},{2,4},{6,0},{10,12},{14,8},{1,7},{5,3},... | collective-permute-start | bytes 368648 | tf_op jit(solution)/shard_map/ppermute | solution.py:54
  10.8 1.5 %collective-permute-start = (bf16[1,160,384]{2,1,0:T(8,128)(2,1)S(1)}, bf16[1,160,384]{2,1,0:T(8,128)(2,1)S(1)}, u32[]{:S(2)}, u32[]{:S(2)}) collective-permute-start(bf16[1,160,384]{2,1,0:T(8,128)(2,1)S(1)} %window_second.1), channel_id=1, source_target_pairs={{0,2},{4,6},{8,10},{12,14},{2,0},{6,4},{10,8},{14,12},{1,3},{5,7},... | collective-permute-start | bytes 368648 | tf_op jit(solution)/shard_map/ppermute | solution.py:54
  12.2 0.0 copy-done
  12.2 0.4 collective-permute-start.1
  12.7 3.8 %collective-permute-done.3.refs_4_.refs_5_ = bf16[1,160,384]{2,1,0:T(8,128)(2,1)S(1)} collective-permute-done((bf16[1,160,384]{2,1,0:T(8,128)(2,1)}, bf16[1,160,384]{2,1,0:T(8,128)(2,1)S(1)}, u32[]{:S(2)}, u32[]{:S(2)}) %collective-permute-start.3) | collective-permute-done | bytes 122912 | tf_op jit(solution)/shard_map/ppermute | solution.py:54
  16.5 0.1 collective-permute-start.5
  16.6 2.7 %collective-permute-done.4.refs_5_.refs_6_ = bf16[1,160,384]{2,1,0:T(8,128)(2,1)S(1)} collective-permute-done((bf16[1,160,384]{2,1,0:T(8,128)(2,1)}, bf16[1,160,384]{2,1,0:T(8,128)(2,1)S(1)}, u32[]{:S(2)}, u32[]{:S(2)}) %collective-permute-start.4) | collective-permute-done | bytes 122912 | tf_op jit(solution)/shard_map/ppermute | solution.py:54
  19.3 0.0 collective-permute-start.6
  19.3 1.1 %collective-permute-done.2.refs_3_.refs_4_ = bf16[1,160,384]{2,1,0:T(8,128)(2,1)S(1)} collective-permute-done((bf16[1,160,384]{2,1,0:T(8,128)(2,1)S(1)}, bf16[1,160,384]{2,1,0:T(8,128)(2,1)S(1)}, u32[]{:S(2)}, u32[]{:S(2)}) %collective-permute-start.2) | collective-permute-done | bytes 122912 | tf_op jit(solution)/shard_map/ppermute | solution.py:54
  20.4 0.0 collective-permute-done.refs_1_.refs_2_
  20.5 0.7 %collective-permute-done.1.refs_2_.refs_3_ = bf16[1,160,384]{2,1,0:T(8,128)(2,1)S(1)} collective-permute-done((bf16[1,160,384]{2,1,0:T(8,128)(2,1)S(1)}, bf16[1,160,384]{2,1,0:T(8,128)(2,1)S(1)}, u32[]{:S(2)}, u32[]{:S(2)}) %collective-permute-start.1) | collective-permute-done | bytes 122912 | tf_op jit(solution)/shard_map/ppermute | solution.py:54
  21.2 2.6 %collective-permute-done.5.refs_6_.refs_7_ = bf16[1,160,384]{2,1,0:T(8,128)(2,1)S(1)} collective-permute-done((bf16[1,160,384]{2,1,0:T(8,128)(2,1)S(1)}, bf16[1,160,384]{2,1,0:T(8,128)(2,1)S(1)}, u32[]{:S(2)}, u32[]{:S(2)}) %collective-permute-start.5) | collective-permute-done | bytes 122912 | tf_op jit(solution)/shard_map/ppermute | solution.py:54
  23.8 1.9 %collective-permute-done.6.refs_7_.refs_8_ = bf16[1,160,384]{2,1,0:T(8,128)(2,1)S(1)} collective-permute-done((bf16[1,160,384]{2,1,0:T(8,128)(2,1)S(1)}, bf16[1,160,384]{2,1,0:T(8,128)(2,1)S(1)}, u32[]{:S(2)}, u32[]{:S(2)}) %collective-permute-start.6) | collective-permute-done | bytes 122912 | tf_op jit(solution)/shard_map/ppermute | solution.py:54
  25.7 0.0 slice-done
  25.7 0.0 slice-done.1
  25.7 0.0 slice-done.2
  25.7 0.0 slice-start.9
  25.7 0.0 slice-start.10
  25.7 2.2 %forward_g.1 = (bf16[160,1536]{1,0:T(8,128)(2,1)S(1)}, bf16[160,4096]{1,0:T(8,128)(2,1)S(1)}) custom-call(bf16[1,160,384]{2,1,0:T(8,128)(2,1)S(1)} %copy-done, bf16[1,160,384]{2,1,0:T(8,128)(2,1)S(1)} %collective-permute-done.refs_1_.refs_2_, bf16[1,160,384]{2,1,0:T(8,128)(2,1)S(1)} %collective-permute-done.1.refs_2_.refs_3_, ...), custom_call_target="tpu_custom_call" | custom-call | flops 2013265920 | bytes 8388608 | tf_op jit(solution)/shard_map/forward_g/pallas_call | solution.py:166
  28.0 0.1 collective-permute-start.7
  28.1 0.0 slice-done.3
  28.1 0.0 slice-done.4
  28.1 0.0 slice-done.5
  28.1 0.0 slice-start.11
  28.1 2.2 %forward_u.1.u0 = bf16[160,4096]{1,0:T(8,128)(2,1)S(1)} custom-call(bf16[160,1536]{1,0:T(8,128)(2,1)S(1)} %get-tuple-element.34.refs_0_.refs_2_, bf16[1536,4096]{1,0:T(8,128)(2,1)S(1)} %bitcast.5), custom_call_target="tpu_custom_call" | custom-call | flops 2013265920 | bytes 8388608 | tf_op jit(solution)/shard_map/forward_u/pallas_call | solution.py:166
  30.3 0.5 collective-permute-start.8
  30.9 0.2 collective-permute-done.7.g1.refs_0_
  31.1 0.0 slice-done.9
  31.1 0.0 slice-done.10
  31.1 0.0 slice-done.11
  31.1 0.0 slice-start.6
  31.1 0.0 slice-start.7
  31.1 2.2 %forward_h.1 = (bf16[160,1536]{1,0:T(8,128)(2,1)S(1)}, bf16[160,4096]{1,0:T(8,128)(2,1)S(1)}) custom-call(bf16[160,4096]{1,0:T(8,128)(2,1)S(1)} %collective-permute-done.7.g1.refs_0_, bf16[1,160,384]{2,1,0:T(8,128)(2,1)S(1)} %copy-done, bf16[1,160,384]{2,1,0:T(8,128)(2,1)S(1)} %collective-permute-done.refs_1_.refs_2_, ...), custom_call_target="tpu_custom_call" | custom-call | flops 2013265920 | bytes 8388608 | tf_op jit(solution)/shard_map/forward_h/pallas_call | solution.py:166
  33.4 0.0 slice-start.8
  33.4 0.2 collective-permute-start.9
  33.6 0.0 collective-permute-done.8.u1
  33.6 1.7 %activations.1 = (bf16[160,4096]{1,0:T(8,128)(2,1)S(1)}, bf16[160,4096]{1,0:T(8,128)(2,1)S(1)}, bf16[160,4096]{1,0:T(8,128)(2,1)S(1)}) custom-call(bf16[160,4096]{1,0:T(8,128)(2,1)S(1)} %get-tuple-element.33.g0, bf16[160,4096]{1,0:T(8,128)(2,1)S(1)} %collective-permute-done.7.g1.refs_0_, bf16[160,4096]{1,0:T(8,128)(2,1)S(1)} %forward_u.1.u0, ...), custom_call_target="tpu_custom_call" | custom-call | flops 5898240000 | bytes 9175040 | tf_op jit(solution)/shard_map/activations/pallas_call | solution.py:191
  35.3 1.2 %collective-permute-done.9.d1 = bf16[160,4096]{1,0:T(8,128)(2,1)S(1)} collective-permute-done((bf16[160,4096]{1,0:T(8,128)(2,1)S(1)}, bf16[160,4096]{1,0:T(8,128)(2,1)S(1)}, u32[]{:S(2)}, u32[]{:S(2)}) %collective-permute-start.9) | collective-permute-done | bytes 1310752 | tf_op jit(solution)/shard_map/ppermute | solution.py:324
  36.5 0.0 slice-done.6
  36.5 0.0 slice-done.7
  36.5 0.0 slice-done.8
  36.5 7.4 %row_grads.1 = (bf16[160,4096]{1,0:T(8,128)(2,1)S(1)}, bf16[160,4096]{1,0:T(8,128)(2,1)S(1)}, bf16[4,80,384]{2,1,0:T(8,128)(2,1)S(1)}, bf16[4,80,384]{2,1,0:T(8,128)(2,1)S(1)}) custom-call(bf16[160,4096]{1,0:T(8,128)(2,1)S(1)} %get-tuple-element.35.by_gate_ref, bf16[160,4096]{1,0:T(8,128)(2,1)S(1)} %get-tuple-element.36.by_up_ref, ...), custom_call_target="tpu_custom_call" | custom-call | flops 4026531840 | bytes 25165824 | tf_op jit(solution)/shard_map/row_grads/pallas_call | solution.py:229
  43.9 0.1 collective-permute-start.10
  44.0 9.1 %grads_gu.1 = (bf16[1536,4096]{1,0:T(8,128)(2,1)}, bf16[1536,4096]{1,0:T(8,128)(2,1)}, f32[8,128]{1,0:T(8,128)S(1)}) custom-call(bf16[160,1536]{1,0:T(8,128)(2,1)S(1)} %get-tuple-element.34.refs_0_.refs_2_, bf16[160,4096]{1,0:T(8,128)(2,1)S(1)} %get-tuple-element.40.refs_1_, bf16[160,1536]{1,0:T(8,128)(2,1)S(1)} %get-tuple-element.34.refs_0_.refs_2_, ...), custom_call_target="tpu_custom_call" | custom-call | flops 4026531840 | bytes 25165824 | tf_op jit(solution)/shard_map/grads_gu/pallas_call | solution.py:263
  53.1 0.0 collective-permute-done.10.got_ref
  53.1 0.1 pair_sum.1
  53.2 1.8 %collective-permute-start.11 = (bf16[1,80,384]{2,1,0:T(8,128)(2,1)S(1)}, bf16[1,80,384]{2,1,0:T(8,128)(2,1)S(1)}, u32[]{:S(2)}, u32[]{:S(2)}) collective-permute-start(bf16[1,80,384]{2,1,0:T(8,128)(2,1)S(1)} %get-tuple-element.44), channel_id=1, source_target_pairs={{0,2},{4,6},{8,10},{12,14},{2,0},{6,4},{10,8},{14,12},{1,3},{5,7},... | collective-permute-start | bytes 184328 | tf_op jit(solution)/shard_map/ppermute | solution.py:54
  55.1 4.9 %collective-permute-start.12 = (bf16[1,80,384]{2,1,0:T(8,128)(2,1)S(1)}, bf16[1,80,384]{2,1,0:T(8,128)(2,1)S(1)}, u32[]{:S(2)}, u32[]{:S(2)}) collective-permute-start(bf16[1,80,384]{2,1,0:T(8,128)(2,1)S(1)} %get-tuple-element.45), channel_id=1, source_target_pairs={{0,8},{4,12},{8,0},{12,4},{2,10},{6,14},{10,2},{14,6},{1,9},{5,13}... | collective-permute-start | bytes 184328 | tf_op jit(solution)/shard_map/ppermute | solution.py:54
  60.0 0.0 collective-permute-start.13
  60.0 5.9 %grad_down.1 = (bf16[1536,4096]{1,0:T(8,128)(2,1)}, f32[8,128]{1,0:T(8,128)}) custom-call(bf16[160,1536]{1,0:T(8,128)(2,1)S(1)} %get-tuple-element.49.refs_0_, bf16[160,4096]{1,0:T(8,128)(2,1)S(1)} %get-tuple-element.50.refs_1_, bf16[1,80,384]{2,1,0:T(8,128)(2,1)S(1)} %get-tuple-element.43.refs_0_.refs_2_), custom_call_target="tpu_custom_call" | custom-call | flops 2013265920 | bytes 12582912 | tf_op jit(solution)/shard_map/grad_down/pallas_call | solution.py:263
  65.8 0.0 collective-permute-done.11.refs_1_
  65.9 0.0 collective-permute-done.12.refs_2_
  65.9 0.2 collective-permute-done.13.refs_3_
  66.1 0.0 copy-done.1
  66.1 0.9 %combine.1 = bf16[128,384]{1,0:T(8,128)(2,1)} custom-call(bf16[4,80,128]{2,1,0:T(8,128)(2,1)S(1)} %copy-done.1, bf16[1,80,384]{2,1,0:T(8,128)(2,1)S(1)} %get-tuple-element.43.refs_0_.refs_2_, bf16[1,80,384]{2,1,0:T(8,128)(2,1)S(1)} %collective-permute-done.11.refs_1_, bf16[1,80,384]{2,1,0:T(8,128)(2,1)S(1)} %collective-permute-done.12.refs_2_, ...), custom_call_target="tpu_custom_call" | custom-call | tf_op jit(solution)/shard_map/combine/pallas_call | solution.py:308
  (10 shorter events, 0.0 us)
Async XLA Ops:
  2.8 13.7 %collective-permute-start.3 = (bf16[1,160,384]{2,1,0:T(8,128)(2,1)}, bf16[1,160,384]{2,1,0:T(8,128)(2,1)S(1)}, u32[]{:S(2)}, u32[]{:S(2)}) collective-permute-start(bf16[1,160,384]{2,1,0:T(8,128)(2,1)} %get-tuple-element.31), channel_id=1, source_target_pairs={{0,8},{4,12},{8,0},{12,4},{2,10},{6,14},{10,2},{14,6},{1,9},{5,13}... | collective-permute-start | bytes 368648 | tf_op jit(solution)/shard_map/ppermute | solution.py:54
  6.9 12.4 %collective-permute-start.4 = (bf16[1,160,384]{2,1,0:T(8,128)(2,1)}, bf16[1,160,384]{2,1,0:T(8,128)(2,1)S(1)}, u32[]{:S(2)}, u32[]{:S(2)}) collective-permute-start(bf16[1,160,384]{2,1,0:T(8,128)(2,1)} %get-tuple-element.32), channel_id=1, source_target_pairs={{0,10},{4,14},{8,2},{12,6},{2,8},{6,12},{10,0},{14,4},{1,11},{5,15... | collective-permute-start | bytes 368648 | tf_op jit(solution)/shard_map/ppermute | solution.py:54
  8.1 0.9 %copy-start.2 = (bf16[1,160,384]{2,1,0:T(8,128)(2,1)S(1)}, bf16[1,160,384]{2,1,0:T(8,128)(2,1)}, u32[]{:S(2)}) copy-start(bf16[1,160,384]{2,1,0:T(8,128)(2,1)} %get-tuple-element.30.array_ref) | copy-start | bytes 368644
  9.0 16.7 %slice-start = ((s8[12582912]{0:T(1024)(128)(4,1)}), s8[4194304]{0:T(1024)(128)(4,1)S(1)}, s32[]{:S(2)}) async-start(s8[12582912]{0:T(1024)(128)(4,1)} %bitcast.2), calls=%async_computation | async-start | bytes 8388608
  9.0 19.0 %slice-start.3 = ((s8[12582912]{0:T(1024)(128)(4,1)}), s8[4194304]{0:T(1024)(128)(4,1)S(1)}, s32[]{:S(2)}) async-start(s8[12582912]{0:T(1024)(128)(4,1)} %bitcast.4), calls=%async_computation.3 | async-start | bytes 8388608
  9.1 3.2 %copy-start = (bf16[1,160,384]{2,1,0:T(8,128)(2,1)S(1)}, bf16[1,160,384]{2,1,0:T(8,128)(2,1)}, u32[]{:S(2)}) copy-start(bf16[1,160,384]{2,1,0:T(8,128)(2,1)} %get-tuple-element.29.refs_0_.refs_1_) | copy-start | bytes 368644
  9.1 16.6 %slice-start.1 = ((s8[12582912]{0:T(1024)(128)(4,1)}), s8[4194304]{0:T(1024)(128)(4,1)S(1)}, s32[]{:S(2)}) async-start(s8[12582912]{0:T(1024)(128)(4,1)} %bitcast.2), calls=%async_computation.1 | async-start | bytes 8388608
  9.1 16.6 %slice-start.2 = ((s8[12582912]{0:T(1024)(128)(4,1)}), s8[4194304]{0:T(1024)(128)(4,1)S(1)}, s32[]{:S(2)}) async-start(s8[12582912]{0:T(1024)(128)(4,1)} %bitcast.2), calls=%async_computation.2 | async-start | bytes 8388608
  9.1 19.0 %slice-start.4 = ((s8[12582912]{0:T(1024)(128)(4,1)}), s8[4194304]{0:T(1024)(128)(4,1)S(1)}, s32[]{:S(2)}) async-start(s8[12582912]{0:T(1024)(128)(4,1)} %bitcast.4), calls=%async_computation.4 | async-start | bytes 8388608
  9.1 19.0 %slice-start.5 = ((s8[12582912]{0:T(1024)(128)(4,1)}), s8[4194304]{0:T(1024)(128)(4,1)S(1)}, s32[]{:S(2)}) async-start(s8[12582912]{0:T(1024)(128)(4,1)} %bitcast.4), calls=%async_computation.5 | async-start | bytes 8388608
  9.1 11.3 %collective-permute-start.2 = (bf16[1,160,384]{2,1,0:T(8,128)(2,1)S(1)}, bf16[1,160,384]{2,1,0:T(8,128)(2,1)S(1)}, u32[]{:S(2)}, u32[]{:S(2)}) collective-permute-start(bf16[1,160,384]{2,1,0:T(8,128)(2,1)S(1)} %window_second.1), channel_id=1, source_target_pairs={{0,6},{4,2},{8,14},{12,10},{2,4},{6,0},{10,12},{14,8},{1,7},{5,3},... | collective-permute-start | bytes 368648 | tf_op jit(solution)/shard_map/ppermute | solution.py:54
  10.8 9.7 %collective-permute-start = (bf16[1,160,384]{2,1,0:T(8,128)(2,1)S(1)}, bf16[1,160,384]{2,1,0:T(8,128)(2,1)S(1)}, u32[]{:S(2)}, u32[]{:S(2)}) collective-permute-start(bf16[1,160,384]{2,1,0:T(8,128)(2,1)S(1)} %window_second.1), channel_id=1, source_target_pairs={{0,2},{4,6},{8,10},{12,14},{2,0},{6,4},{10,8},{14,12},{1,3},{5,7},... | collective-permute-start | bytes 368648 | tf_op jit(solution)/shard_map/ppermute | solution.py:54
  12.2 8.9 %collective-permute-start.1 = (bf16[1,160,384]{2,1,0:T(8,128)(2,1)S(1)}, bf16[1,160,384]{2,1,0:T(8,128)(2,1)S(1)}, u32[]{:S(2)}, u32[]{:S(2)}) collective-permute-start(bf16[1,160,384]{2,1,0:T(8,128)(2,1)S(1)} %copy-done), channel_id=1, source_target_pairs={{0,4},{4,0},{8,12},{12,8},{2,6},{6,2},{10,14},{14,10},{1,5},{5,1},... | collective-permute-start | bytes 368648 | tf_op jit(solution)/shard_map/ppermute | solution.py:54
  16.5 7.3 %collective-permute-start.5 = (bf16[1,160,384]{2,1,0:T(8,128)(2,1)S(1)}, bf16[1,160,384]{2,1,0:T(8,128)(2,1)S(1)}, u32[]{:S(2)}, u32[]{:S(2)}) collective-permute-start(bf16[1,160,384]{2,1,0:T(8,128)(2,1)S(1)} %collective-permute-done.3.refs_4_.refs_5_), channel_id=1, source_target_pairs={{0,4},{4,0},{8,12},{12,8},{2,6},{6,2},{10,14},{14,10},{1,5},{5,1},... | collective-permute-start | bytes 368648 | tf_op jit(solution)/shard_map/ppermute | solution.py:54
  19.3 6.4 %collective-permute-start.6 = (bf16[1,160,384]{2,1,0:T(8,128)(2,1)S(1)}, bf16[1,160,384]{2,1,0:T(8,128)(2,1)S(1)}, u32[]{:S(2)}, u32[]{:S(2)}) collective-permute-start(bf16[1,160,384]{2,1,0:T(8,128)(2,1)S(1)} %collective-permute-done.4.refs_5_.refs_6_), channel_id=1, source_target_pairs={{0,4},{4,0},{8,12},{12,8},{2,6},{6,2},{10,14},{14,10},{1,5},{5,1},... | collective-permute-start | bytes 368648 | tf_op jit(solution)/shard_map/ppermute | solution.py:54
  25.7 5.4 %slice-start.9 = ((s8[12582912]{0:T(1024)(128)(4,1)}), s8[4194304]{0:T(1024)(128)(4,1)S(1)}, s32[]{:S(2)}) async-start(s8[12582912]{0:T(1024)(128)(4,1)} %bitcast.8), calls=%async_computation.9 | async-start | bytes 8388608
  25.7 5.4 %slice-start.10 = ((s8[12582912]{0:T(1024)(128)(4,1)}), s8[4194304]{0:T(1024)(128)(4,1)S(1)}, s32[]{:S(2)}) async-start(s8[12582912]{0:T(1024)(128)(4,1)} %bitcast.8), calls=%async_computation.10 | async-start | bytes 8388608
  28.0 3.1 %collective-permute-start.7 = (bf16[160,4096]{1,0:T(8,128)(2,1)S(1)}, bf16[160,4096]{1,0:T(8,128)(2,1)S(1)}, u32[]{:S(2)}, u32[]{:S(2)}) collective-permute-start(bf16[160,4096]{1,0:T(8,128)(2,1)S(1)} %get-tuple-element.33.g0), channel_id=1, source_target_pairs={{0,1},{1,0},{2,3},{3,2},{4,5},{5,4},{6,7},{7,6},{8,9},{9,8},{10,11... | collective-permute-start | bytes 3932168 | tf_op jit(solution)/shard_map/ppermute | solution.py:324
  28.1 3.0 %slice-start.11 = ((s8[12582912]{0:T(1024)(128)(4,1)}), s8[4194304]{0:T(1024)(128)(4,1)S(1)}, s32[]{:S(2)}) async-start(s8[12582912]{0:T(1024)(128)(4,1)} %bitcast.8), calls=%async_computation.11 | async-start | bytes 8388608
  30.3 3.3 %collective-permute-start.8 = (bf16[160,4096]{1,0:T(8,128)(2,1)S(1)}, bf16[160,4096]{1,0:T(8,128)(2,1)S(1)}, u32[]{:S(2)}, u32[]{:S(2)}) collective-permute-start(bf16[160,4096]{1,0:T(8,128)(2,1)S(1)} %forward_u.1.u0), channel_id=1, source_target_pairs={{0,1},{1,0},{2,3},{3,2},{4,5},{5,4},{6,7},{7,6},{8,9},{9,8},{10,11... | collective-permute-start | bytes 3932168 | tf_op jit(solution)/shard_map/ppermute | solution.py:324
  31.1 5.4 %slice-start.6 = ((s8[12582912]{0:T(1024)(128)(4,1)}), s8[4194304]{0:T(1024)(128)(4,1)S(1)}, s32[]{:S(2)}) async-start(s8[12582912]{0:T(1024)(128)(4,1)} %bitcast.6), calls=%async_computation.6 | async-start | bytes 8388608
  31.1 5.4 %slice-start.7 = ((s8[12582912]{0:T(1024)(128)(4,1)}), s8[4194304]{0:T(1024)(128)(4,1)S(1)}, s32[]{:S(2)}) async-start(s8[12582912]{0:T(1024)(128)(4,1)} %bitcast.6), calls=%async_computation.7 | async-start | bytes 8388608
  33.4 3.1 %slice-start.8 = ((s8[12582912]{0:T(1024)(128)(4,1)}), s8[4194304]{0:T(1024)(128)(4,1)S(1)}, s32[]{:S(2)}) async-start(s8[12582912]{0:T(1024)(128)(4,1)} %bitcast.6), calls=%async_computation.8 | async-start | bytes 8388608
  33.4 3.1 %collective-permute-start.9 = (bf16[160,4096]{1,0:T(8,128)(2,1)S(1)}, bf16[160,4096]{1,0:T(8,128)(2,1)S(1)}, u32[]{:S(2)}, u32[]{:S(2)}) collective-permute-start(bf16[160,4096]{1,0:T(8,128)(2,1)S(1)} %get-tuple-element.37.d0), channel_id=1, source_target_pairs={{0,1},{1,0},{2,3},{3,2},{4,5},{5,4},{6,7},{7,6},{8,9},{9,8},{10,11... | collective-permute-start | bytes 3932168 | tf_op jit(solution)/shard_map/ppermute | solution.py:324
  43.9 9.2 %collective-permute-start.10 = (bf16[4,80,384]{2,1,0:T(8,128)(2,1)S(1)}, bf16[4,80,384]{2,1,0:T(8,128)(2,1)S(1)}, u32[]{:S(2)}, u32[]{:S(2)}) collective-permute-start(bf16[4,80,384]{2,1,0:T(8,128)(2,1)S(1)} %get-tuple-element.39), channel_id=1, source_target_pairs={{0,4},{4,0},{8,12},{12,8},{2,6},{6,2},{10,14},{14,10},{1,5},{5,1},... | collective-permute-start | bytes 737288 | tf_op jit(solution)/shard_map/ppermute | solution.py:54
  53.2 12.6 %collective-permute-start.11 = (bf16[1,80,384]{2,1,0:T(8,128)(2,1)S(1)}, bf16[1,80,384]{2,1,0:T(8,128)(2,1)S(1)}, u32[]{:S(2)}, u32[]{:S(2)}) collective-permute-start(bf16[1,80,384]{2,1,0:T(8,128)(2,1)S(1)} %get-tuple-element.44), channel_id=1, source_target_pairs={{0,2},{4,6},{8,10},{12,14},{2,0},{6,4},{10,8},{14,12},{1,3},{5,7},... | collective-permute-start | bytes 184328 | tf_op jit(solution)/shard_map/ppermute | solution.py:54
  55.1 10.8 %collective-permute-start.12 = (bf16[1,80,384]{2,1,0:T(8,128)(2,1)S(1)}, bf16[1,80,384]{2,1,0:T(8,128)(2,1)S(1)}, u32[]{:S(2)}, u32[]{:S(2)}) collective-permute-start(bf16[1,80,384]{2,1,0:T(8,128)(2,1)S(1)} %get-tuple-element.45), channel_id=1, source_target_pairs={{0,8},{4,12},{8,0},{12,4},{2,10},{6,14},{10,2},{14,6},{1,9},{5,13}... | collective-permute-start | bytes 184328 | tf_op jit(solution)/shard_map/ppermute | solution.py:54
  60.0 6.1 %collective-permute-start.13 = (bf16[1,80,384]{2,1,0:T(8,128)(2,1)S(1)}, bf16[1,80,384]{2,1,0:T(8,128)(2,1)S(1)}, u32[]{:S(2)}, u32[]{:S(2)}) collective-permute-start(bf16[1,80,384]{2,1,0:T(8,128)(2,1)S(1)} %get-tuple-element.46), channel_id=1, source_target_pairs={{0,10},{4,14},{8,2},{12,6},{2,8},{6,12},{10,0},{14,4},{1,11},{5,15... | collective-permute-start | bytes 184328 | tf_op jit(solution)/shard_map/ppermute | solution.py:54
  60.0 6.1 %copy-start.1 = (bf16[4,80,128]{2,1,0:T(8,128)(2,1)S(1)}, bf16[4,80,128]{2,1,0:T(8,128)(2,1)}, u32[]{:S(2)}) copy-start(bf16[4,80,128]{2,1,0:T(8,128)(2,1)} %get-tuple-element.28.sel_ref) | copy-start | bytes 245764

commit v6 on v5

--- a/solution.py
+++ b/solution.py
@@ -353,7 +353,7 @@
         done = backs[0]
     else:
         backs = [arrived]
-    grad_down, _ = weight_grads(factor, ((q_full, h),), done, "grad_down")
+    grad_down, _ = weight_grads(factor, ((q_full, h),), done, "grad_down", 256)
     token_grad = combine(plan, sel, backs)
     return (token_grad, grad_gate, grad_up, grad_down)
 

time: 67.2 us -> 67.2 us (level)
  no operation moved by 1% of the time
where the time goes in v6:
time: 67.2 us; the launch traced here: 67 us
  Pallas kernels  34 us (51%)
  starting transfers between devices  16.7 us (25%)
  waiting for transfers between devices  14.5 us (22%)
  local copies, waits for them, and re-layouts  0.99 us (1%)
  between operations  0.92 us (1%)
    ppermute x11, starting transfers between devices, send(): return lax.ppermute(array, ('dp', 'expert'), pairs)  15.9 us
    pallas_call x2, Pallas kernels, weight_grads(): pl.pallas_call(functools.partial(weights_kernel, factor, block, many), ou...  15 us
    ppermute x11, waiting for transfers between devices, send(): return lax.ppermute(array, ('dp', 'expert'), pairs)  13.1 us
    pallas_call x1, Pallas kernels, row_grads(): pl.pallas_call(functools.partial(rows_kernel, plan, block_of(columns, wan...  7.4 us
    pallas_call x3, Pallas kernels, forward(): pl.pallas_call(functools.partial(forward_kernel, plan, half, len(after),...  6.68 us
    pallas_call x1, Pallas kernels, dispatch(): pl.pallas_call(functools.partial(dispatch_kernel, plan), out_shape=[jax.S...  2.13 us
    pallas_call x1, Pallas kernels, activations(): pl.pallas_call(functools.partial(act_kernel, block_of(columns, wanted)),...  1.71 us
    ppermute x3, waiting for transfers between devices, swap(): return lax.ppermute(part, 'tensor', [(i, i ^ 1) for i in range(size)])  1.41 us
  transfers between devices with their start and end apart: 14, of which 9 were waited for; matrix products, arithmetic and copies ran while one was open for 0% of the time, Pallas kernels for 32%

profile of v6, /device:TPU:0, one launch (start us, length us, event | category | flops | bytes accessed | tf_op | source)
XLA Modules:
  0.0 67.0 jit_solution(6106673706318517089)
XLA Ops:
  0.6 2.1 %dispatch.1 = (bf16[4,80,128]{2,1,0:T(8,128)(2,1)}, bf16[1,160,384]{2,1,0:T(8,128)(2,1)}, bf16[1,160,384]{2,1,0:T(8,128)(2,1)}, bf16[1,160,384]{2,1,0:T(8,128)(2,1)}, bf16[1,160,384]{2,1,0:T(8,128)(2,1)}) custom-call(s32[2,128]{1,0:T(2,128)} %bitcast.10, bf16[2,128]{1,0:T(2,128)(2,1)} %bitcast.11, bf16[128,384]{1,0:T(8,128)(2,1)} %refs_2_.1, ...), custom_call_target="tpu_custom_call" | custom-call | tf_op jit(solution)/shard_map/dispatch/pallas_call | solution.py:109
  2.8 4.1 %collective-permute-start.3 = (bf16[1,160,384]{2,1,0:T(8,128)(2,1)}, bf16[1,160,384]{2,1,0:T(8,128)(2,1)S(1)}, u32[]{:S(2)}, u32[]{:S(2)}) collective-permute-start(bf16[1,160,384]{2,1,0:T(8,128)(2,1)} %get-tuple-element.31), channel_id=1, source_target_pairs={{0,8},{4,12},{8,0},{12,4},{2,10},{6,14},{10,2},{14,6},{1,9},{5,13}... | collective-permute-start | bytes 368648 | tf_op jit(solution)/shard_map/ppermute | solution.py:54
  6.9 1.3 %collective-permute-start.4 = (bf16[1,160,384]{2,1,0:T(8,128)(2,1)}, bf16[1,160,384]{2,1,0:T(8,128)(2,1)S(1)}, u32[]{:S(2)}, u32[]{:S(2)}) collective-permute-start(bf16[1,160,384]{2,1,0:T(8,128)(2,1)} %get-tuple-element.32), channel_id=1, source_target_pairs={{0,10},{4,14},{8,2},{12,6},{2,8},{6,12},{10,0},{14,4},{1,11},{5,15... | collective-permute-start | bytes 368648 | tf_op jit(solution)/shard_map/ppermute | solution.py:54
  8.1 0.9 %copy-done.2 = bf16[1,160,384]{2,1,0:T(8,128)(2,1)S(1)} copy-done((bf16[1,160,384]{2,1,0:T(8,128)(2,1)S(1)}, bf16[1,160,384]{2,1,0:T(8,128)(2,1)}, u32[]{:S(2)}) %copy-start.2) | copy-done | bytes 122904
  9.1 0.0 copy-start
  9.1 0.0 slice-start.1
  9.1 0.0 slice-start.2
  9.1 0.0 slice-start.4
  9.1 0.0 slice-start.5
  9.1 1.6 %collective-permute-start.2 = (bf16[1,160,384]{2,1,0:T(8,128)(2,1)S(1)}, bf16[1,160,384]{2,1,0:T(8,128)(2,1)S(1)}, u32[]{:S(2)}, u32[]{:S(2)}) collective-permute-start(bf16[1,160,384]{2,1,0:T(8,128)(2,1)S(1)} %window_second.1), channel_id=1, source_target_pairs={{0,6},{4,2},{8,14},{12,10},{2,4},{6,0},{10,12},{14,8},{1,7},{5,3},... | collective-permute-start | bytes 368648 | tf_op jit(solution)/shard_map/ppermute | solution.py:54
  10.8 1.5 %collective-permute-start = (bf16[1,160,384]{2,1,0:T(8,128)(2,1)S(1)}, bf16[1,160,384]{2,1,0:T(8,128)(2,1)S(1)}, u32[]{:S(2)}, u32[]{:S(2)}) collective-permute-start(bf16[1,160,384]{2,1,0:T(8,128)(2,1)S(1)} %window_second.1), channel_id=1, source_target_pairs={{0,2},{4,6},{8,10},{12,14},{2,0},{6,4},{10,8},{14,12},{1,3},{5,7},... | collective-permute-start | bytes 368648 | tf_op jit(solution)/shard_map/ppermute | solution.py:54
  12.2 0.0 copy-done
  12.2 0.4 collective-permute-start.1
  12.7 3.8 %collective-permute-done.3.refs_4_.refs_5_ = bf16[1,160,384]{2,1,0:T(8,128)(2,1)S(1)} collective-permute-done((bf16[1,160,384]{2,1,0:T(8,128)(2,1)}, bf16[1,160,384]{2,1,0:T(8,128)(2,1)S(1)}, u32[]{:S(2)}, u32[]{:S(2)}) %collective-permute-start.3) | collective-permute-done | bytes 122912 | tf_op jit(solution)/shard_map/ppermute | solution.py:54
  16.5 0.1 collective-permute-start.5
  16.6 2.7 %collective-permute-done.4.refs_5_.refs_6_ = bf16[1,160,384]{2,1,0:T(8,128)(2,1)S(1)} collective-permute-done((bf16[1,160,384]{2,1,0:T(8,128)(2,1)}, bf16[1,160,384]{2,1,0:T(8,128)(2,1)S(1)}, u32[]{:S(2)}, u32[]{:S(2)}) %collective-permute-start.4) | collective-permute-done | bytes 122912 | tf_op jit(solution)/shard_map/ppermute | solution.py:54
  19.3 0.0 collective-permute-start.6
  19.3 1.1 %collective-permute-done.2.refs_3_.refs_4_ = bf16[1,160,384]{2,1,0:T(8,128)(2,1)S(1)} collective-permute-done((bf16[1,160,384]{2,1,0:T(8,128)(2,1)S(1)}, bf16[1,160,384]{2,1,0:T(8,128)(2,1)S(1)}, u32[]{:S(2)}, u32[]{:S(2)}) %collective-permute-start.2) | collective-permute-done | bytes 122912 | tf_op jit(solution)/shard_map/ppermute | solution.py:54
  20.4 0.0 collective-permute-done.refs_1_.refs_2_
  20.5 0.7 %collective-permute-done.1.refs_2_.refs_3_ = bf16[1,160,384]{2,1,0:T(8,128)(2,1)S(1)} collective-permute-done((bf16[1,160,384]{2,1,0:T(8,128)(2,1)S(1)}, bf16[1,160,384]{2,1,0:T(8,128)(2,1)S(1)}, u32[]{:S(2)}, u32[]{:S(2)}) %collective-permute-start.1) | collective-permute-done | bytes 122912 | tf_op jit(solution)/shard_map/ppermute | solution.py:54
  21.2 2.6 %collective-permute-done.5.refs_6_.refs_7_ = bf16[1,160,384]{2,1,0:T(8,128)(2,1)S(1)} collective-permute-done((bf16[1,160,384]{2,1,0:T(8,128)(2,1)S(1)}, bf16[1,160,384]{2,1,0:T(8,128)(2,1)S(1)}, u32[]{:S(2)}, u32[]{:S(2)}) %collective-permute-start.5) | collective-permute-done | bytes 122912 | tf_op jit(solution)/shard_map/ppermute | solution.py:54
  23.8 1.9 %collective-permute-done.6.refs_7_.refs_8_ = bf16[1,160,384]{2,1,0:T(8,128)(2,1)S(1)} collective-permute-done((bf16[1,160,384]{2,1,0:T(8,128)(2,1)S(1)}, bf16[1,160,384]{2,1,0:T(8,128)(2,1)S(1)}, u32[]{:S(2)}, u32[]{:S(2)}) %collective-permute-start.6) | collective-permute-done | bytes 122912 | tf_op jit(solution)/shard_map/ppermute | solution.py:54
  25.7 0.0 slice-done
  25.7 0.0 slice-done.1
  25.7 0.0 slice-done.2
  25.7 0.0 slice-start.9
  25.7 0.0 slice-start.10
  25.7 2.2 %forward_g.1 = (bf16[160,1536]{1,0:T(8,128)(2,1)S(1)}, bf16[160,4096]{1,0:T(8,128)(2,1)S(1)}) custom-call(bf16[1,160,384]{2,1,0:T(8,128)(2,1)S(1)} %copy-done, bf16[1,160,384]{2,1,0:T(8,128)(2,1)S(1)} %collective-permute-done.refs_1_.refs_2_, bf16[1,160,384]{2,1,0:T(8,128)(2,1)S(1)} %collective-permute-done.1.refs_2_.refs_3_, ...), custom_call_target="tpu_custom_call" | custom-call | flops 2013265920 | bytes 8388608 | tf_op jit(solution)/shard_map/forward_g/pallas_call | solution.py:166
  28.0 0.1 collective-permute-start.7
  28.1 0.0 slice-done.3
  28.1 0.0 slice-done.4
  28.1 0.0 slice-done.5
  28.1 0.0 slice-start.11
  28.1 2.2 %forward_u.1.u0 = bf16[160,4096]{1,0:T(8,128)(2,1)S(1)} custom-call(bf16[160,1536]{1,0:T(8,128)(2,1)S(1)} %get-tuple-element.34.refs_0_.refs_2_, bf16[1536,4096]{1,0:T(8,128)(2,1)S(1)} %bitcast.5), custom_call_target="tpu_custom_call" | custom-call | flops 2013265920 | bytes 8388608 | tf_op jit(solution)/shard_map/forward_u/pallas_call | solution.py:166
  30.3 0.5 collective-permute-start.8
  30.9 0.2 collective-permute-done.7.g1.refs_0_
  31.1 0.0 slice-done.9
  31.1 0.0 slice-done.10
  31.1 0.0 slice-done.11
  31.1 0.0 slice-start.6
  31.1 0.0 slice-start.7
  31.1 2.2 %forward_h.1 = (bf16[160,1536]{1,0:T(8,128)(2,1)S(1)}, bf16[160,4096]{1,0:T(8,128)(2,1)S(1)}) custom-call(bf16[160,4096]{1,0:T(8,128)(2,1)S(1)} %collective-permute-done.7.g1.refs_0_, bf16[1,160,384]{2,1,0:T(8,128)(2,1)S(1)} %copy-done, bf16[1,160,384]{2,1,0:T(8,128)(2,1)S(1)} %collective-permute-done.refs_1_.refs_2_, ...), custom_call_target="tpu_custom_call" | custom-call | flops 2013265920 | bytes 8388608 | tf_op jit(solution)/shard_map/forward_h/pallas_call | solution.py:166
  33.4 0.0 slice-start.8
  33.4 0.2 collective-permute-start.9
  33.6 0.0 collective-permute-done.8.u1
  33.6 1.7 %activations.1 = (bf16[160,4096]{1,0:T(8,128)(2,1)S(1)}, bf16[160,4096]{1,0:T(8,128)(2,1)S(1)}, bf16[160,4096]{1,0:T(8,128)(2,1)S(1)}) custom-call(bf16[160,4096]{1,0:T(8,128)(2,1)S(1)} %get-tuple-element.33.g0, bf16[160,4096]{1,0:T(8,128)(2,1)S(1)} %collective-permute-done.7.g1.refs_0_, bf16[160,4096]{1,0:T(8,128)(2,1)S(1)} %forward_u.1.u0, ...), custom_call_target="tpu_custom_call" | custom-call | flops 5898240000 | bytes 9175040 | tf_op jit(solution)/shard_map/activations/pallas_call | solution.py:191
  35.3 1.2 %collective-permute-done.9.d1 = bf16[160,4096]{1,0:T(8,128)(2,1)S(1)} collective-permute-done((bf16[160,4096]{1,0:T(8,128)(2,1)S(1)}, bf16[160,4096]{1,0:T(8,128)(2,1)S(1)}, u32[]{:S(2)}, u32[]{:S(2)}) %collective-permute-start.9) | collective-permute-done | bytes 1310752 | tf_op jit(solution)/shard_map/ppermute | solution.py:324
  36.5 0.0 slice-done.6
  36.5 0.0 slice-done.7
  36.5 0.0 slice-done.8
  36.5 7.4 %row_grads.1 = (bf16[160,4096]{1,0:T(8,128)(2,1)S(1)}, bf16[160,4096]{1,0:T(8,128)(2,1)S(1)}, bf16[4,80,384]{2,1,0:T(8,128)(2,1)S(1)}, bf16[4,80,384]{2,1,0:T(8,128)(2,1)S(1)}) custom-call(bf16[160,4096]{1,0:T(8,128)(2,1)S(1)} %get-tuple-element.35.by_gate_ref, bf16[160,4096]{1,0:T(8,128)(2,1)S(1)} %get-tuple-element.36.by_up_ref, ...), custom_call_target="tpu_custom_call" | custom-call | flops 4026531840 | bytes 25165824 | tf_op jit(solution)/shard_map/row_grads/pallas_call | solution.py:229
  43.9 0.1 collective-permute-start.10
  44.0 9.1 %grads_gu.1 = (bf16[1536,4096]{1,0:T(8,128)(2,1)}, bf16[1536,4096]{1,0:T(8,128)(2,1)}, f32[8,128]{1,0:T(8,128)S(1)}) custom-call(bf16[160,1536]{1,0:T(8,128)(2,1)S(1)} %get-tuple-element.34.refs_0_.refs_2_, bf16[160,4096]{1,0:T(8,128)(2,1)S(1)} %get-tuple-element.40.refs_1_, bf16[160,1536]{1,0:T(8,128)(2,1)S(1)} %get-tuple-element.34.refs_0_.refs_2_, ...), custom_call_target="tpu_custom_call" | custom-call | flops 4026531840 | bytes 25165824 | tf_op jit(solution)/shard_map/grads_gu/pallas_call | solution.py:263
  53.1 0.0 collective-permute-done.10.got_ref
  53.1 0.1 pair_sum.1
  53.2 1.8 %collective-permute-start.11 = (bf16[1,80,384]{2,1,0:T(8,128)(2,1)S(1)}, bf16[1,80,384]{2,1,0:T(8,128)(2,1)S(1)}, u32[]{:S(2)}, u32[]{:S(2)}) collective-permute-start(bf16[1,80,384]{2,1,0:T(8,128)(2,1)S(1)} %get-tuple-element.44), channel_id=1, source_target_pairs={{0,2},{4,6},{8,10},{12,14},{2,0},{6,4},{10,8},{14,12},{1,3},{5,7},... | collective-permute-start | bytes 184328 | tf_op jit(solution)/shard_map/ppermute | solution.py:54
  55.1 4.9 %collective-permute-start.12 = (bf16[1,80,384]{2,1,0:T(8,128)(2,1)S(1)}, bf16[1,80,384]{2,1,0:T(8,128)(2,1)S(1)}, u32[]{:S(2)}, u32[]{:S(2)}) collective-permute-start(bf16[1,80,384]{2,1,0:T(8,128)(2,1)S(1)} %get-tuple-element.45), channel_id=1, source_target_pairs={{0,8},{4,12},{8,0},{12,4},{2,10},{6,14},{10,2},{14,6},{1,9},{5,13}... | collective-permute-start | bytes 184328 | tf_op jit(solution)/shard_map/ppermute | solution.py:54
  60.0 0.0 collective-permute-start.13
  60.0 5.9 %grad_down.1 = (bf16[1536,4096]{1,0:T(8,128)(2,1)}, f32[8,128]{1,0:T(8,128)}) custom-call(bf16[160,1536]{1,0:T(8,128)(2,1)S(1)} %get-tuple-element.49.refs_0_, bf16[160,4096]{1,0:T(8,128)(2,1)S(1)} %get-tuple-element.50.refs_1_, bf16[1,80,384]{2,1,0:T(8,128)(2,1)S(1)} %get-tuple-element.43.refs_0_.refs_2_), custom_call_target="tpu_custom_call" | custom-call | flops 2013265920 | bytes 12582912 | tf_op jit(solution)/shard_map/grad_down/pallas_call | solution.py:263
  65.9 0.0 collective-permute-done.11.refs_1_
  65.9 0.0 collective-permute-done.12.refs_2_
  65.9 0.2 collective-permute-done.13.refs_3_
  66.1 0.0 copy-done.1
  66.1 0.9 %combine.1 = bf16[128,384]{1,0:T(8,128)(2,1)} custom-call(bf16[4,80,128]{2,1,0:T(8,128)(2,1)S(1)} %copy-done.1, bf16[1,80,384]{2,1,0:T(8,128)(2,1)S(1)} %get-tuple-element.43.refs_0_.refs_2_, bf16[1,80,384]{2,1,0:T(8,128)(2,1)S(1)} %collective-permute-done.11.refs_1_, bf16[1,80,384]{2,1,0:T(8,128)(2,1)S(1)} %collective-permute-done.12.refs_2_, ...), custom_call_target="tpu_custom_call" | custom-call | tf_op jit(solution)/shard_map/combine/pallas_call | solution.py:308
  (10 shorter events, 0.0 us)
Async XLA Ops:
  2.8 13.7 %collective-permute-start.3 = (bf16[1,160,384]{2,1,0:T(8,128)(2,1)}, bf16[1,160,384]{2,1,0:T(8,128)(2,1)S(1)}, u32[]{:S(2)}, u32[]{:S(2)}) collective-permute-start(bf16[1,160,384]{2,1,0:T(8,128)(2,1)} %get-tuple-element.31), channel_id=1, source_target_pairs={{0,8},{4,12},{8,0},{12,4},{2,10},{6,14},{10,2},{14,6},{1,9},{5,13}... | collective-permute-start | bytes 368648 | tf_op jit(solution)/shard_map/ppermute | solution.py:54
  6.9 12.4 %collective-permute-start.4 = (bf16[1,160,384]{2,1,0:T(8,128)(2,1)}, bf16[1,160,384]{2,1,0:T(8,128)(2,1)S(1)}, u32[]{:S(2)}, u32[]{:S(2)}) collective-permute-start(bf16[1,160,384]{2,1,0:T(8,128)(2,1)} %get-tuple-element.32), channel_id=1, source_target_pairs={{0,10},{4,14},{8,2},{12,6},{2,8},{6,12},{10,0},{14,4},{1,11},{5,15... | collective-permute-start | bytes 368648 | tf_op jit(solution)/shard_map/ppermute | solution.py:54
  8.1 0.9 %copy-start.2 = (bf16[1,160,384]{2,1,0:T(8,128)(2,1)S(1)}, bf16[1,160,384]{2,1,0:T(8,128)(2,1)}, u32[]{:S(2)}) copy-start(bf16[1,160,384]{2,1,0:T(8,128)(2,1)} %get-tuple-element.30.array_ref) | copy-start | bytes 368644
  9.0 16.7 %slice-start = ((s8[12582912]{0:T(1024)(128)(4,1)}), s8[4194304]{0:T(1024)(128)(4,1)S(1)}, s32[]{:S(2)}) async-start(s8[12582912]{0:T(1024)(128)(4,1)} %bitcast.2), calls=%async_computation | async-start | bytes 8388608
  9.0 19.0 %slice-start.3 = ((s8[12582912]{0:T(1024)(128)(4,1)}), s8[4194304]{0:T(1024)(128)(4,1)S(1)}, s32[]{:S(2)}) async-start(s8[12582912]{0:T(1024)(128)(4,1)} %bitcast.4), calls=%async_computation.3 | async-start | bytes 8388608
  9.1 3.2 %copy-start = (bf16[1,160,384]{2,1,0:T(8,128)(2,1)S(1)}, bf16[1,160,384]{2,1,0:T(8,128)(2,1)}, u32[]{:S(2)}) copy-start(bf16[1,160,384]{2,1,0:T(8,128)(2,1)} %get-tuple-element.29.refs_0_.refs_1_) | copy-start | bytes 368644
  9.1 16.6 %slice-start.1 = ((s8[12582912]{0:T(1024)(128)(4,1)}), s8[4194304]{0:T(1024)(128)(4,1)S(1)}, s32[]{:S(2)}) async-start(s8[12582912]{0:T(1024)(128)(4,1)} %bitcast.2), calls=%async_computation.1 | async-start | bytes 8388608
  9.1 16.6 %slice-start.2 = ((s8[12582912]{0:T(1024)(128)(4,1)}), s8[4194304]{0:T(1024)(128)(4,1)S(1)}, s32[]{:S(2)}) async-start(s8[12582912]{0:T(1024)(128)(4,1)} %bitcast.2), calls=%async_computation.2 | async-start | bytes 8388608
  9.1 19.0 %slice-start.4 = ((s8[12582912]{0:T(1024)(128)(4,1)}), s8[4194304]{0:T(1024)(128)(4,1)S(1)}, s32[]{:S(2)}) async-start(s8[12582912]{0:T(1024)(128)(4,1)} %bitcast.4), calls=%async_computation.4 | async-start | bytes 8388608
  9.1 19.0 %slice-start.5 = ((s8[12582912]{0:T(1024)(128)(4,1)}), s8[4194304]{0:T(1024)(128)(4,1)S(1)}, s32[]{:S(2)}) async-start(s8[12582912]{0:T(1024)(128)(4,1)} %bitcast.4), calls=%async_computation.5 | async-start | bytes 8388608
  9.1 11.3 %collective-permute-start.2 = (bf16[1,160,384]{2,1,0:T(8,128)(2,1)S(1)}, bf16[1,160,384]{2,1,0:T(8,128)(2,1)S(1)}, u32[]{:S(2)}, u32[]{:S(2)}) collective-permute-start(bf16[1,160,384]{2,1,0:T(8,128)(2,1)S(1)} %window_second.1), channel_id=1, source_target_pairs={{0,6},{4,2},{8,14},{12,10},{2,4},{6,0},{10,12},{14,8},{1,7},{5,3},... | collective-permute-start | bytes 368648 | tf_op jit(solution)/shard_map/ppermute | solution.py:54
  10.8 9.7 %collective-permute-start = (bf16[1,160,384]{2,1,0:T(8,128)(2,1)S(1)}, bf16[1,160,384]{2,1,0:T(8,128)(2,1)S(1)}, u32[]{:S(2)}, u32[]{:S(2)}) collective-permute-start(bf16[1,160,384]{2,1,0:T(8,128)(2,1)S(1)} %window_second.1), channel_id=1, source_target_pairs={{0,2},{4,6},{8,10},{12,14},{2,0},{6,4},{10,8},{14,12},{1,3},{5,7},... | collective-permute-start | bytes 368648 | tf_op jit(solution)/shard_map/ppermute | solution.py:54
  12.2 8.9 %collective-permute-start.1 = (bf16[1,160,384]{2,1,0:T(8,128)(2,1)S(1)}, bf16[1,160,384]{2,1,0:T(8,128)(2,1)S(1)}, u32[]{:S(2)}, u32[]{:S(2)}) collective-permute-start(bf16[1,160,384]{2,1,0:T(8,128)(2,1)S(1)} %copy-done), channel_id=1, source_target_pairs={{0,4},{4,0},{8,12},{12,8},{2,6},{6,2},{10,14},{14,10},{1,5},{5,1},... | collective-permute-start | bytes 368648 | tf_op jit(solution)/shard_map/ppermute | solution.py:54
  16.5 7.3 %collective-permute-start.5 = (bf16[1,160,384]{2,1,0:T(8,128)(2,1)S(1)}, bf16[1,160,384]{2,1,0:T(8,128)(2,1)S(1)}, u32[]{:S(2)}, u32[]{:S(2)}) collective-permute-start(bf16[1,160,384]{2,1,0:T(8,128)(2,1)S(1)} %collective-permute-done.3.refs_4_.refs_5_), channel_id=1, source_target_pairs={{0,4},{4,0},{8,12},{12,8},{2,6},{6,2},{10,14},{14,10},{1,5},{5,1},... | collective-permute-start | bytes 368648 | tf_op jit(solution)/shard_map/ppermute | solution.py:54
  19.3 6.4 %collective-permute-start.6 = (bf16[1,160,384]{2,1,0:T(8,128)(2,1)S(1)}, bf16[1,160,384]{2,1,0:T(8,128)(2,1)S(1)}, u32[]{:S(2)}, u32[]{:S(2)}) collective-permute-start(bf16[1,160,384]{2,1,0:T(8,128)(2,1)S(1)} %collective-permute-done.4.refs_5_.refs_6_), channel_id=1, source_target_pairs={{0,4},{4,0},{8,12},{12,8},{2,6},{6,2},{10,14},{14,10},{1,5},{5,1},... | collective-permute-start | bytes 368648 | tf_op jit(solution)/shard_map/ppermute | solution.py:54
  25.7 5.4 %slice-start.9 = ((s8[12582912]{0:T(1024)(128)(4,1)}), s8[4194304]{0:T(1024)(128)(4,1)S(1)}, s32[]{:S(2)}) async-start(s8[12582912]{0:T(1024)(128)(4,1)} %bitcast.8), calls=%async_computation.9 | async-start | bytes 8388608
  25.7 5.4 %slice-start.10 = ((s8[12582912]{0:T(1024)(128)(4,1)}), s8[4194304]{0:T(1024)(128)(4,1)S(1)}, s32[]{:S(2)}) async-start(s8[12582912]{0:T(1024)(128)(4,1)} %bitcast.8), calls=%async_computation.10 | async-start | bytes 8388608
  28.0 3.1 %collective-permute-start.7 = (bf16[160,4096]{1,0:T(8,128)(2,1)S(1)}, bf16[160,4096]{1,0:T(8,128)(2,1)S(1)}, u32[]{:S(2)}, u32[]{:S(2)}) collective-permute-start(bf16[160,4096]{1,0:T(8,128)(2,1)S(1)} %get-tuple-element.33.g0), channel_id=1, source_target_pairs={{0,1},{1,0},{2,3},{3,2},{4,5},{5,4},{6,7},{7,6},{8,9},{9,8},{10,11... | collective-permute-start | bytes 3932168 | tf_op jit(solution)/shard_map/ppermute | solution.py:324
  28.1 3.0 %slice-start.11 = ((s8[12582912]{0:T(1024)(128)(4,1)}), s8[4194304]{0:T(1024)(128)(4,1)S(1)}, s32[]{:S(2)}) async-start(s8[12582912]{0:T(1024)(128)(4,1)} %bitcast.8), calls=%async_computation.11 | async-start | bytes 8388608
  30.3 3.3 %collective-permute-start.8 = (bf16[160,4096]{1,0:T(8,128)(2,1)S(1)}, bf16[160,4096]{1,0:T(8,128)(2,1)S(1)}, u32[]{:S(2)}, u32[]{:S(2)}) collective-permute-start(bf16[160,4096]{1,0:T(8,128)(2,1)S(1)} %forward_u.1.u0), channel_id=1, source_target_pairs={{0,1},{1,0},{2,3},{3,2},{4,5},{5,4},{6,7},{7,6},{8,9},{9,8},{10,11... | collective-permute-start | bytes 3932168 | tf_op jit(solution)/shard_map/ppermute | solution.py:324
  31.1 5.4 %slice-start.6 = ((s8[12582912]{0:T(1024)(128)(4,1)}), s8[4194304]{0:T(1024)(128)(4,1)S(1)}, s32[]{:S(2)}) async-start(s8[12582912]{0:T(1024)(128)(4,1)} %bitcast.6), calls=%async_computation.6 | async-start | bytes 8388608
  31.1 5.4 %slice-start.7 = ((s8[12582912]{0:T(1024)(128)(4,1)}), s8[4194304]{0:T(1024)(128)(4,1)S(1)}, s32[]{:S(2)}) async-start(s8[12582912]{0:T(1024)(128)(4,1)} %bitcast.6), calls=%async_computation.7 | async-start | bytes 8388608
  33.4 3.1 %slice-start.8 = ((s8[12582912]{0:T(1024)(128)(4,1)}), s8[4194304]{0:T(1024)(128)(4,1)S(1)}, s32[]{:S(2)}) async-start(s8[12582912]{0:T(1024)(128)(4,1)} %bitcast.6), calls=%async_computation.8 | async-start | bytes 8388608
  33.4 3.1 %collective-permute-start.9 = (bf16[160,4096]{1,0:T(8,128)(2,1)S(1)}, bf16[160,4096]{1,0:T(8,128)(2,1)S(1)}, u32[]{:S(2)}, u32[]{:S(2)}) collective-permute-start(bf16[160,4096]{1,0:T(8,128)(2,1)S(1)} %get-tuple-element.37.d0), channel_id=1, source_target_pairs={{0,1},{1,0},{2,3},{3,2},{4,5},{5,4},{6,7},{7,6},{8,9},{9,8},{10,11... | collective-permute-start | bytes 3932168 | tf_op jit(solution)/shard_map/ppermute | solution.py:324
  43.9 9.2 %collective-permute-start.10 = (bf16[4,80,384]{2,1,0:T(8,128)(2,1)S(1)}, bf16[4,80,384]{2,1,0:T(8,128)(2,1)S(1)}, u32[]{:S(2)}, u32[]{:S(2)}) collective-permute-start(bf16[4,80,384]{2,1,0:T(8,128)(2,1)S(1)} %get-tuple-element.39), channel_id=1, source_target_pairs={{0,4},{4,0},{8,12},{12,8},{2,6},{6,2},{10,14},{14,10},{1,5},{5,1},... | collective-permute-start | bytes 737288 | tf_op jit(solution)/shard_map/ppermute | solution.py:54
  53.2 12.7 %collective-permute-start.11 = (bf16[1,80,384]{2,1,0:T(8,128)(2,1)S(1)}, bf16[1,80,384]{2,1,0:T(8,128)(2,1)S(1)}, u32[]{:S(2)}, u32[]{:S(2)}) collective-permute-start(bf16[1,80,384]{2,1,0:T(8,128)(2,1)S(1)} %get-tuple-element.44), channel_id=1, source_target_pairs={{0,2},{4,6},{8,10},{12,14},{2,0},{6,4},{10,8},{14,12},{1,3},{5,7},... | collective-permute-start | bytes 184328 | tf_op jit(solution)/shard_map/ppermute | solution.py:54
  55.1 10.8 %collective-permute-start.12 = (bf16[1,80,384]{2,1,0:T(8,128)(2,1)S(1)}, bf16[1,80,384]{2,1,0:T(8,128)(2,1)S(1)}, u32[]{:S(2)}, u32[]{:S(2)}) collective-permute-start(bf16[1,80,384]{2,1,0:T(8,128)(2,1)S(1)} %get-tuple-element.45), channel_id=1, source_target_pairs={{0,8},{4,12},{8,0},{12,4},{2,10},{6,14},{10,2},{14,6},{1,9},{5,13}... | collective-permute-start | bytes 184328 | tf_op jit(solution)/shard_map/ppermute | solution.py:54
  60.0 6.1 %collective-permute-start.13 = (bf16[1,80,384]{2,1,0:T(8,128)(2,1)S(1)}, bf16[1,80,384]{2,1,0:T(8,128)(2,1)S(1)}, u32[]{:S(2)}, u32[]{:S(2)}) collective-permute-start(bf16[1,80,384]{2,1,0:T(8,128)(2,1)S(1)} %get-tuple-element.46), channel_id=1, source_target_pairs={{0,10},{4,14},{8,2},{12,6},{2,8},{6,12},{10,0},{14,4},{1,11},{5,15... | collective-permute-start | bytes 184328 | tf_op jit(solution)/shard_map/ppermute | solution.py:54
  60.0 6.1 %copy-start.1 = (bf16[4,80,128]{2,1,0:T(8,128)(2,1)S(1)}, bf16[4,80,128]{2,1,0:T(8,128)(2,1)}, u32[]{:S(2)}) copy-start(bf16[4,80,128]{2,1,0:T(8,128)(2,1)} %get-tuple-element.28.sel_ref) | copy-start | bytes 245764
